TPU v7x, 32 devices: a whole 2x2x4 slice. The times are simulated.
32 devices in a mesh: grp: 4 (over x, core), shard: 8 (over z, y).
Axes of the slice: x: 2, y: 2, z: 4, core: 2. Of those that a mesh axis runs over, the one named last changes fastest.
Arguments:
- tokens: bfloat16 [4096, 1024], P(('grp', 'shard')), may hold values from -6 to 6
- cotangent: bfloat16 [4096, 1024], P(('grp', 'shard')), may hold values from -6 to 6
- item_ids: int32 [4096], P('grp'), may hold values from 0 to 2, as said below
- live_mask: int32 [4096], P('grp'), may hold values from 0 to 1, as said below
- qkv_weight: bfloat16 [1024, 3072], P('shard'), may hold values from -0.1875 to 0.1875
- out_weight: bfloat16 [1024, 1024], P('shard'), may hold values from -3 to 3
- up_weight: bfloat16 [1024, 4096], P('shard'), may hold values from -0.1875 to 0.1875
- down_weight: bfloat16 [4096, 1024], P('shard'), may hold values from -0.09375 to 0.09375
- norm_weight: bfloat16 [4, 1024], P(None, 'shard'), may hold values from -1.2 to 1.4, as said below
- qkv_master: float32 [1024, 3072], P(('grp', 'shard')), may hold values from -0.1875 to 0.1875
- qkv_first: float32 [1024, 3072], P(('grp', 'shard')), may hold values from -0.0546875 to 0.0546875
- qkv_second: float32 [1024, 3072], P(('grp', 'shard')), may hold values from 8.789063e-05 to 0.0003515625
- out_master: float32 [1024, 1024], P(('grp', 'shard')), may hold values from -3 to 3
- out_first: float32 [1024, 1024], P(('grp', 'shard')), may hold values from -0.0078125 to 0.0078125
- out_second: float32 [1024, 1024], P(('grp', 'shard')), may hold values from 2.1457672e-06 to 8.583069e-06
- up_master: float32 [1024, 4096], P(('grp', 'shard')), may hold values from -0.1875 to 0.1875
- up_first: float32 [1024, 4096], P(('grp', 'shard')), may hold values from -0.0390625 to 0.0390625
- up_second: float32 [1024, 4096], P(('grp', 'shard')), may hold values from 4.8828126e-05 to 0.0001953125
- down_master: float32 [4096, 1024], P(('grp', 'shard')), may hold values from -0.09375 to 0.09375
- down_first: float32 [4096, 1024], P(('grp', 'shard')), may hold values from -0.078125 to 0.078125
- down_second: float32 [4096, 1024], P(('grp', 'shard')), may hold values from 0.00015625 to 0.000625
- norm_master: float32 [4, 1024], P(None, ('grp', 'shard')), may hold values from -1.2 to 1.4, as said below
- norm_first: float32 [4, 1024], P(None, ('grp', 'shard')), may hold values from -0.75 to 0.75
- norm_second: float32 [4, 1024], P(None, ('grp', 'shard')), may hold values from 0.015625 to 0.0625
Outputs:
- block_out: float32 [4096, 1024], P(('grp', 'shard'))
- input_grad: float32 [4096, 1024], P(('grp', 'shard'))
- qkv_grad: float32 [1024, 3072], P(('grp', 'shard'))
- qkv_moment: float32 [1024, 3072], P(('grp', 'shard'))
- qkv_square: float32 [1024, 3072], P(('grp', 'shard'))
- qkv_fresh: float32 [1024, 3072], P(('grp', 'shard'))
- qkv_copy: bfloat16 [1024, 3072], P(('grp', 'shard'))
- out_grad: float32 [1024, 1024], P(('grp', 'shard'))
- out_moment: float32 [1024, 1024], P(('grp', 'shard'))
- out_square: float32 [1024, 1024], P(('grp', 'shard'))
- out_fresh: float32 [1024, 1024], P(('grp', 'shard'))
- out_copy: bfloat16 [1024, 1024], P(('grp', 'shard'))
- up_grad: float32 [1024, 4096], P(('grp', 'shard'))
- up_moment: float32 [1024, 4096], P(('grp', 'shard'))
- up_square: float32 [1024, 4096], P(('grp', 'shard'))
- up_fresh: float32 [1024, 4096], P(('grp', 'shard'))
- up_copy: bfloat16 [1024, 4096], P(('grp', 'shard'))
- down_grad: float32 [4096, 1024], P(('grp', 'shard'))
- down_moment: float32 [4096, 1024], P(('grp', 'shard'))
- down_square: float32 [4096, 1024], P(('grp', 'shard'))
- down_fresh: float32 [4096, 1024], P(('grp', 'shard'))
- down_copy: bfloat16 [4096, 1024], P(('grp', 'shard'))
- norm_grad: float32 [4, 1024], P(None, ('grp', 'shard'))
- norm_moment: float32 [4, 1024], P(None, ('grp', 'shard'))
- norm_square: float32 [4, 1024], P(None, ('grp', 'shard'))
- norm_fresh: float32 [4, 1024], P(None, ('grp', 'shard'))
- norm_copy: bfloat16 [4, 1024], P(None, ('grp', 'shard'))
Inputs may be any that keep to these rules, and one draw needn't show every extreme that they name: `item_ids`: within each group of 1024 consecutive rows the item number never falls; item 1 starts at one of rows 1 to 63 of the group and ends in its last 64 rows, items 0 and 2 fill the rest. `live_mask`: the first row of every item is 1. `norm_weight`: rows 0 and 2 are gains, rows 1 and 3 biases. `norm_master`: rows 0 and 2 are gains, rows 1 and 3 biases.
All inputs are finite; a program needn't handle non-finite values.
Results may differ from a plain program's by a relative error of at most 0.018.
Values may be sent and summed in bfloat16 or wider, within the bound.
A program may use at most 256 MiB of HBM per device.

v0:
```python
import math

import jax
import jax.numpy as jnp
from jax import lax
from jax.sharding import PartitionSpec as P

HEADS = 16
HEAD_DIM = 64
STEP = 5


eps_norm = 1e-06
score_scale = 0.125


def exact_gelu(inputs):
    return jax.nn.gelu(inputs, approximate=False)


def outer_sum(left, right):
    return lax.dot_general(
        left, right, (((0,), (0,)), ((), ())), preferred_element_type=jnp.float32
    )


def back_dot(gradient, weight):
    return lax.dot_general(
        gradient, weight, (((1,), (1,)), ((), ())), preferred_element_type=jnp.float32
    )


def norm_forward(values, gain, shift):
    mean = jnp.mean(values, -1, keepdims=True)
    centred = values - mean
    variance = jnp.mean(centred * centred, -1, keepdims=True)
    inverse = lax.rsqrt(variance + eps_norm)
    normed = centred * inverse
    return (normed * gain + shift, normed, inverse)


def norm_backward(upstream, normed, inverse, gain):
    scaled = upstream * gain
    mean_one = jnp.mean(scaled, -1, keepdims=True)
    mean_two = jnp.mean(scaled * normed, -1, keepdims=True)
    return (
        inverse * (scaled - mean_one - normed * mean_two),
        jnp.sum(upstream * normed, 0),
        jnp.sum(upstream, 0),
    )


def block_scores(queries, query_items, key_heads, key_items, key_live):
    scores = (
        jnp.einsum("qhd,khd->qhk", queries, key_heads, preferred_element_type=jnp.float32)
        * score_scale
    )
    allowed = (query_items[:, None] == key_items[None, :]) & (key_live[None, :] > 0)
    return (scores, allowed[:, None, :])


def score_grads(
    queries, query_items, grad_out, log_total, grad_dot, key_heads, value_heads, key_items, key_live
):
    scores, allowed = block_scores(queries, query_items, key_heads, key_items, key_live)
    attention = jnp.where(allowed, jnp.exp(scores - log_total[..., None]), 0.0)
    grad_attention = jnp.einsum(
        "qhd,khd->qhk", grad_out, value_heads, preferred_element_type=jnp.float32
    )
    grad_scores = (attention * (grad_attention - grad_dot[..., None])).astype(jnp.bfloat16)
    return (grad_scores, attention.astype(jnp.bfloat16))


def key_terms(grad_scores, attention_low, queries, grad_out):
    grad_key = (
        jnp.einsum("qhk,qhd->khd", grad_scores, queries, preferred_element_type=jnp.float32)
        * score_scale
    )
    grad_value = jnp.einsum(
        "qhk,qhd->khd", attention_low, grad_out, preferred_element_type=jnp.float32
    )
    return (grad_key, grad_value)


def query_term(grad_scores, key_heads):
    return (
        jnp.einsum("qhk,khd->qhd", grad_scores, key_heads, preferred_element_type=jnp.float32)
        * score_scale
    )


def key_blocks(shard_piece, item_ids, live_mask):
    piece_rows = shard_piece.shape[0]
    block_rows = math.gcd(piece_rows, 512)
    block_count = piece_rows // block_rows
    heads = shard_piece.reshape(block_count, block_rows, 2, HEADS, HEAD_DIM)
    key_items = item_ids.reshape(block_count, block_rows)
    key_live = live_mask.reshape(block_count, block_rows)
    return (heads[:, :, 0], heads[:, :, 1], key_items, key_live, block_rows)


def attend_fold(queries, query_items, item_ids, live_mask, carried, shard_piece):
    key_heads, value_heads, key_items, key_live, block_rows = key_blocks(
        shard_piece, item_ids, live_mask
    )

    def attend_advance(running, current):
        running_max, running_sum, weighted_sum = running
        key_block, value_block, item_block, live_block = current
        scores, allowed = block_scores(queries, query_items, key_block, item_block, live_block)
        new_max = jnp.maximum(running_max, jnp.max(jnp.where(allowed, scores, -1e30), -1))
        attention = jnp.where(allowed, jnp.exp(scores - new_max[..., None]), 0.0)
        factor = jnp.exp(running_max - new_max)
        running_sum = running_sum * factor + jnp.sum(attention, -1)
        weighted_sum = weighted_sum * factor[..., None] + jnp.einsum(
            "qhk,khd->qhd",
            attention.astype(jnp.bfloat16),
            value_block,
            preferred_element_type=jnp.float32,
        )
        return ((new_max, running_sum, weighted_sum), None)

    carried, _ = lax.scan(attend_advance, carried, (key_heads, value_heads, key_items, key_live))
    return carried


def summed_fold(queries, query_items, grad_out, log_total, grad_dot, item_ids, live_mask):

    def fold_keys(carried, shard_piece, first_row):
        grad_query, grad_pairs = carried
        key_heads, value_heads, key_items, key_live, block_rows = key_blocks(
            shard_piece, item_ids, live_mask
        )

        def fold_advance(running, current):
            key_block, value_block, item_block, live_block = current
            grad_scores, attention_low = score_grads(
                queries,
                query_items,
                grad_out,
                log_total,
                grad_dot,
                key_block,
                value_block,
                item_block,
                live_block,
            )
            grad_key, grad_value = key_terms(grad_scores, attention_low, queries, grad_out)
            paired = jnp.concatenate(
                [grad_key.reshape(block_rows, -1), grad_value.reshape(block_rows, -1)], 1
            )
            return (running + query_term(grad_scores, key_block), paired)

        grad_query, pieces = lax.scan(
            fold_advance, grad_query, (key_heads, value_heads, key_items, key_live)
        )
        grad_pairs = pieces.reshape(shard_piece.shape[0], -1)
        return (grad_query, grad_pairs)

    return fold_keys


def adamw(summed, live_total, master, old_first, old_second, step_rate, shrink):
    gradient = summed / live_total
    moment = 0.5 * old_first + 0.5 * gradient
    square = 0.5 * old_second + 0.5 * gradient * gradient
    correction = 1.0 - 0.5**STEP
    updated = master - step_rate * (
        moment / correction / (jnp.sqrt(square / correction) + 1e-08) + shrink * master
    )
    return (gradient, moment, square, updated, updated.astype(jnp.bfloat16))


def body(
    tokens,
    cotangent,
    item_ids,
    live_mask,
    qkv_weight,
    out_weight,
    up_weight,
    down_weight,
    norm_weight,
    qkv_master,
    qkv_first,
    qkv_second,
    out_master,
    out_first,
    out_second,
    up_master,
    up_first,
    up_second,
    down_master,
    down_first,
    down_second,
    norm_master,
    norm_first,
    norm_second,
):
    local_rows = tokens.shape[0]
    model_width = tokens.shape[1]
    group_rows = item_ids.shape[0]
    offset = lax.axis_index("shard") * local_rows
    qkv_full, out_full, up_full, down_full, norm_full = (
        lax.all_gather(qkv_weight, "shard", axis=0, tiled=True),
        lax.all_gather(out_weight, "shard", axis=0, tiled=True),
        lax.all_gather(up_weight, "shard", axis=0, tiled=True),
        lax.all_gather(down_weight, "shard", axis=0, tiled=True),
        lax.all_gather(norm_weight, "shard", axis=1, tiled=True),
    )
    hidden = up_full.shape[1]
    norm_values = norm_full.astype(jnp.float32)
    live_rows = lax.dynamic_slice_in_dim(live_mask, offset, local_rows)
    query_items = lax.dynamic_slice_in_dim(item_ids, offset, local_rows)
    group_count = jnp.sum(live_mask).astype(jnp.float32)
    total_count = lax.psum(group_count, "grp")
    inputs = tokens.astype(jnp.float32)
    first_norm, normed_one, inverse_one = norm_forward(inputs, norm_values[0], norm_values[1])
    first_low = first_norm.astype(jnp.bfloat16)
    projected = jnp.dot(first_low, qkv_full, preferred_element_type=jnp.float32).astype(
        jnp.bfloat16
    )
    query_flat = projected[:, :model_width]
    queries = query_flat.reshape(local_rows, HEADS, HEAD_DIM)
    key_values = projected[:, model_width:]
    start_state = (
        jnp.full((local_rows, HEADS), -1e30, jnp.float32),
        jnp.zeros((local_rows, HEADS), jnp.float32),
        jnp.zeros((local_rows, HEADS, HEAD_DIM), jnp.float32),
    )
    running_max, running_sum, weighted_sum = attend_fold(
        queries,
        query_items,
        item_ids,
        live_mask,
        start_state,
        lax.all_gather(key_values, "shard", axis=0, tiled=True),
    )
    attended = weighted_sum / running_sum[..., None]
    log_total = running_max + jnp.log(running_sum)
    attended_low = attended.reshape(local_rows, model_width).astype(jnp.bfloat16)
    mixed = inputs + jnp.dot(attended_low, out_full, preferred_element_type=jnp.float32)
    second_norm, normed_two, inverse_two = norm_forward(mixed, norm_values[2], norm_values[3])
    second_low = second_norm.astype(jnp.bfloat16)
    expanded = jnp.dot(second_low, up_full, preferred_element_type=jnp.float32)
    activated, gelu_pull = jax.vjp(exact_gelu, expanded)
    activated_low = activated.astype(jnp.bfloat16)
    block_out = mixed + jnp.dot(activated_low, down_full, preferred_element_type=jnp.float32)
    upstream = cotangent.astype(jnp.float32) * live_rows.astype(jnp.float32)[:, None]
    upstream_low = upstream.astype(jnp.bfloat16)
    down_term = outer_sum(activated_low, upstream_low)
    (grad_expanded,) = gelu_pull(back_dot(upstream_low, down_full))
    expanded_low = grad_expanded.astype(jnp.bfloat16)
    up_term = outer_sum(second_low, expanded_low)
    grad_mixed, gain_two, shift_two = norm_backward(
        back_dot(expanded_low, up_full), normed_two, inverse_two, norm_values[2]
    )
    grad_mixed = grad_mixed + upstream
    mixed_low = grad_mixed.astype(jnp.bfloat16)
    out_term = outer_sum(attended_low, mixed_low)
    grad_flat = back_dot(mixed_low, out_full).astype(jnp.bfloat16)
    grad_attended = grad_flat.reshape(local_rows, HEADS, HEAD_DIM)
    grad_dot = jnp.sum(grad_attended.astype(jnp.float32) * attended, -1)
    zero_query = jnp.zeros((local_rows, HEADS, HEAD_DIM), jnp.float32)
    fold_back = summed_fold(
        queries, query_items, grad_attended, log_total, grad_dot, item_ids, live_mask
    )
    start_back = (zero_query, jnp.zeros((group_rows, 2 * model_width), jnp.float32))
    folded = fold_back(
        start_back, lax.all_gather(key_values, "shard", axis=0, tiled=True), jnp.int32(0)
    )
    grad_query, grad_pairs = folded
    grad_kv = lax.psum_scatter(
        grad_pairs.astype(jnp.bfloat16), "shard", scatter_dimension=0, tiled=True
    ).astype(jnp.float32)
    grad_projected = jnp.concatenate(
        [grad_query.reshape(local_rows, model_width), grad_kv], 1
    ).astype(jnp.bfloat16)
    qkv_term = outer_sum(first_low, grad_projected)
    grad_first, gain_one, shift_one = norm_backward(
        back_dot(grad_projected, qkv_full), normed_one, inverse_one, norm_values[0]
    )
    input_grad = grad_first + grad_mixed
    norm_term = jnp.stack([gain_one, shift_one, gain_two, shift_two])
    qkv_sum, out_sum, up_sum, down_sum, norm_sum = (
        lax.psum_scatter(qkv_term, ("grp", "shard"), scatter_dimension=0, tiled=True),
        lax.psum_scatter(out_term, ("grp", "shard"), scatter_dimension=0, tiled=True),
        lax.psum_scatter(up_term, ("grp", "shard"), scatter_dimension=0, tiled=True),
        lax.psum_scatter(down_term, ("grp", "shard"), scatter_dimension=0, tiled=True),
        lax.psum_scatter(norm_term, ("grp", "shard"), scatter_dimension=1, tiled=True),
    )
    qkv_grad, qkv_moment, qkv_square, qkv_fresh, qkv_copy = adamw(
        qkv_sum, total_count, qkv_master, qkv_first, qkv_second, model_width ** (-0.5), 0.1
    )
    out_grad, out_moment, out_square, out_fresh, out_copy = adamw(
        out_sum, total_count, out_master, out_first, out_second, math.sqrt(group_rows) / 64, 0.1
    )
    up_grad, up_moment, up_square, up_fresh, up_copy = adamw(
        up_sum, total_count, up_master, up_first, up_second, model_width ** (-0.5), 0.1
    )
    down_grad, down_moment, down_square, down_fresh, down_copy = adamw(
        down_sum, total_count, down_master, down_first, down_second, hidden ** (-0.5), 0.1
    )
    norm_grad, norm_moment, norm_square, norm_fresh, norm_copy = adamw(
        norm_sum, total_count, norm_master, norm_first, norm_second, 0.4, 0.0
    )
    return (
        block_out,
        input_grad,
        qkv_grad,
        qkv_moment,
        qkv_square,
        qkv_fresh,
        qkv_copy,
        out_grad,
        out_moment,
        out_square,
        out_fresh,
        out_copy,
        up_grad,
        up_moment,
        up_square,
        up_fresh,
        up_copy,
        down_grad,
        down_moment,
        down_square,
        down_fresh,
        down_copy,
        norm_grad,
        norm_moment,
        norm_square,
        norm_fresh,
        norm_copy,
    )


def solution(mesh):
    placed = (
        P(("grp", "shard"), None),
        P(("grp", "shard"), None),
        P("grp"),
        P("grp"),
        P("shard", None),
        P("shard", None),
        P("shard", None),
        P("shard", None),
        P(None, "shard"),
        P(("grp", "shard"), None),
        P(("grp", "shard"), None),
        P(("grp", "shard"), None),
        P(("grp", "shard"), None),
        P(("grp", "shard"), None),
        P(("grp", "shard"), None),
        P(("grp", "shard"), None),
        P(("grp", "shard"), None),
        P(("grp", "shard"), None),
        P(("grp", "shard"), None),
        P(("grp", "shard"), None),
        P(("grp", "shard"), None),
        P(None, ("grp", "shard")),
        P(None, ("grp", "shard")),
        P(None, ("grp", "shard")),
    )
    return jax.shard_map(
        body,
        mesh=mesh,
        in_specs=placed,
        out_specs=(
            P(("grp", "shard"), None),
            P(("grp", "shard"), None),
            P(("grp", "shard"), None),
            P(("grp", "shard"), None),
            P(("grp", "shard"), None),
            P(("grp", "shard"), None),
            P(("grp", "shard"), None),
            P(("grp", "shard"), None),
            P(("grp", "shard"), None),
            P(("grp", "shard"), None),
            P(("grp", "shard"), None),
            P(("grp", "shard"), None),
            P(("grp", "shard"), None),
            P(("grp", "shard"), None),
            P(("grp", "shard"), None),
            P(("grp", "shard"), None),
            P(("grp", "shard"), None),
            P(("grp", "shard"), None),
            P(("grp", "shard"), None),
            P(("grp", "shard"), None),
            P(("grp", "shard"), None),
            P(("grp", "shard"), None),
            P(None, ("grp", "shard")),
            P(None, ("grp", "shard")),
            P(None, ("grp", "shard")),
            P(None, ("grp", "shard")),
            P(None, ("grp", "shard")),
        ),
        check_vma=False,
    )
```

profile of v0, /device:TPU:0, one launch (start us, length us, event | category | flops | bytes accessed | tf_op | source)
XLA Modules:
  0.0 1792.9 jit_solution(9785939809882353636)
XLA Ops:
  8.0 22.7 %all_gather.19 = bf16[4,1024]{1,0:T(4,128)(2,1)S(1)} all-gather(bf16[4,128]{1,0:T(4,128)(2,1)} %param.36), channel_id=1, replica_groups=mesh['grp'=4,'shard'=8] {'shard'}, dimensions={1}, use_global_device_ids=true | all-gather | bytes 9216 | tf_op jit(solution)/shard_map/all_gather | solution.py:209
  33.0 79.0 %all-gather.6.cloned.1.call-done = bf16[1024,3072]{1,0:T(8,128)(2,1)} async-done(((bf16[128,3072]{1,0:T(8,128)(2,1)}), bf16[1024,3072]{1,0:T(8,128)(2,1)}) %all-gather.6.cloned.1.call-update) | async-done | bytes 6291472 | tf_op jit(solution)/shard_map/all_gather | solution.py:205
  112.0 4.0 convolution_convert_fusion
  119.2 69.4 %all-gather.8.cloned.1.call-done = bf16[1024,2048]{1,0:T(8,128)(2,1)} async-done(((bf16[128,2048]{1,0:T(8,128)(2,1)}), bf16[1024,2048]{1,0:T(8,128)(2,1)}) %all-gather.8.cloned.1.call-update) | async-done | bytes 4194320 | tf_op jit(solution)/shard_map/all_gather | solution.py:237
  188.6 6.4 copy.92
  195.0 7.9 reshape.208
  202.8 4.7 slice_bitcast_fusion
  211.1 20.7 %while.28 = (s32[]{:T(128)}, f32[128,16]{0,1:T(8,128)S(1)}, f32[128,16]{0,1:T(8,128)S(1)}, f32[128,16,64]{0,2,1:T(8,128)S(1)}, s32[128]{0:T(128)S(1)}, /*index=5...) while((s32[]{:T(128)}, f32[128,16]{0,1:T(8,128)S(1)}, ...), condition=%wide.region_5.6_spmd.clone, body=%wide.region_2.5_spmd.clone.sunk | while | flops 280504832 | bytes 33171124 | solution.py:123
  211.3 4.2 fusion.151
  215.5 3.2 fusion.152
  219.0 2.4 fusion.154
  221.7 4.2 fusion.151
  225.9 3.2 fusion.152
  229.4 2.4 fusion.154
  231.9 6.4 all-gather.10.cloned.1.call-done
  238.3 2.1 fusion.107
  240.7 123.1 %all-gather.12.cloned.1.call-done = bf16[1024,4096]{1,0:T(8,128)(2,1)} async-done(((bf16[128,4096]{1,0:T(8,128)(2,1)}), bf16[1024,4096]{1,0:T(8,128)(2,1)}) %all-gather.12.cloned.1.call-update) | async-done | bytes 8388624 | tf_op jit(solution)/shard_map/all_gather | solution.py:207
  363.7 6.1 fusion.95
  369.8 119.0 %all-gather.14.cloned.1.call-done = bf16[4096,1024]{1,0:T(8,128)(2,1)} async-done(((bf16[512,1024]{1,0:T(8,128)(2,1)}), bf16[4096,1024]{1,0:T(8,128)(2,1)}) %all-gather.14.cloned.1.call-update) | async-done | bytes 8388624 | tf_op jit(solution)/shard_map/all_gather | solution.py:208
  488.9 10.0 add_convert_fusion
  498.9 3.0 multiply_reduce_fusion
  505.7 33.0 %while.29 = (s32[]{:T(128)}, f32[128,16,64]{0,2,1:T(8,128)S(1)}, bf16[2,512,2048]{2,1,0:T(8,128)(2,1)}, bf16[2,512,16,64]{1,3,2,0:T(8,128)(2,1)}, s32[128]{0:T(1...) while((s32[]{:T(128)}, f32[128,16,64]{0,2,1:T(8,128)S(1)}, ...), condition=%wide.region_12.13_spmd.clone, body=%wide.region_11.12_spmd.clone.sunk | while | flops 687342080 | bytes 80971512 | solution.py:154
  505.7 2.2 fusion.165
  508.2 2.8 fusion.166
  511.0 2.1 fusion.167
  513.5 1.9 fusion.168
  517.8 2.9 copy.123
  522.2 2.2 fusion.165
  524.6 2.8 fusion.166
  527.5 2.1 fusion.167
  534.3 2.9 copy.123
  539.8 2.7 fusion.80
  542.8 82.4 %reduce-scatter.9.cloned.1.call-done = bf16[128,2048]{1,0:T(8,128)(2,1)} async-done(((bf16[1024,2048]{1,0:T(8,128)(2,1)}), bf16[128,2048]{1,0:T(8,128)(2,1)}) %reduce-scatter.9.cloned.1.call-update) | async-done | bytes 524304 | tf_op jit(solution)/shard_map/reduce_scatter | solution.py:273
  625.2 5.4 fusion.70
  631.9 6.4 fusion.75
  639.5 8.2 fusion.94
  648.6 11.0 fusion.83
  661.6 7.8 psum.7
  669.4 10.3 convolution_add_fusion.1
  679.7 91.8 %reduce-scatter.13.cloned.1.call-done = f32[32,1024]{1,0:T(8,128)} async-done(((f32[1024,1024]{1,0:T(8,128)}), f32[32,1024]{1,0:T(8,128)}) %reduce-scatter.13.cloned.1.call-update) | async-done | bytes 131088 | tf_op jit(solution)/shard_map/reduce_scatter | solution.py:287
  771.6 2.4 fusion.102
  775.0 130.8 %reduce-scatter.19.cloned.1.call-done = f32[32,4]{1,0:T(8,128)} async-done(((f32[1024,4]{1,0:T(8,128)}), f32[32,4]{1,0:T(8,128)}) %reduce-scatter.19.cloned.1.call-update) | async-done | bytes 528
  907.8 155.6 %reduce-scatter.11.cloned.1.call-done = f32[32,3072]{1,0:T(8,128)} async-done(((f32[1024,3072]{1,0:T(8,128)}), f32[32,3072]{1,0:T(8,128)}) %reduce-scatter.11.cloned.1.call-update) | async-done | bytes 393232 | tf_op jit(solution)/shard_map/reduce_scatter | solution.py:286
  1063.4 3.0 fusion.104
  1066.5 356.4 %reduce-scatter.15.cloned.1.call-done = f32[32,4096]{1,0:T(8,128)} async-done(((f32[1024,4096]{1,0:T(8,128)}), f32[32,4096]{1,0:T(8,128)}) %reduce-scatter.15.cloned.1.call-update) | async-done | bytes 524304 | tf_op jit(solution)/shard_map/reduce_scatter | solution.py:288
  1422.9 3.2 fusion.100
  1426.1 356.5 %reduce-scatter.17.cloned.1.call-done = f32[128,1024]{1,0:T(8,128)} async-done(((f32[4096,1024]{1,0:T(8,128)}), f32[128,1024]{1,0:T(8,128)}) %reduce-scatter.17.cloned.1.call-update) | async-done | bytes 524304 | tf_op jit(solution)/shard_map/reduce_scatter | solution.py:289
  1782.6 3.2 fusion.98
  (162 shorter events, 34.9 us)
Async XLA Ops:
  7.2 104.8 %all-gather.6.cloned.1.call-start = ((), (), s32[]{:S(2)}) async-start(), calls=%async_computation.6 | async-start | bytes 7077888 | tf_op jit(solution)/shard_map/all_gather | solution.py:205
  7.9 180.7 %all-gather.8.cloned.1.call-start = ((), (), s32[]{:S(2)}) async-start(), calls=%async_computation.7 | async-start | bytes 4718592 | tf_op jit(solution)/shard_map/all_gather | solution.py:237
  116.0 2.9 copy-start.30
  116.0 3.0 copy-start.28
  116.8 121.5 %all-gather.10.cloned.1.call-start = ((), (), s32[]{:S(2)}) async-start(), calls=%async_computation.8 | async-start | bytes 2359296 | tf_op jit(solution)/shard_map/all_gather | solution.py:206
  117.6 246.2 %all-gather.12.cloned.1.call-start = ((), (), s32[]{:S(2)}) async-start(), calls=%async_computation.9 | async-start | bytes 9437184 | tf_op jit(solution)/shard_map/all_gather | solution.py:207
  118.2 370.7 %all-gather.14.cloned.1.call-start = ((), (), s32[]{:S(2)}) async-start(), calls=%async_computation.10 | async-start | bytes 9437184 | tf_op jit(solution)/shard_map/all_gather | solution.py:208
  118.7 506.4 %reduce-scatter.9.cloned.1.call-start = ((), (), s32[]{:S(2)}) async-start(), calls=%async_computation.11 | async-start | bytes 4718592 | tf_op jit(solution)/shard_map/reduce_scatter | solution.py:273
  211.1 27.2 %copy-start.4 = (bf16[128,1024]{1,0:T(8,128)(2,1)S(1)}, bf16[128,1024]{1,0:T(8,128)(2,1)}, u32[]{:S(2)}) copy-start(bf16[128,1024]{1,0:T(8,128)(2,1)} %param.28) | copy-start | bytes 786436
  215.5 3.5 copy-start
  225.9 3.5 copy-start
  231.9 138.0 %copy-start.11 = (bf16[128,16,64]{0,2,1:T(8,128)(2,1)}, bf16[128,16,64]{0,2,1:T(8,128)(2,1)S(1)}, u32[]{:S(2)}) copy-start(bf16[128,16,64]{0,2,1:T(8,128)(2,1)S(1)} %fusion.78) | copy-start | bytes 786436
  363.7 125.1 %copy-start.23 = (bf16[128,1024]{1,0:T(8,128)(2,1)S(1)}, bf16[128,1024]{1,0:T(8,128)(2,1)}, u32[]{:S(2)}) copy-start(bf16[128,1024]{1,0:T(8,128)(2,1)} %param.29) | copy-start | bytes 786436
  488.9 10.0 copy-start.3
  498.8 3.1 copy-start.9
  498.9 4.1 copy-start.6
  502.2 0.8 copy-start.7
  505.7 2.4 copy-start.13
  507.9 3.1 copy-start.1
  511.0 2.5 copy-start.2
  522.2 2.4 copy-start.13
  524.4 3.1 copy-start.1
  527.5 2.5 copy-start.2
  538.7 1.0 copy-start.8
  538.7 1.1 copy-start.12
  538.7 232.8 %reduce-scatter.13.cloned.1.call-start = ((), (), s32[]{:S(2)}) async-start(), calls=%async_computation.13 | async-start | bytes 4325376 | tf_op jit(solution)/shard_map/reduce_scatter | solution.py:287
  542.5 82.7 %copy-start.5 = (bf16[128,1024]{1,0:T(8,128)(2,1)S(1)}, bf16[128,1024]{1,0:T(8,128)(2,1)}, u32[]{:S(2)}) copy-start(bf16[128,1024]{1,0:T(8,128)(2,1)} %param.28) | copy-start | bytes 786436
  542.5 363.2 %reduce-scatter.19.cloned.1.call-start = ((), (), s32[]{:S(2)}) async-start(), calls=%async_computation.16 | async-start | bytes 540672
  625.2 6.7 copy-start.20
  631.6 431.8 %reduce-scatter.11.cloned.1.call-start = ((), (), s32[]{:S(2)}) async-start(), calls=%async_computation.12 | async-start | bytes 12976128 | tf_op jit(solution)/shard_map/reduce_scatter | solution.py:286
  638.3 1.2 copy-start.10
  638.3 784.6 %reduce-scatter.15.cloned.1.call-start = ((), (), s32[]{:S(2)}) async-start(), calls=%async_computation.14 | async-start | bytes 17301504 | tf_op jit(solution)/shard_map/reduce_scatter | solution.py:288
  647.7 0.9 copy-start.24
  647.7 1134.9 %reduce-scatter.17.cloned.1.call-start = ((), (), s32[]{:S(2)}) async-start(), calls=%async_computation.15 | async-start | bytes 17301504 | tf_op jit(solution)/shard_map/reduce_scatter | solution.py:289
  669.4 102.2 %copy-start.25 = (f32[32,1024]{1,0:T(8,128)S(1)}, f32[32,1024]{1,0:T(8,128)}, u32[]{:S(2)}) copy-start(f32[32,1024]{1,0:T(8,128)} %param.40) | copy-start | bytes 393220
  669.4 102.2 %copy-start.26 = (f32[32,1024]{1,0:T(8,128)S(1)}, f32[32,1024]{1,0:T(8,128)}, u32[]{:S(2)}) copy-start(f32[32,1024]{1,0:T(8,128)} %param.42) | copy-start | bytes 393220
  669.4 102.2 %copy-start.27 = (f32[32,1024]{1,0:T(8,128)S(1)}, f32[32,1024]{1,0:T(8,128)}, u32[]{:S(2)}) copy-start(f32[32,1024]{1,0:T(8,128)} %param.41) | copy-start | bytes 393220
  679.7 226.8 %copy-start.31 = (f32[4,32]{1,0:T(4,128)S(1)}, f32[4,32]{1,0:T(4,128)}, u32[]{:S(2)}) copy-start(f32[4,32]{1,0:T(4,128)} %param.49) | copy-start | bytes 1540
  679.7 226.8 %copy-start.32 = (f32[4,32]{1,0:T(4,128)S(1)}, f32[4,32]{1,0:T(4,128)}, u32[]{:S(2)}) copy-start(f32[4,32]{1,0:T(4,128)} %param.51) | copy-start | bytes 1540
  679.7 226.8 %copy-start.33 = (f32[4,32]{1,0:T(4,128)S(1)}, f32[4,32]{1,0:T(4,128)}, u32[]{:S(2)}) copy-start(f32[4,32]{1,0:T(4,128)} %param.50) | copy-start | bytes 1540
  679.7 383.7 %copy-start.21 = (f32[32,3072]{1,0:T(8,128)S(1)}, f32[32,3072]{1,0:T(8,128)}, u32[]{:S(2)}) copy-start(f32[32,3072]{1,0:T(8,128)} %param.37) | copy-start | bytes 1179652
  679.7 383.7 %copy-start.22 = (f32[32,3072]{1,0:T(8,128)S(1)}, f32[32,3072]{1,0:T(8,128)}, u32[]{:S(2)}) copy-start(f32[32,3072]{1,0:T(8,128)} %param.39) | copy-start | bytes 1179652
  775.0 647.9 %copy-start.14 = (f32[32,4096]{1,0:T(8,128)S(1)}, f32[32,4096]{1,0:T(8,128)}, u32[]{:S(2)}) copy-start(f32[32,4096]{1,0:T(8,128)} %param.43) | copy-start | bytes 1572868
  775.0 647.9 %copy-start.15 = (f32[32,4096]{1,0:T(8,128)S(1)}, f32[32,4096]{1,0:T(8,128)}, u32[]{:S(2)}) copy-start(f32[32,4096]{1,0:T(8,128)} %param.45) | copy-start | bytes 1572868
  775.0 647.9 %copy-start.16 = (f32[32,4096]{1,0:T(8,128)S(1)}, f32[32,4096]{1,0:T(8,128)}, u32[]{:S(2)}) copy-start(f32[32,4096]{1,0:T(8,128)} %param.44) | copy-start | bytes 1572868
  1066.5 716.2 %copy-start.17 = (f32[128,1024]{1,0:T(8,128)S(1)}, f32[128,1024]{1,0:T(8,128)}, u32[]{:S(2)}) copy-start(f32[128,1024]{1,0:T(8,128)} %param.46) | copy-start | bytes 1572868
  1066.5 716.2 %copy-start.18 = (f32[128,1024]{1,0:T(8,128)S(1)}, f32[128,1024]{1,0:T(8,128)}, u32[]{:S(2)}) copy-start(f32[128,1024]{1,0:T(8,128)} %param.48) | copy-start | bytes 1572868
  1066.5 716.2 %copy-start.19 = (f32[128,1024]{1,0:T(8,128)S(1)}, f32[128,1024]{1,0:T(8,128)}, u32[]{:S(2)}) copy-start(f32[128,1024]{1,0:T(8,128)} %param.47) | copy-start | bytes 1572868
  (1 other events, 0.7 us)
Sparse Core Ops, SparseCore 0:
  10.2 101.7 all-gather.5
  117.0 71.5 all-gather.7
  190.7 47.5 all-gather.9
  240.3 123.4 all-gather.11
  365.7 123.1 all-gather.13
  538.9 86.2 reduce-scatter.8
  627.5 143.9 reduce-scatter.12
  774.4 131.2 reduce-scatter.18
  911.8 151.6 reduce-scatter.10
  1065.7 357.1 reduce-scatter.14
  1425.3 357.3 reduce-scatter.16
where the time goes:
time: 1800 us; the launch traced here: 1790 us
  waiting for transfers between devices  1570 us (87%)
  matrix products  103 us (6%)
  local copies, waits for them, and re-layouts  41.2 us (2%)
  blocking collectives  30.5 us (2%)
  other arithmetic  29.1 us (2%)
    reduce_scatter x1, waiting for transfers between devices, body(): lax.psum_scatter(down_term, ('grp', 'shard'), scatter_dimension=0, tiled=...  357 us
    reduce_scatter x1, waiting for transfers between devices, body(): lax.psum_scatter(up_term, ('grp', 'shard'), scatter_dimension=0, tiled=True)  356 us
    reduce_scatter x1, waiting for transfers between devices, body(): lax.psum_scatter(qkv_term, ('grp', 'shard'), scatter_dimension=0, tiled=T...  156 us
    unnamed x12, waiting for transfers between devices  133 us
    all_gather x1, waiting for transfers between devices, body(): lax.all_gather(up_weight, 'shard', axis=0, tiled=True)  123 us
    all_gather x1, waiting for transfers between devices, body(): lax.all_gather(down_weight, 'shard', axis=0, tiled=True)  119 us
    reduce_scatter x1, waiting for transfers between devices, body(): lax.psum_scatter(out_term, ('grp', 'shard'), scatter_dimension=0, tiled=T...  91.8 us
    reduce_scatter x1, waiting for transfers between devices, body(): lax.psum_scatter(grad_pairs.astype(jnp.bfloat16), 'shard', scatter_dimens...  82.4 us
  transfers between devices with their start and end apart: 11, of which 11 were waited for; matrix products, arithmetic and copies ran while one was open for 6% of the time, Pallas kernels for 0%

commit v1 on v0

--- a/solution.py
+++ b/solution.py
@@ -3,6 +3,8 @@
 import jax
 import jax.numpy as jnp
 from jax import lax
+from jax.experimental import pallas as pl
+from jax.experimental.pallas import tpu as pltpu
 from jax.sharding import PartitionSpec as P
 
 HEADS = 16
@@ -335,6 +337,792 @@
     )
 
 
+MESH = pl.DeviceIdType.MESH
+F32, LOW = jnp.float32, jnp.bfloat16
+VMEM = pl.BlockSpec(memory_space=pltpu.VMEM)
+SHARDS, GROUPS = 8, 4
+WIDTH, ROWS, HALF = 1024, 128, 64
+LANES = 128
+DMA = pltpu.SemaphoreType.DMA
+
+
+class Place:
+    def __init__(self):
+        self.g, self.s = lax.axis_index("grp"), lax.axis_index("shard")
+        self.z, self.y = self.s // 2, self.s % 2
+        self.x, self.c = self.g // 2, self.g % 2
+        self.across = (self.g, self.s + 1 - 2 * self.y)
+        self.up = (self.g, self.s + 2)
+        self.down = (self.g, self.s - 2)
+        self.sibling = (self.g + 1 - 2 * self.c, self.s)
+        self.beside = ((self.g + 2) % GROUPS, self.s)
+
+    def at_shard(self, k):
+        return (self.g, (self.s + k) % SHARDS)
+
+    def from_shard(self, k):
+        return (self.s + SHARDS - k) % SHARDS
+
+
+def remote(src, dst, send, recv, device):
+    return pltpu.make_async_remote_copy(
+        src_ref=src, dst_ref=dst, send_sem=send, recv_sem=recv, device_id=device, device_id_type=MESH
+    )
+
+
+def greet(devices):
+    barrier = pltpu.get_barrier_semaphore()
+    for device in devices:
+        pl.semaphore_signal(barrier, inc=1, device_id=device, device_id_type=MESH)
+    pl.semaphore_wait(barrier, len(devices))
+
+
+def rows_of(ref):
+    return ref[...].reshape(-1, ref.shape[-1])
+
+
+def dot(left, right):
+    return lax.dot_general(left, right, (((1,), (0,)), ((), ())), preferred_element_type=F32)
+
+
+def dot_nt(left, right):
+    return lax.dot_general(left, right, (((1,), (1,)), ((), ())), preferred_element_type=F32)
+
+
+def dot_tn(left, right):
+    return lax.dot_general(left, right, (((0,), (0,)), ((), ())), preferred_element_type=F32)
+
+
+def gather_sems():
+    return [DMA((3, 4)), DMA((SHARDS,))]
+
+
+def plane_gather(here, block, sems):
+    send, recv = sems
+    z, y, s = here.z, here.y, here.s
+
+    def copy(lane, zz, yy):
+        device = (here.across, here.up, here.down)[lane]
+        i = zz * 2 + yy
+        return remote(block(i), block(i), send.at[lane, zz], recv.at[i], device)
+
+    def arrived(zz, yy):
+        copy(0, zz, yy).wait_recv()
+
+    @pl.when(z < 3)
+    def _():
+        copy(1, z, y).start()
+
+    @pl.when(z > 0)
+    def _():
+        copy(2, z, y).start()
+
+    copy(0, z, y).start()
+    yield
+    for step in range(1, 4):
+
+        @pl.when(z >= step)
+        def _():
+            zz = z - step
+            arrived(zz, y)
+
+            @pl.when(z < 3)
+            def _():
+                copy(1, zz, y).start()
+
+            copy(0, zz, y).start()
+
+        @pl.when(z + step <= 3)
+        def _():
+            zz = z + step
+            arrived(zz, y)
+
+            @pl.when(z > 0)
+            def _():
+                copy(2, zz, y).start()
+
+            copy(0, zz, y).start()
+
+        yield
+    for zz in range(4):
+        arrived(zz, 1 - y)
+        copy(0, zz, y).wait_send()
+
+        @pl.when((zz <= z) & (z < 3))
+        def _():
+            copy(1, zz, y).wait_send()
+
+        @pl.when((zz >= z) & (z > 0))
+        def _():
+            copy(2, zz, y).wait_send()
+
+    yield
+
+
+def sum_sems():
+    return [DMA((4,)), DMA((4,)), DMA((3,)), DMA((3,))]
+
+
+def sum_scratch(cols):
+    return [
+        pltpu.VMEM((4, ROWS, cols), LOW),
+        pltpu.VMEM((3, ROWS, cols), LOW),
+        pltpu.VMEM((3, ROWS, cols), LOW),
+    ]
+
+
+def plane_sum(here, part, total, scratch, sems):
+    landed, ready, final = scratch
+    y_send, y_recv, z_send, z_recv = sems
+    z, y = here.z, here.y
+    order = [(z + 2) % 4, 3 - z, z + 1 - 2 * (z % 2), z]
+    first = [
+        remote(part.at[zz * 2 + 1 - y], landed.at[i], y_send.at[i], y_recv.at[i], here.across)
+        for i, zz in enumerate(order)
+    ]
+    second = [
+        remote(ready.at[i], final.at[i], z_send.at[i], z_recv.at[i], (here.g, order[i] * 2 + y))
+        for i in range(3)
+    ]
+    for copy in first:
+        copy.start()
+    yield
+    for i, zz in enumerate(order):
+        first[i].wait_recv()
+        here_sum = part[zz * 2 + y].astype(F32) + landed[i].astype(F32)
+        if i < 3:
+            ready[i] = here_sum.astype(LOW)
+            second[i].start()
+        else:
+            total[...] = here_sum
+        yield
+    for copy in second:
+        copy.wait_recv()
+    total[...] += final[0].astype(F32) + final[1].astype(F32) + final[2].astype(F32)
+    for copy in first + second:
+        copy.wait_send()
+    yield
+
+
+def cross_sems():
+    return [DMA((2,)), DMA((2,)), DMA((1,)), DMA((1,))]
+
+
+def cross_scratch(rows, cols):
+    return [
+        pltpu.VMEM((2, rows, cols), LOW),
+        pltpu.VMEM((rows, cols), LOW),
+        pltpu.VMEM((rows, cols), LOW),
+    ]
+
+
+def cross_sum(here, part, total, scratch, sems):
+    landed, ready, final = scratch
+    c_send, c_recv, x_send, x_recv = sems
+    g, x, c = here.g, here.x, here.c
+    first = [
+        remote(part.at[xx * 2 + 1 - c], landed.at[xx], c_send.at[xx], c_recv.at[xx], here.sibling)
+        for xx in range(2)
+    ]
+    second = remote(ready, final, x_send.at[0], x_recv.at[0], here.beside)
+    for copy in first:
+        copy.start()
+    yield
+    for copy in first:
+        copy.wait_recv()
+    ready[...] = (part[(1 - x) * 2 + c].astype(F32) + landed[1 - x].astype(F32)).astype(LOW)
+    second.start()
+    yield
+    second.wait_recv()
+    total[...] = (
+        part[g].astype(F32) + landed[x].astype(F32) + final[...].astype(F32)
+    ).astype(total.dtype).reshape(total.shape)
+    for copy in first + [second]:
+        copy.wait_send()
+    yield
+
+
+def trade_sems():
+    return [DMA((SHARDS,)), DMA((SHARDS,))]
+
+
+def plane_trade(here, mine, theirs, sems):
+    send, recv = sems
+
+    def copy(k):
+        device = here.at_shard(k)
+        return remote(mine.at[device[1]], theirs.at[here.s], send.at[k], recv.at[k], device)
+
+    theirs[here.s] = mine[here.s]
+    for k in range(1, SHARDS):
+        copy(k).start()
+    yield
+    for k in range(1, SHARDS):
+        copy(k).wait_recv()
+    for k in range(1, SHARDS):
+        copy(k).wait_send()
+    yield
+
+
+def run(*steps):
+    for step in steps:
+        for _ in step:
+            pass
+
+
+def centre(values):
+    mean = jnp.mean(values, -1, keepdims=True)
+    centred = values - mean
+    variance = jnp.mean(centred * centred, -1, keepdims=True)
+    inverse = lax.rsqrt(variance + eps_norm)
+    return centred * inverse, inverse
+
+
+def wide(norm, row):
+    return jnp.concatenate([norm[j, row : row + 1, :] for j in range(SHARDS)], 1)
+
+
+def head_lanes(rows):
+    lane = lax.broadcasted_iota(jnp.int32, (rows, LANES), 1)
+    return [lane < HEAD_DIM, lane >= HEAD_DIM]
+
+
+def forward_kernel(
+    tok, cot, own_items, key_items, live, own_norm, wqkv, wout, wup,
+    norm, wq, wo, wu, a1, a2, dz, qkv, probs, attended, mixed, n2, r2,
+    o_send, norm_send, norm_recv, wq_send, wq_recv, wq_sib, wu_send, wu_recv, wu_sib, wo_sib,
+    o_ssem, o_rsem, a1_s, a1_r, wo_s, wo_r, dz_s, dz_r, a2_s, a2_r,
+):
+    here = Place()
+    g, s, c = here.g, here.s, here.c
+    greet([here.at_shard(k) for k in range(1, SHARDS)] + [here.sibling])
+    half = pl.ds(pl.multiple_of(c * HALF, HALF), HALF)
+
+    norm[s] = own_norm[...]
+
+    def norm_copy(k):
+        return remote(own_norm, norm.at[s], norm_send.at[k], norm_recv.at[k], here.at_shard(k))
+
+    def column_copy(weight, held, send, recv, k, parts, width):
+        device = here.at_shard(k)
+        return [
+            remote(
+                weight.at[half, pl.ds(pl.multiple_of(j * WIDTH + device[1] * width, LANES), width)],
+                held.at[s, c, :, pl.ds(j * width, width)],
+                send.at[k],
+                recv.at[k],
+                device,
+            )
+            for j in range(parts)
+        ]
+
+    def whole(held, send, recv, k):
+        return remote(
+            held.at[here.from_shard(k), c], held.at[here.from_shard(k), c], send.at[k], recv.at[k], here.at_shard(k)
+        )
+
+    for k in range(1, SHARDS):
+        norm_copy(k).start()
+    for k in range(1, SHARDS):
+        for copy in column_copy(wqkv, wq, wq_send, wq_recv, k, 3, LANES):
+            copy.start()
+    for j in range(3):
+        wq[s, c, :, j * LANES : (j + 1) * LANES] = wqkv[
+            half, pl.ds(pl.multiple_of(j * WIDTH + s * LANES, LANES), LANES)
+        ]
+    inputs = tok[...].astype(F32)
+    n1, _ = centre(inputs)
+    for k in range(1, SHARDS):
+        norm_copy(k).wait_recv()
+    a1[s] = (n1 * wide(norm, 0) + wide(norm, 1)).astype(LOW)
+    step = plane_gather(here, lambda i: a1.at[i], (a1_s, a1_r))
+    next(step)
+    own = pl.ds(pl.multiple_of(s * ROWS, ROWS), ROWS)
+    dz[s] = (cot[...].astype(F32) * live[own, :].astype(F32)).astype(LOW)
+    for k in range(1, SHARDS):
+        whole(wq, wq_send, wq_recv, k).wait_recv()
+    wq_core = remote(wq.at[:, c], wq.at[:, c], wq_sib.at[0], wq_sib.at[1], here.sibling)
+    wq_core.start()
+    run(step)
+    wq_core.wait_recv()
+
+    wo[s, c] = wout[half, :]
+    wo_step = plane_gather(here, lambda i: wo.at[i, c], (wo_s, wo_r))
+    next(wo_step)
+
+    weight = wq[...].reshape(WIDTH, 3 * LANES)
+
+    def project(j, carry):
+        qkv[j] = dot(a1[j], weight).astype(LOW)
+        return carry
+
+    lax.fori_loop(0, SHARDS, project, 0)
+    keys = qkv[:, :, LANES : 2 * LANES].reshape(-1, LANES)
+    values = qkv[:, :, 2 * LANES :].reshape(-1, LANES)
+    mine = head_lanes(ROWS)
+
+    def o_copy(k):
+        device = here.at_shard(k)
+        return remote(o_send.at[device[1]], attended.at[s], o_ssem.at[k], o_rsem.at[k], device)
+
+    def attend(j):
+        queries = qkv[j, :, :LANES]
+        items = own_items[pl.ds(pl.multiple_of(j * ROWS, ROWS), ROWS), :]
+        allowed = items == key_items[...]
+        outs = []
+        for h in range(2):
+            scores = dot_nt(jnp.where(mine[h], queries, jnp.zeros_like(queries)), keys) * score_scale
+            scores = jnp.where(allowed, scores, -1e30)
+            peak = jnp.max(scores, -1, keepdims=True)
+            expo = jnp.exp(scores - peak)
+            chance = (expo / jnp.sum(expo, -1, keepdims=True)).astype(LOW)
+            probs[h, j] = chance
+            outs.append(dot(chance, values))
+        return jnp.where(mine[0], outs[0], outs[1]).astype(LOW)
+
+    def attend_step(k, carry):
+        j = (s + k) % SHARDS
+        o_send[j] = attend(j)
+        o_copy(k).start()
+        return carry
+
+    lax.fori_loop(1, 3, attend_step, 0)
+    next(wo_step)
+    lax.fori_loop(3, 5, attend_step, 0)
+    next(wo_step)
+    lax.fori_loop(5, 7, attend_step, 0)
+    next(wo_step)
+    lax.fori_loop(7, 8, attend_step, 0)
+    attended[s] = attend(s)
+    run(wo_step)
+    wo_core = remote(wo.at[:, c], wo.at[:, c], wo_sib.at[0], wo_sib.at[1], here.sibling)
+    wo_core.start()
+
+    for k in range(1, SHARDS):
+        for copy in column_copy(wup, wu, wu_send, wu_recv, k, 1, 4 * LANES):
+            copy.start()
+    wu[s, c] = wup[half, pl.ds(pl.multiple_of(s * 4 * LANES, LANES), 4 * LANES)]
+    dz_step = plane_gather(here, lambda i: dz.at[i], (dz_s, dz_r))
+    next(dz_step)
+
+    for k in range(1, SHARDS):
+        o_copy(k).wait_recv()
+    wo_core.wait_recv()
+    flat = jnp.concatenate([attended[j] for j in range(SHARDS)], 1)
+    h1 = inputs + dot(flat, wo[...].reshape(WIDTH, WIDTH))
+    mixed[...] = h1
+    normed, inverse = centre(h1)
+    n2[...] = normed
+    r2[...] = jnp.broadcast_to(inverse, (ROWS, LANES))
+    a2[s] = (normed * wide(norm, 2) + wide(norm, 3)).astype(LOW)
+    a2_step = plane_gather(here, lambda i: a2.at[i], (a2_s, a2_r))
+    for _ in range(4):
+        next(a2_step)
+        next(dz_step)
+    for k in range(1, SHARDS):
+        whole(wu, wu_send, wu_recv, k).wait_recv()
+    wu_core = remote(wu.at[:, c], wu.at[:, c], wu_sib.at[0], wu_sib.at[1], here.sibling)
+    wu_core.start()
+    run(dz_step, a2_step)
+    wu_core.wait_recv()
+    for k in range(1, SHARDS):
+        norm_copy(k).wait_send()
+        whole(wq, wq_send, wq_recv, k).wait_send()
+        whole(wu, wu_send, wu_recv, k).wait_send()
+        o_copy(k).wait_send()
+    for copy in (wq_core, wo_core, wu_core):
+        copy.wait_send()
+
+
+def middle_kernel(
+    a2, dz, wu, wd, wo, norm, n2, r2, live, cot, attended,
+    ffn, gup, gdown, gout, grad_out, grad_mixed, norm_two,
+    act, du, da2, total, do_send, lands, ready, final, y_s, y_r, z_s, z_r, o_ssem, o_rsem,
+):
+    here = Place()
+    s = here.s
+    greet([here.at_shard(k) for k in range(1, SHARDS)])
+    up = wu[...].reshape(WIDTH, -1)
+
+    def feed(j, carry):
+        u = dot(a2[j], up)
+        half_erf = 0.5 + 0.5 * lax.erf(u * (0.5**0.5))
+        activated = (u * half_erf).astype(LOW)
+        act[j] = activated
+        slope = half_erf + u * jnp.exp(-0.5 * u * u) * (1.0 / math.sqrt(2.0 * math.pi))
+        grad = (dot_nt(dz[j], wd[...]) * slope).astype(LOW)
+        du[j] = grad
+        da2[j] = dot_nt(grad, up).astype(LOW)
+        return carry
+
+    lax.fori_loop(0, SHARDS, feed, 0)
+    step = plane_sum(here, da2, total, (lands, ready, final), (y_s, y_r, z_s, z_r))
+    next(step)
+
+    def rest(j, carry):
+        ffn[j] = dot(act[j], wd[...]).astype(LOW)
+        return carry
+
+    lax.fori_loop(0, SHARDS, rest, 0)
+    next(step)
+    down = dot_tn(rows_of(act), rows_of(dz)).astype(LOW)
+    gdown[...] = down.reshape(gdown.shape)
+    next(step)
+    gup[...] = dot_tn(rows_of(a2), rows_of(du)).astype(LOW).reshape(gup.shape)
+    run(step)
+
+    e = total[...]
+    normed = n2[...]
+    scaled = e * wide(norm, 2)
+    mean_one = jnp.mean(scaled, -1, keepdims=True)
+    mean_two = jnp.mean(scaled * normed, -1, keepdims=True)
+    own = pl.ds(pl.multiple_of(s * ROWS, ROWS), ROWS)
+    upstream = cot[...].astype(F32) * live[own, :].astype(F32)
+    grad = r2[:, :1] * (scaled - mean_one - normed * mean_two) + upstream
+    grad_mixed[...] = grad
+    norm_two[0:1, :] = jnp.sum(e * normed, 0, keepdims=True)
+    norm_two[1:2, :] = jnp.sum(e, 0, keepdims=True)
+    low = grad.astype(LOW)
+    for k in range(SHARDS):
+        do_send[k] = dot_nt(low, wo[k].reshape(ROWS, WIDTH)).astype(LOW)
+    trade = plane_trade(here, do_send, grad_out, (o_ssem, o_rsem))
+    next(trade)
+    flat = jnp.concatenate([attended[j] for j in range(SHARDS)], 1)
+    gout[...] = dot_tn(flat, low).astype(LOW).reshape(gout.shape)
+    run(trade)
+
+
+def last_kernel(*refs):
+    (
+        qkv, probs, grad_out, a1, wq, norm, tok, ffn, gup, gdown, gout, norm_two, live,
+        block_sum, dx, qkv_sum, up_sum, out_sum, down_sum, norm_sum,
+        dqkv, da1, gq, first_total,
+        *scratch,
+    ) = refs
+    scratch = list(scratch)
+
+    def take(n):
+        out = scratch[:n]
+        del scratch[:n]
+        return out
+
+    here = Place()
+    g, s = here.g, here.s
+    gs = [(g + k) % GROUPS for k in range(1, GROUPS)]
+    away = (s // 2, (s % 2) * 4 + g)
+    home = (s // 4 + 2 * g, s % 4)
+    home = (home[1], home[0])
+    stays = (away[0] == g) & (away[1] == s)
+    barrier = pltpu.get_barrier_semaphore()
+    around = [here.at_shard(k) for k in range(1, SHARDS)] + [(k, s) for k in gs]
+    for device in around:
+        pl.semaphore_signal(barrier, inc=1, device_id=device, device_id_type=MESH)
+
+    @pl.when(stays)
+    def _():
+        pl.semaphore_wait(barrier, len(around))
+
+    @pl.when(jnp.logical_not(stays))
+    def _():
+        for device in (away, home):
+            pl.semaphore_signal(barrier, inc=1, device_id=device, device_id_type=MESH)
+        pl.semaphore_wait(barrier, len(around) + 2)
+
+    ffn_scr, ffn_sem = take(3), take(4)
+    d_scr, d_sem = take(3), take(4)
+    cross = {}
+    for name in ("up", "down", "out", "qkv"):
+        cross[name] = (take(3), take(4), take(1)[0])
+    trades = {}
+    for name in ("up", "out", "qkv"):
+        trades[name] = (take(1)[0], take(2))
+    away_buf, away_sem = take(1)[0], take(1)[0]
+    norm_mine, norm_land, norm_all, n_s, n_r, m_s, m_r = take(7)
+
+    steps = plane_sum(here, ffn, block_sum, ffn_scr, ffn_sem)
+    next(steps)
+    up_step = cross_sum(here, gup, cross["up"][2], cross["up"][0], cross["up"][1])
+    down_step = cross_sum(here, gdown, cross["down"][2], cross["down"][0], cross["down"][1])
+    out_step = cross_sum(here, gout, cross["out"][2], cross["out"][0], cross["out"][1])
+    next(up_step)
+    next(down_step)
+    next(out_step)
+
+    keys = qkv[:, :, LANES : 2 * LANES].reshape(-1, LANES)
+    values = qkv[:, :, 2 * LANES :].reshape(-1, LANES)
+    mine = head_lanes(ROWS)
+    dqkv[...] = jnp.zeros_like(dqkv)
+
+    def back(j, carry):
+        queries, outs = qkv[j, :, :LANES], grad_out[j]
+        grad_query, grad_key, grad_value = [], [], []
+        for h in range(2):
+            chance_low = probs[h, j]
+            chance = chance_low.astype(F32)
+            grad_chance = dot_nt(jnp.where(mine[h], outs, jnp.zeros_like(outs)), values)
+            inner = jnp.sum(chance * grad_chance, -1, keepdims=True)
+            grad_scores = (chance * (grad_chance - inner)).astype(LOW)
+            grad_query.append(dot(grad_scores, keys))
+            grad_key.append(dot_tn(grad_scores, queries))
+            grad_value.append(dot_tn(chance_low, outs))
+        dqkv[j, :, :LANES] = jnp.where(mine[0], grad_query[0], grad_query[1]) * score_scale
+        wide_mine = head_lanes(WIDTH)[0]
+        gk = jnp.where(wide_mine, grad_key[0], grad_key[1]) * score_scale
+        gv = jnp.where(wide_mine, grad_value[0], grad_value[1])
+        dqkv[:, :, LANES : 2 * LANES] += gk.reshape(SHARDS, ROWS, LANES)
+        dqkv[:, :, 2 * LANES :] += gv.reshape(SHARDS, ROWS, LANES)
+        return carry
+
+    lax.fori_loop(0, SHARDS // 2, back, 0)
+    next(steps)
+    next(up_step)
+    next(down_step)
+    next(out_step)
+    lax.fori_loop(SHARDS // 2, SHARDS, back, 0)
+    weight = wq[...].reshape(WIDTH, 3 * LANES)
+
+    def spread(j, carry):
+        da1[j] = dot_nt(dqkv[j].astype(LOW), weight).astype(LOW)
+        return carry
+
+    lax.fori_loop(0, SHARDS, spread, 0)
+    d_step = plane_sum(here, da1, first_total, d_scr, d_sem)
+    next(d_step)
+    gq[...] = dot_tn(rows_of(a1), rows_of(dqkv).astype(LOW)).astype(LOW).reshape(gq.shape)
+    q_step = cross_sum(here, gq, cross["qkv"][2], cross["qkv"][0], cross["qkv"][1])
+    next(q_step)
+    run(up_step, down_step, out_step)
+    up_trade = plane_trade(here, cross["up"][2], *trades["up"])
+    out_trade = plane_trade(here, cross["out"][2], *trades["out"])
+    next(up_trade)
+    next(out_trade)
+    moved = remote(cross["down"][2], away_buf, away_sem.at[0], away_sem.at[1], away)
+
+    @pl.when(jnp.logical_not(stays))
+    def _():
+        moved.start()
+
+    next(steps)
+    next(d_step)
+    run(q_step)
+    qkv_trade = plane_trade(here, cross["qkv"][2], *trades["qkv"])
+    next(qkv_trade)
+    next(d_step)
+    next(steps)
+    run(d_step)
+
+    e = first_total[...]
+    normed, inverse = centre(tok[...].astype(F32))
+    scaled = e * wide(norm, 0)
+    mean_one = jnp.mean(scaled, -1, keepdims=True)
+    mean_two = jnp.mean(scaled * normed, -1, keepdims=True)
+    own = pl.ds(pl.multiple_of(s * ROWS, ROWS), ROWS)
+    count = jnp.sum(live[own, :].astype(F32), 0, keepdims=True)
+    part = jnp.concatenate(
+        [
+            jnp.sum(e * normed, 0, keepdims=True),
+            jnp.sum(e, 0, keepdims=True),
+            norm_two[0:2, :],
+            jnp.broadcast_to(count, (4, WIDTH)),
+        ],
+        0,
+    )
+    for k in range(GROUPS):
+        norm_mine[k] = part[:, k * 2 * LANES : (k + 1) * 2 * LANES]
+
+    def grp_copy(k):
+        to = (g + k) % GROUPS
+        return remote(norm_mine.at[to], norm_land.at[k - 1], n_s.at[k], n_r.at[k], (to, s))
+
+    for k in range(1, GROUPS):
+        grp_copy(k).start()
+    dx[...] = inverse * (scaled - mean_one - normed * mean_two)
+    for k in range(1, GROUPS):
+        grp_copy(k).wait_recv()
+    norm_all[s] = norm_mine[g] + norm_land[0] + norm_land[1] + norm_land[2]
+
+    def all_copy(k):
+        return remote(norm_all.at[s], norm_all.at[s], m_s.at[k], m_r.at[k], here.at_shard(k))
+
+    for k in range(1, SHARDS):
+        all_copy(k).start()
+
+    run(steps, up_trade, out_trade, qkv_trade)
+    up_land, out_land, qkv_land = trades["up"][0], trades["out"][0], trades["qkv"][0]
+    for j in range(SHARDS):
+        up_sum[:, j * 512 : (j + 1) * 512] = up_land[j].astype(F32)
+        for i in range(3):
+            qkv_sum[:, i * WIDTH + j * LANES : i * WIDTH + (j + 1) * LANES] = qkv_land[
+                j, :, i * LANES : (i + 1) * LANES
+            ].astype(F32)
+    gathered = out_land[0].astype(F32)
+    for j in range(1, SHARDS):
+        gathered += out_land[j].astype(F32)
+    out_sum[...] = gathered
+
+    @pl.when(stays)
+    def _():
+        down_sum[...] = cross["down"][2][...].astype(F32)
+
+    @pl.when(jnp.logical_not(stays))
+    def _():
+        moved.wait_recv()
+        down_sum[...] = away_buf[...].astype(F32)
+        moved.wait_send()
+
+    for k in range(1, SHARDS):
+        all_copy(k).wait_recv()
+    reduced = norm_all[0]
+    for j in range(1, SHARDS):
+        reduced += norm_all[j]
+    norm_sum[...] = reduced
+    for k in range(1, GROUPS):
+        grp_copy(k).wait_send()
+    for k in range(1, SHARDS):
+        all_copy(k).wait_send()
+
+
+def params(ident):
+    return pltpu.CompilerParams(
+        collective_id=ident, has_side_effects=True, vmem_limit_bytes=60 * 2**20
+    )
+
+
+def shaped(kind, *shape):
+    return jax.ShapeDtypeStruct(shape, kind)
+
+
+def call(kernel, ident, outs, scratch, args):
+    return pl.pallas_call(
+        kernel,
+        out_shape=outs,
+        in_specs=[VMEM] * len(args),
+        out_specs=[VMEM] * len(outs),
+        scratch_shapes=scratch,
+        compiler_params=params(ident),
+    )(*args)
+
+
+def fast_body(
+    tokens, cotangent, item_ids, live_mask, qkv_weight, out_weight, up_weight, down_weight, norm_weight,
+    qkv_master, qkv_first, qkv_second, out_master, out_first, out_second, up_master, up_first, up_second,
+    down_master, down_first, down_second, norm_master, norm_first, norm_second,
+):
+    rows = item_ids.shape[0]
+    own_norm = jnp.pad(norm_weight.astype(F32), ((0, 4), (0, 0)))
+    key_items = jnp.where(live_mask > 0, item_ids, -1).reshape(1, rows)
+    own_items = item_ids.reshape(rows, 1)
+    live = live_mask.reshape(rows, 1)
+    norm, wq, wo, wu, a1, a2, dz, qkv, probs, attended, mixed, n2, r2 = call(
+        forward_kernel,
+        0,
+        [
+            shaped(F32, SHARDS, 8, LANES),
+            shaped(LOW, SHARDS, 2, HALF, 3 * LANES),
+            shaped(LOW, SHARDS, 2, HALF, WIDTH),
+            shaped(LOW, SHARDS, 2, HALF, 4 * LANES),
+            shaped(LOW, SHARDS, ROWS, WIDTH),
+            shaped(LOW, SHARDS, ROWS, WIDTH),
+            shaped(LOW, SHARDS, ROWS, WIDTH),
+            shaped(LOW, SHARDS, ROWS, 3 * LANES),
+            shaped(LOW, 2, SHARDS, ROWS, WIDTH),
+            shaped(LOW, SHARDS, ROWS, LANES),
+            shaped(F32, ROWS, WIDTH),
+            shaped(F32, ROWS, WIDTH),
+            shaped(F32, ROWS, LANES),
+        ],
+        [pltpu.VMEM((SHARDS, ROWS, LANES), LOW)]
+        + [DMA((SHARDS,))] * 4
+        + [DMA((2,))]
+        + [DMA((SHARDS,))] * 2
+        + [DMA((2,))] * 2
+        + [DMA((SHARDS,))] * 2
+        + gather_sems() * 4,
+        (tokens, cotangent, own_items, key_items, live, own_norm, qkv_weight, out_weight, up_weight),
+    )
+    ffn, gup, gdown, gout, grad_out, grad_mixed, norm_two = call(
+        middle_kernel,
+        1,
+        [
+            shaped(LOW, SHARDS, ROWS, WIDTH),
+            shaped(LOW, GROUPS, 256, 512),
+            shaped(LOW, GROUPS, ROWS, WIDTH),
+            shaped(LOW, GROUPS, 256, WIDTH),
+            shaped(LOW, SHARDS, ROWS, LANES),
+            shaped(F32, ROWS, WIDTH),
+            shaped(F32, 8, WIDTH),
+        ],
+        [
+            pltpu.VMEM((SHARDS, ROWS, 512), LOW),
+            pltpu.VMEM((SHARDS, ROWS, 512), LOW),
+            pltpu.VMEM((SHARDS, ROWS, WIDTH), LOW),
+            pltpu.VMEM((ROWS, WIDTH), F32),
+            pltpu.VMEM((SHARDS, ROWS, LANES), LOW),
+        ]
+        + sum_scratch(WIDTH)
+        + sum_sems()
+        + trade_sems(),
+        (a2, dz, wu, down_weight, wo, norm, n2, r2, live, cotangent, attended),
+    )
+    scratch = [
+        pltpu.VMEM((SHARDS, ROWS, 3 * LANES), F32),
+        pltpu.VMEM((SHARDS, ROWS, WIDTH), LOW),
+        pltpu.VMEM((GROUPS, 256, 3 * LANES), LOW),
+        pltpu.VMEM((ROWS, WIDTH), F32),
+    ]
+    for _ in range(2):
+        scratch += sum_scratch(WIDTH) + sum_sems()
+    for r, cols in ((256, 512), (ROWS, WIDTH), (256, WIDTH), (256, 3 * LANES)):
+        total = (SHARDS, r // SHARDS, cols) if r == 256 else (r, cols)
+        scratch += cross_scratch(r, cols) + cross_sems() + [pltpu.VMEM(total, LOW)]
+    for cols in (512, WIDTH, 3 * LANES):
+        scratch += [pltpu.VMEM((SHARDS, 32, cols), LOW)] + trade_sems()
+    scratch += [pltpu.VMEM((ROWS, WIDTH), LOW), DMA((2,))]
+    scratch += [
+        pltpu.VMEM((GROUPS, 8, 256), F32),
+        pltpu.VMEM((GROUPS - 1, 8, 256), F32),
+        pltpu.VMEM((SHARDS, 8, 256), F32),
+        DMA((GROUPS,)),
+        DMA((GROUPS,)),
+        DMA((SHARDS,)),
+        DMA((SHARDS,)),
+    ]
+    block_sum, dx, qkv_sum, up_sum, out_sum, down_sum, norm_sum = call(
+        last_kernel,
+        2,
+        [
+            shaped(F32, ROWS, WIDTH),
+            shaped(F32, ROWS, WIDTH),
+            shaped(F32, 32, 3 * WIDTH),
+            shaped(F32, 32, 4 * WIDTH),
+            shaped(F32, 32, WIDTH),
+            shaped(F32, ROWS, WIDTH),
+            shaped(F32, 8, 256),
+        ],
+        scratch,
+        (qkv, probs, grad_out, a1, wq, norm, tokens, ffn, gup, gdown, gout, norm_two, live),
+    )
+    block_out = mixed + block_sum
+    input_grad = dx + grad_mixed
+    columns = norm_master.shape[1]
+    norm_own = lax.dynamic_slice(norm_sum, (0, lax.axis_index("shard") * columns), (8, columns))
+    total_count = norm_own[4, 0]
+    model_width, hidden = tokens.shape[1], up_weight.shape[1]
+    return (
+        block_out,
+        input_grad,
+        *adamw(qkv_sum, total_count, qkv_master, qkv_first, qkv_second, model_width ** (-0.5), 0.1),
+        *adamw(out_sum, total_count, out_master, out_first, out_second, math.sqrt(rows) / 64, 0.1),
+        *adamw(up_sum, total_count, up_master, up_first, up_second, model_width ** (-0.5), 0.1),
+        *adamw(down_sum, total_count, down_master, down_first, down_second, hidden ** (-0.5), 0.1),
+        *adamw(norm_own[:4], total_count, norm_master, norm_first, norm_second, 0.4, 0.0),
+    )
+
+
+def suits(mesh):
+    return mesh.shape["grp"] == GROUPS and mesh.shape["shard"] == SHARDS
+
+
 def solution(mesh):
     placed = (
         P(("grp", "shard"), None),
@@ -363,7 +1151,7 @@
         P(None, ("grp", "shard")),
     )
     return jax.shard_map(
-        body,
+        fast_body if suits(mesh) else body,
         mesh=mesh,
         in_specs=placed,
         out_specs=(

time: 1800 us -> 308 us (0.17)
  waiting for transfers between devices: 1570 us -> 0 us
  Pallas kernels: 0 us -> 287 us
  matrix products: 103 us -> 0 us
  local copies, waits for them, and re-layouts: 41.2 us -> 4.81 us
  blocking collectives: 30.5 us -> 0 us
    reduce_scatter x5 -> x0, waiting for transfers between devices: 1040 us -> none  [the longest x1 357 us: body(): lax.psum_scatter(down_term, ('grp', 'shard'), scatter_dimension=0, tiled=...]
    all_gather x5 -> x0, waiting for transfers between devices: 397 us -> none  [the longest x1 123 us: body(): lax.all_gather(up_weight, 'shard', axis=0, tiled=True)]
    pallas_call x0 -> x3, Pallas kernels: none -> 287 us  [call(): pl.pallas_call(kernel, out_shape=outs, in_specs=[VMEM] * len(args), out_s...]
    unnamed x12 -> x0, waiting for transfers between devices: 133 us -> none
    dot_general x26 -> x0, matrix products: 103 us -> none  [the longest x4 28.2 us: outer_sum(): lax.dot_general(left, right, (((0,), (0,)), ((), ())), preferred_element_...]
    all_gather x1 -> x0, blocking collectives: 22.7 us -> none  [body(): lax.all_gather(norm_weight, 'shard', axis=1, tiled=True)]
  transfers between devices with their start and end apart: 11 -> 0, of which waited for: 11 -> 0; matrix products, arithmetic and copies ran while one was open for 6% -> 0% of each run, Pallas kernels for 0% -> 0%
where the time goes in v1:
time: 308 us; the launch traced here: 307 us
  Pallas kernels  287 us (93%)
  other arithmetic  14.9 us (5%)
  local copies, waits for them, and re-layouts  4.81 us (2%)
    pallas_call x3, Pallas kernels, call(): pl.pallas_call(kernel, out_shape=outs, in_specs=[VMEM] * len(args), out_s...  287 us
    convert_element_type x5, other arithmetic, adamw(): return (gradient, moment, square, updated, updated.astype(jnp.bfloat16))  10.6 us

profile of v1, /device:TPU:0, one launch (start us, length us, event | category | flops | bytes accessed | tf_op | source)
XLA Modules:
  0.0 307.4 jit_solution(13477062860392058914)
XLA Ops:
  0.7 1.7 copy.52.live.refs_12_
  2.4 1.7 copy.51.own_items
  4.1 1.3 compare_select_fusion
  5.4 1.3 pad_convert_fusion.own_norm
  6.7 118.9 %shard_map.439 = (f32[8,8,128]{2,1,0:T(8,128)}, bf16[8,2,64,384]{3,2,1,0:T(8,128)(2,1)}, bf16[8,2,64,1024]{3,2,1,0:T(8,128)(2,1)}, bf16[8,2,64,512]{3,2,1,0:T(8,...) custom-call(bf16[128,1024]{1,0:T(8,128)(2,1)} %refs_6_.1, ...), custom_call_target="tpu_custom_call" | custom-call | tf_op jit(solution)/shard_map/pallas_call | solution.py:996
  125.6 52.7 %shard_map.440 = (bf16[8,128,1024]{2,1,0:T(8,128)(2,1)}, bf16[4,256,512]{2,1,0:T(8,128)(2,1)}, bf16[4,128,1024]{2,1,0:T(8,128)(2,1)}, bf16[4,256,1024]{2,1,0:T(8...) custom-call(bf16[8,128,1024]{2,1,0:T(8,128)(2,1)} %get-tuple-element.57.a2, ...), custom_call_target="tpu_custom_call" | custom-call | tf_op jit(solution)/shard_map/pallas_call | solution.py:996
  178.3 0.0 copy-start.19
  178.3 0.0 copy-start.20
  178.3 0.0 copy-start.21
  178.3 0.0 copy-start
  178.3 0.0 copy-start.1
  178.3 0.0 copy-start.2
  178.4 115.1 %shard_map.441 = (f32[128,1024]{1,0:T(8,128)}, f32[128,1024]{1,0:T(8,128)}, f32[32,3072]{1,0:T(8,128)}, f32[32,4096]{1,0:T(8,128)}, f32[32,1024]{1,0:T(8,128)}, /*index=5*/f32[128,1024]{1,0:T(8,128)}, f32[8,256]{1,0:T(8,128)}) custom-call(bf16[8,128,384]{2,1,0:T(8,128)(2,1)} %get-tuple-element.55.refs_0_, ...), custom_call_target="tpu_custom_call" | custom-call | tf_op jit(solution)/shard_map/pallas_call | solution.py:996
  293.5 0.8 constant_dynamic-slice_fusion
  294.3 0.5 slice.6
  294.8 0.0 copy-done.19
  294.8 0.0 copy-done.20
  294.8 0.0 copy-done.21
  294.8 1.3 fusion.5
  296.1 0.0 copy-done
  296.1 0.0 copy-done.1
  296.1 0.0 copy-done.2
  296.1 0.0 copy-start.3
  296.1 0.0 copy-start.4
  296.1 0.0 copy-start.5
  296.1 0.0 copy-start.10
  296.1 3.4 %fusion.7 = (bf16[128,1024]{1,0:T(8,128)(2,1)}, f32[128,1024]{1,0:T(8,128)}, f32[128,1024]{1,0:T(8,128)}, f32[128,1024]{1,0:T(8,128)}, f32[128,1024]{1,0:T(8,128)}) fusion(f32[128,1024]{1,0:T(8,128)S(1)} %copy-done, f32[128,1024]{1,0:T(8,128)S(1)} %copy-done.1, f32[128,1024]{1,0:T(8,128)S(1)} %copy-done.2, f32[128,1024]{1,0:T(8,128)} %get-tuple-element.80, ...), kind=kLoop, calls=%fused_computation.29 | loop fusion | flops 2097152 | bytes 4456452 | tf_op jit(solution)/shard_map/convert_element_type | solution.py:173
  299.5 0.0 copy-done.3
  299.5 0.0 copy-done.4
  299.5 0.0 copy-done.5
  299.5 0.0 copy-done.10
  299.5 0.0 copy-start.15
  299.6 0.0 copy-start.16
  299.6 0.0 copy-start.17
  299.6 0.0 copy-start.18
  299.6 0.0 copy-start.11
  299.6 0.0 copy-start.12
  299.6 0.0 copy-start.13
  299.6 0.0 copy-start.14
  299.6 2.3 fusion.9
  302.0 0.0 copy-done.16
  302.0 1.6 fusion.11
  303.6 0.0 copy-done.11
  303.6 0.0 copy-done.13
  303.6 2.0 fusion.13
  305.6 0.0 copy-done.7
  305.6 0.9 add.87
  306.5 0.9 add.86
  (12 shorter events, 0.0 us)
Async XLA Ops:
  178.3 116.5 %copy-start.19 = (f32[4,32]{1,0:T(4,128)S(1)}, f32[4,32]{1,0:T(4,128)}, u32[]{:S(2)}) copy-start(f32[4,32]{1,0:T(4,128)} %param.45) | copy-start | bytes 1540
  178.3 116.5 %copy-start.20 = (f32[4,32]{1,0:T(4,128)S(1)}, f32[4,32]{1,0:T(4,128)}, u32[]{:S(2)}) copy-start(f32[4,32]{1,0:T(4,128)} %param.47) | copy-start | bytes 1540
  178.3 116.5 %copy-start.21 = (f32[4,32]{1,0:T(4,128)S(1)}, f32[4,32]{1,0:T(4,128)}, u32[]{:S(2)}) copy-start(f32[4,32]{1,0:T(4,128)} %param.46) | copy-start | bytes 1540
  178.3 117.7 %copy-start = (f32[128,1024]{1,0:T(8,128)S(1)}, f32[128,1024]{1,0:T(8,128)}, u32[]{:S(2)}) copy-start(f32[128,1024]{1,0:T(8,128)} %param.42) | copy-start | bytes 1572868
  178.3 117.7 %copy-start.1 = (f32[128,1024]{1,0:T(8,128)S(1)}, f32[128,1024]{1,0:T(8,128)}, u32[]{:S(2)}) copy-start(f32[128,1024]{1,0:T(8,128)} %param.44) | copy-start | bytes 1572868
  178.3 117.7 %copy-start.2 = (f32[128,1024]{1,0:T(8,128)S(1)}, f32[128,1024]{1,0:T(8,128)}, u32[]{:S(2)}) copy-start(f32[128,1024]{1,0:T(8,128)} %param.43) | copy-start | bytes 1572868
  296.1 3.5 %copy-start.3 = (f32[32,4096]{1,0:T(8,128)S(1)}, f32[32,4096]{1,0:T(8,128)}, u32[]{:S(2)}) copy-start(f32[32,4096]{1,0:T(8,128)} %param.39) | copy-start | bytes 1572868
  296.1 3.4 %copy-start.4 = (f32[32,4096]{1,0:T(8,128)S(1)}, f32[32,4096]{1,0:T(8,128)}, u32[]{:S(2)}) copy-start(f32[32,4096]{1,0:T(8,128)} %param.41) | copy-start | bytes 1572868
  296.1 3.4 %copy-start.5 = (f32[32,4096]{1,0:T(8,128)S(1)}, f32[32,4096]{1,0:T(8,128)}, u32[]{:S(2)}) copy-start(f32[32,4096]{1,0:T(8,128)} %param.40) | copy-start | bytes 1572868
  296.1 3.4 %copy-start.10 = (f32[32,4096]{1,0:T(8,128)S(1)}, f32[32,4096]{1,0:T(8,128)}, u32[]{:S(2)}) copy-start(f32[32,4096]{1,0:T(8,128)} %get-tuple-element.79) | copy-start | bytes 1572868
  299.5 2.4 copy-start.15
  299.6 2.4 copy-start.16
  299.6 2.4 copy-start.17
  299.6 2.4 copy-start.18
  299.6 4.0 %copy-start.11 = (f32[32,3072]{1,0:T(8,128)S(1)}, f32[32,3072]{1,0:T(8,128)}, u32[]{:S(2)}) copy-start(f32[32,3072]{1,0:T(8,128)} %param.33) | copy-start | bytes 1179652
  299.6 4.0 %copy-start.12 = (f32[32,3072]{1,0:T(8,128)S(1)}, f32[32,3072]{1,0:T(8,128)}, u32[]{:S(2)}) copy-start(f32[32,3072]{1,0:T(8,128)} %param.35) | copy-start | bytes 1179652
  299.6 4.0 %copy-start.13 = (f32[32,3072]{1,0:T(8,128)S(1)}, f32[32,3072]{1,0:T(8,128)}, u32[]{:S(2)}) copy-start(f32[32,3072]{1,0:T(8,128)} %param.34) | copy-start | bytes 1179652
  299.6 4.0 %copy-start.14 = (f32[32,3072]{1,0:T(8,128)S(1)}, f32[32,3072]{1,0:T(8,128)}, u32[]{:S(2)}) copy-start(f32[32,3072]{1,0:T(8,128)} %get-tuple-element.76) | copy-start | bytes 1179652
  302.0 3.7 %copy-start.7 = (f32[128,1024]{1,0:T(8,128)S(1)}, f32[128,1024]{1,0:T(8,128)}, u32[]{:S(2)}) copy-start(f32[128,1024]{1,0:T(8,128)} %get-tuple-element.75) | copy-start | bytes 1572868
  302.0 3.7 %copy-start.9 = (f32[128,1024]{1,0:T(8,128)S(1)}, f32[128,1024]{1,0:T(8,128)}, u32[]{:S(2)}) copy-start(f32[128,1024]{1,0:T(8,128)} %get-tuple-element.74) | copy-start | bytes 1572868
  303.6 2.9 copy-start.6
  303.6 2.9 copy-start.8

commit v2 on v0

--- a/solution.py
+++ b/solution.py
@@ -3,6 +3,8 @@
 import jax
 import jax.numpy as jnp
 from jax import lax
+from jax.experimental import pallas as pl
+from jax.experimental.pallas import tpu as pltpu
 from jax.sharding import PartitionSpec as P
 
 HEADS = 16
@@ -335,6 +337,1022 @@
     )
 
 
+MESH = pl.DeviceIdType.MESH
+F32, LOW = jnp.float32, jnp.bfloat16
+VMEM = pl.BlockSpec(memory_space=pltpu.VMEM)
+ANY = pl.BlockSpec(memory_space=pl.ANY)
+SHARDS, GROUPS = 8, 4
+WIDTH, ROWS, LANES = 1024, 128, 128
+HIDDEN = 512
+DMA = pltpu.SemaphoreType.DMA
+
+
+class Place:
+    def __init__(self):
+        self.g, self.s = lax.axis_index("grp"), lax.axis_index("shard")
+        self.z, self.y = self.s // 2, self.s % 2
+        self.x, self.c = self.g // 2, self.g % 2
+        self.half, self.near = self.z // 2, self.z % 2
+        self.corner = self.near * 2 + self.y
+        g, s = self.g, self.s
+        over = 1 - 2 * self.y
+        along = 2 - 4 * self.near
+        self.across = (g, s + over)
+        self.up = (g, s + 2)
+        self.down = (g, s - 2)
+        self.far = (g, (s + 4) % SHARDS)
+        self.sibling = (g + 1 - 2 * self.c, s)
+        self.beside = ((g + 2) % GROUPS, s)
+        self.square = [(g, s), self.across, (g, s + along), (g, s + along + over)]
+        self.corners = [
+            self.corner,
+            self.corner + over,
+            (self.corner + 2) % 4,
+            (self.corner + over + 2) % 4,
+        ]
+
+    def at_shard(self, k):
+        return (self.g, (self.s + k) % SHARDS)
+
+    def from_shard(self, k):
+        return (self.s + SHARDS - k) % SHARDS
+
+
+def remote(src, dst, send, recv, device):
+    return pltpu.make_async_remote_copy(
+        src_ref=src, dst_ref=dst, send_sem=send, recv_sem=recv, device_id=device, device_id_type=MESH
+    )
+
+
+def greet_all(here):
+    barrier = pltpu.get_barrier_semaphore()
+    me, everyone = here.g * SHARDS + here.s, GROUPS * SHARDS
+
+    def greet(k, carry):
+        other = (me + k) % everyone
+        pl.semaphore_signal(
+            barrier, inc=1, device_id=(other // SHARDS, other % SHARDS), device_id_type=MESH
+        )
+        return carry
+
+    lax.fori_loop(1, everyone, greet, 0)
+    pl.semaphore_wait(barrier, everyone - 1)
+
+
+def flat(value):
+    return value.reshape(-1, value.shape[-1])
+
+
+def dot(left, right):
+    return lax.dot_general(left, right, (((1,), (0,)), ((), ())), preferred_element_type=F32)
+
+
+def dot_nt(left, right):
+    return lax.dot_general(left, right, (((1,), (1,)), ((), ())), preferred_element_type=F32)
+
+
+def dot_tn(left, right):
+    return lax.dot_general(left, right, (((0,), (0,)), ((), ())), preferred_element_type=F32)
+
+
+def run(*steps):
+    for step in steps:
+        for _ in step:
+            pass
+
+
+def buffer(kind, *shape):
+    return pltpu.VMEM(shape, kind)
+
+
+def gather_sems():
+    return [DMA((3, 4)), DMA((SHARDS,))]
+
+
+def plane_gather(here, block, sems, ends):
+    send, recv = sems
+    z, y = here.z, here.y
+
+    def copy(lane, zz, yy):
+        device = (here.across, here.up, here.down)[lane]
+        i = zz * 2 + yy
+        return remote(block(i), block(i), send.at[lane, zz], recv.at[i], device)
+
+    def arrived(zz, yy):
+        copy(0, zz, yy).wait_recv()
+
+    def finish():
+        for zz in range(4):
+            copy(0, zz, y).wait_send()
+
+            @pl.when((zz <= z) & (z < 3))
+            def _():
+                copy(1, zz, y).wait_send()
+
+            @pl.when((zz >= z) & (z > 0))
+            def _():
+                copy(2, zz, y).wait_send()
+
+    ends.append(finish)
+
+    @pl.when(z < 3)
+    def _():
+        copy(1, z, y).start()
+
+    @pl.when(z > 0)
+    def _():
+        copy(2, z, y).start()
+
+    copy(0, z, y).start()
+    yield
+    for step in range(1, 4):
+
+        @pl.when(z >= step)
+        def _():
+            zz = z - step
+            arrived(zz, y)
+
+            @pl.when(z < 3)
+            def _():
+                copy(1, zz, y).start()
+
+            copy(0, zz, y).start()
+
+        @pl.when(z + step <= 3)
+        def _():
+            zz = z + step
+            arrived(zz, y)
+
+            @pl.when(z > 0)
+            def _():
+                copy(2, zz, y).start()
+
+            copy(0, zz, y).start()
+
+        yield
+    for zz in range(4):
+        arrived(zz, 1 - y)
+    yield
+
+
+def sum_scratch(rows):
+    shape = (4, rows, WIDTH)
+    return [buffer(LOW, *shape), buffer(LOW, *shape), buffer(LOW, 2, *shape)] + [DMA((4,))] * 3 + [DMA((2, 4))]
+
+
+def plane_sum(here, part, total, scratch, ends, prepare=None):
+    landed, ready, relayed, y_send, y_recv, z_send, z_recv = scratch
+    z, y = here.z, here.y
+    order = [
+        jnp.where(z < 2, 3, 0),
+        jnp.where(z == 0, 2, jnp.where(z == 1, 0, jnp.where(z == 2, 3, 1))),
+        1 + z % 2,
+        z,
+    ]
+    first = [
+        remote(part.at[zz * 2 + 1 - y], landed.at[i], y_send.at[i], y_recv.at[i], here.across)
+        for i, zz in enumerate(order)
+    ]
+
+    def relay(lane, zz):
+        device = (here.up, here.down)[lane]
+        return remote(ready.at[zz], relayed.at[lane, zz], z_send.at[zz], z_recv.at[lane, zz], device)
+
+    for i, zz in enumerate(order):
+        if prepare is not None:
+            prepare(zz)
+        first[i].start()
+    yield
+    for i, zz in enumerate(order):
+        first[i].wait_recv()
+        if i < 3:
+            ready[zz] = (part[zz * 2 + y].astype(F32) + landed[i].astype(F32)).astype(LOW)
+
+            @pl.when(zz > z)
+            def _():
+                @pl.when(z > 0)
+                def _():
+                    relay(0, zz).wait_recv()
+                    ready[zz] = (ready[zz].astype(F32) + relayed[0, zz].astype(F32)).astype(LOW)
+
+                relay(0, zz).start()
+
+            @pl.when(zz < z)
+            def _():
+                @pl.when(z < 3)
+                def _():
+                    relay(1, zz).wait_recv()
+                    ready[zz] = (ready[zz].astype(F32) + relayed[1, zz].astype(F32)).astype(LOW)
+
+                relay(1, zz).start()
+
+        else:
+            total[...] = part[zz * 2 + y].astype(F32) + landed[i].astype(F32)
+        yield
+
+    @pl.when(z > 0)
+    def _():
+        relay(0, z).wait_recv()
+        total[...] += relayed[0, z].astype(F32)
+
+    @pl.when(z < 3)
+    def _():
+        relay(1, z).wait_recv()
+        total[...] += relayed[1, z].astype(F32)
+
+    def finish():
+        for copy in first:
+            copy.wait_send()
+        for zz in order[:3]:
+            relay(0, zz).wait_send()
+
+    ends.append(finish)
+    yield
+
+
+def square_gather(here, held, sems, ends):
+    send, recv, sib_send, sib_recv = sems
+    c = here.c
+
+    def copy(i):
+        block = held.at[c, here.corner]
+        return remote(block, block, send.at[i], recv.at[i], here.square[i])
+
+    def came(i):
+        block = held.at[c, here.corners[i]]
+        return remote(block, block, send.at[i], recv.at[i], here.square[i])
+
+    def pass_on(i):
+        block = held.at[c, here.corners[i]]
+        return remote(block, block, sib_send.at[i], sib_recv.at[i], here.sibling)
+
+    def passed(i):
+        block = held.at[1 - c, here.corners[i]]
+        return remote(block, block, sib_send.at[i], sib_recv.at[i], here.sibling)
+
+    def finish():
+        for i in range(1, 4):
+            copy(i).wait_send()
+        for i in range(4):
+            pass_on(i).wait_send()
+
+    ends.append(finish)
+    for i in (3, 1, 2):
+        copy(i).start()
+    pass_on(0).start()
+    yield
+    passed(0).wait_recv()
+    yield
+    for i in (1, 2, 3):
+        came(i).wait_recv()
+        pass_on(i).start()
+        passed(i).wait_recv()
+        yield
+
+
+def square_sems():
+    return [DMA((4,))] * 4
+
+
+def square_scratch():
+    shape = (4, ROWS, WIDTH)
+    return [buffer(LOW, *shape)] * 3 + [DMA((4,))] * 4
+
+
+def square_sum(here, part, total, scratch, ends):
+    landed, ready, final, sib_send, sib_recv, send, recv = scratch
+    c = here.c
+
+    def swap(i):
+        return remote(
+            part.at[1 - c, here.corners[i]], landed.at[i], sib_send.at[i], sib_recv.at[i], here.sibling
+        )
+
+    def ship(i):
+        return remote(ready.at[i], final.at[i], send.at[i], recv.at[i], here.square[i])
+
+    def start(i):
+        swap(i).start()
+
+    def go(i):
+        swap(i).wait_recv()
+        value = part[c, here.corners[i]].astype(F32) + landed[i].astype(F32)
+        if i:
+            ready[i] = value.astype(LOW)
+            ship(i).start()
+        else:
+            total[...] = value
+
+    def end():
+        for i in range(1, 4):
+            ship(i).wait_recv()
+        total[...] += final[1].astype(F32) + final[2].astype(F32) + final[3].astype(F32)
+
+    def finish():
+        for i in range(4):
+            swap(i).wait_send()
+        for i in range(1, 4):
+            ship(i).wait_send()
+
+    ends.append(finish)
+    return start, go, end
+
+
+def cross_scratch(rows, cols):
+    return [buffer(LOW, 2, rows, cols)] + [buffer(LOW, rows, cols)] * 2 + [DMA((2,))] * 2 + [DMA((1,))] * 2
+
+
+def cross_sum(here, part, total, scratch, ends):
+    landed, ready, final, c_send, c_recv, x_send, x_recv = scratch
+    g, x, c = here.g, here.x, here.c
+    first = [
+        remote(part.at[xx * 2 + 1 - c], landed.at[xx], c_send.at[xx], c_recv.at[xx], here.sibling)
+        for xx in range(2)
+    ]
+    second = remote(ready, final, x_send.at[0], x_recv.at[0], here.beside)
+    for copy in first:
+        copy.start()
+    yield
+    for copy in first:
+        copy.wait_recv()
+    ready[...] = (part[(1 - x) * 2 + c].astype(F32) + landed[1 - x].astype(F32)).astype(LOW)
+    second.start()
+    yield
+    second.wait_recv()
+    value = part[g].astype(F32) + landed[x].astype(F32) + final[...].astype(F32)
+    total[...] = value.astype(total.dtype).reshape(total.shape)
+
+    def finish():
+        for copy in first + [second]:
+            copy.wait_send()
+
+    ends.append(finish)
+    yield
+
+
+def pair_scratch(rows, cols):
+    return [buffer(LOW, 2, rows, cols)] + [buffer(LOW, rows, cols)] * 2 + [DMA((1,))] * 4
+
+
+def pair_sum(here, outgoing, mine, total, scratch, ends):
+    landed, ready, final, x_send, x_recv, z_send, z_recv = scratch
+    half = here.half
+    first = remote(outgoing, landed, x_send.at[0], x_recv.at[0], here.beside)
+    second = remote(ready, final, z_send.at[0], z_recv.at[0], here.far)
+    first.start()
+    yield
+    first.wait_recv()
+    ready[...] = (mine(1 - half)[...].astype(F32) + landed[1 - half].astype(F32)).astype(LOW)
+    second.start()
+    yield
+    second.wait_recv()
+    value = mine(half)[...].astype(F32) + landed[half].astype(F32) + final[...].astype(F32)
+    total[...] = value.astype(LOW).reshape(total.shape)
+
+    def finish():
+        first.wait_send()
+        second.wait_send()
+
+    ends.append(finish)
+    yield
+
+
+def trade_sems():
+    return [DMA((SHARDS,))] * 2
+
+
+def plane_trade(here, mine, theirs, sems, ends):
+    send, recv = sems
+
+    def copy(k):
+        device = here.at_shard(k)
+        return remote(mine.at[device[1]], theirs.at[here.s], send.at[k], recv.at[k], device)
+
+    for k in range(1, SHARDS):
+        copy(k).start()
+    theirs[here.s] = mine[here.s]
+    yield
+    for k in range(1, SHARDS):
+        copy(k).wait_recv()
+
+    def finish():
+        for k in range(1, SHARDS):
+            copy(k).wait_send()
+
+    ends.append(finish)
+    yield
+
+
+def centre(values):
+    mean = jnp.mean(values, -1, keepdims=True)
+    centred = values - mean
+    variance = jnp.mean(centred * centred, -1, keepdims=True)
+    inverse = lax.rsqrt(variance + eps_norm)
+    return centred * inverse, inverse
+
+
+def centre_back(e, normed, inverse, gain):
+    scaled = e * gain
+    mean_one = jnp.mean(scaled, -1, keepdims=True)
+    mean_two = jnp.mean(scaled * normed, -1, keepdims=True)
+    return inverse * (scaled - mean_one - normed * mean_two)
+
+
+def wide(norm, row):
+    return jnp.concatenate([norm[j, row : row + 1, :] for j in range(SHARDS)], 1)
+
+
+def column(row):
+    return jnp.broadcast_to(row, (LANES, LANES)).T
+
+
+def scratch_plan():
+    plan = dict(
+        own_norm=buffer(F32, 8, LANES),
+        norm=buffer(F32, SHARDS, 8, LANES),
+        norm_sems=trade_sems(),
+        wq=buffer(LOW, SHARDS, 2, 64, 3 * LANES),
+        wq_sems=trade_sems() + [DMA((1,))] * 2,
+        wo=buffer(LOW, SHARDS, GROUPS, 32, WIDTH),
+        wo_sems=gather_sems(),
+        wo_more=[DMA((3,))] * 2,
+        wu=buffer(LOW, SHARDS, 2, 64, HIDDEN),
+        wu_sems=trade_sems() + [DMA((1,))] * 2,
+        wd=buffer(LOW, 2, 2, ROWS, WIDTH),
+        wd_sems=[DMA((2,))] * 2,
+        a1=buffer(LOW, SHARDS, ROWS, WIDTH),
+        a1_sems=gather_sems(),
+        a2=buffer(LOW, 2, 4, ROWS, WIDTH),
+        a2_sems=square_sems(),
+        dz=buffer(LOW, 2, 4, ROWS, WIDTH),
+        dz_sems=square_sems(),
+        qkv=buffer(LOW, SHARDS, ROWS, 3 * LANES),
+        probs=buffer(LOW, 2, SHARDS, ROWS, WIDTH),
+        o_mine=buffer(LOW, SHARDS, ROWS, LANES),
+        o_all=buffer(LOW, SHARDS, ROWS, LANES),
+        o_sems=trade_sems(),
+        n1=buffer(F32, ROWS, WIDTH),
+        r1=buffer(F32, ROWS, LANES),
+        h1=buffer(F32, ROWS, WIDTH),
+        n2=buffer(F32, ROWS, WIDTH),
+        r2=buffer(F32, ROWS, LANES),
+        act=buffer(LOW, 2, 4, ROWS, HIDDEN),
+        du=buffer(LOW, 2, 4, ROWS, HIDDEN),
+        da2=buffer(LOW, 2, 4, ROWS, WIDTH),
+        da2_sum=square_scratch(),
+        e2=buffer(F32, ROWS, WIDTH),
+        ffn=buffer(LOW, 2, 4, ROWS, WIDTH),
+        ffn_sum=square_scratch(),
+        block=buffer(F32, ROWS, WIDTH),
+        dh1=buffer(F32, ROWS, WIDTH),
+        do_mine=buffer(LOW, SHARDS, ROWS, LANES),
+        do_all=buffer(LOW, SHARDS, ROWS, LANES),
+        do_sems=trade_sems(),
+        gk=buffer(F32, LANES, WIDTH),
+        gv=buffer(F32, LANES, WIDTH),
+        dqkv=buffer(LOW, SHARDS, ROWS, 3 * LANES),
+        da1=buffer(LOW, SHARDS, ROWS, WIDTH),
+        da1_sum=sum_scratch(ROWS),
+        e1=buffer(F32, ROWS, WIDTH),
+        gd=buffer(LOW, 2, 2, ROWS, WIDTH),
+        gd_sum=pair_scratch(ROWS, WIDTH),
+        gd_total=buffer(LOW, ROWS, WIDTH),
+        gd_land=buffer(LOW, ROWS, WIDTH),
+        gd_sems=[DMA((1,))] * 2,
+        gu=buffer(LOW, 2, 2, 256, HIDDEN),
+        gu_sum=pair_scratch(256, HIDDEN),
+        gu_total=buffer(LOW, SHARDS, 32, HIDDEN),
+        gu_land=buffer(LOW, 2, 4, 32, HIDDEN),
+        gu_sems=[DMA((SHARDS,)), DMA((2, 4))],
+        go=buffer(LOW, GROUPS, 256, WIDTH),
+        go_sum=cross_scratch(256, WIDTH),
+        go_total=buffer(LOW, SHARDS, 32, WIDTH),
+        go_plane=sum_scratch(32),
+        gq=buffer(LOW, GROUPS, 256, 3 * LANES),
+        gq_sum=cross_scratch(256, 3 * LANES),
+        gq_total=buffer(LOW, SHARDS, 32, 3 * LANES),
+        gq_land=buffer(LOW, SHARDS, 32, 3 * LANES),
+        gq_sems=trade_sems(),
+        np_mine=buffer(F32, GROUPS, 8, 2 * LANES),
+        np_land=buffer(F32, GROUPS, 8, 2 * LANES),
+        np_all=buffer(F32, SHARDS, 8, 2 * LANES),
+        np_sems=[DMA((GROUPS,))] * 2 + trade_sems(),
+    )
+    return plan
+
+
+def step_kernel(*refs):
+    plan = scratch_plan()
+    inputs, refs = refs[:9], refs[9:]
+    outputs, refs = refs[:7], list(refs[7:])
+    tok, cot, item_rows, live_rows, norm_weight, wqkv, wout, wup, wdown = inputs
+    block_out, input_grad, qkv_sum, up_sum, out_sum, down_sum, norm_sum = outputs
+    b = {}
+    for name, kind in plan.items():
+        many = isinstance(kind, list)
+        got = [refs.pop(0) for _ in range(len(kind) if many else 1)]
+        b[name] = got if many else got[0]
+
+    here = Place()
+    g, s, x, c, z, y, half, corner = (
+        here.g, here.s, here.x, here.c, here.z, here.y, here.half, here.corner
+    )
+    ends = []
+    greet_all(here)
+
+    norm, own_norm, wq = b["norm"], b["own_norm"], b["wq"]
+    own_norm[...] = jnp.zeros_like(own_norm)
+    own_norm[0:4, :] = norm_weight[...].astype(F32)
+    norm[s] = own_norm[...]
+
+    def norm_copy(k):
+        send, recv = b["norm_sems"]
+        return remote(own_norm, norm.at[s], send.at[k], recv.at[k], here.at_shard(k))
+
+    def wq_copies(k):
+        device = here.at_shard(k)
+        send, recv = b["wq_sems"][:2]
+        half_rows = pl.ds(pl.multiple_of(c * 64, 64), 64)
+        return [
+            remote(
+                wqkv.at[half_rows, pl.ds(pl.multiple_of(j * WIDTH + device[1] * LANES, LANES), LANES)],
+                wq.at[s, c, :, pl.ds(j * LANES, LANES)],
+                send.at[k],
+                recv.at[k],
+                device,
+            )
+            for j in range(3)
+        ]
+
+    def wq_whole(k):
+        send, recv = b["wq_sems"][:2]
+        block = wq.at[here.from_shard(k), c]
+        return remote(block, block, send.at[k], recv.at[k], here.at_shard(k))
+
+    for k in range(1, SHARDS):
+        norm_copy(k).start()
+    for k in range(1, SHARDS):
+        for copy in wq_copies(k):
+            copy.start()
+    n1, inverse = centre(tok[...].astype(F32))
+    b["n1"][...] = n1
+    b["r1"][...] = jnp.broadcast_to(inverse, (ROWS, LANES))
+    for k in range(1, SHARDS):
+        norm_copy(k).wait_recv()
+    a1 = b["a1"]
+    a1[s] = (n1 * wide(norm, 0) + wide(norm, 1)).astype(LOW)
+    a1_step = plane_gather(here, lambda i: a1.at[i], b["a1_sems"], ends)
+    next(a1_step)
+
+    wd = b["wd"]
+    wd_send, wd_recv = b["wd_sems"]
+    wd_rows = pl.ds(pl.multiple_of(c * 256 + x * ROWS, ROWS), ROWS)
+    wd_far = remote(wdown.at[wd_rows, :], wd.at[half, x], wd_send.at[0], wd_recv.at[0], here.far)
+    wd_far.start()
+    for j in range(2):
+        wd[half, j] = wdown[pl.ds(pl.multiple_of(c * 256 + j * ROWS, ROWS), ROWS), :]
+    wd_beside = remote(
+        wd.at[1 - half, x], wd.at[1 - half, x], wd_send.at[1], wd_recv.at[1], here.beside
+    )
+    for j in range(3):
+        wq[s, c, :, j * LANES : (j + 1) * LANES] = wqkv[
+            pl.ds(pl.multiple_of(c * 64, 64), 64),
+            pl.ds(pl.multiple_of(j * WIDTH + s * LANES, LANES), LANES),
+        ]
+    dz = b["dz"]
+    own_live = column(live_rows[pl.ds(s, 1), :].astype(F32))
+    dz[c, corner] = (cot[...].astype(F32) * jnp.concatenate([own_live] * SHARDS, 1)).astype(LOW)
+    for k in range(1, SHARDS):
+        wq_whole(k).wait_recv()
+    wq_core = remote(
+        wq.at[:, c], wq.at[:, c], b["wq_sems"][2].at[0], b["wq_sems"][3].at[0], here.sibling
+    )
+    wq_core.start()
+    run(a1_step)
+
+    wo = b["wo"]
+    wo[s, g] = wout[pl.ds(pl.multiple_of(g * 32, 32), 32), :]
+    wo_step = plane_gather(here, lambda i: wo.at[i, g], b["wo_sems"], ends)
+    next(wo_step)
+    wo_send, wo_recv = b["wo_more"]
+    beside_g = here.beside[0]
+    wo_beside = remote(wo.at[:, g], wo.at[:, g], wo_send.at[0], wo_recv.at[0], here.beside)
+    wo_core = [
+        remote(wo.at[:, k], wo.at[:, k], wo_send.at[1 + i], wo_recv.at[1 + i], here.sibling)
+        for i, k in enumerate((g, beside_g))
+    ]
+
+    wu = b["wu"]
+    wu_send, wu_recv, wu_xsend, wu_xrecv = b["wu_sems"]
+    wu_rows = pl.ds(pl.multiple_of(x * 64, 64), 64)
+
+    def wu_columns(shard, j):
+        return pl.ds(pl.multiple_of((shard % 4 + j * 4) * HIDDEN + c * 256, 256), 256)
+
+    def wu_copies(k):
+        device = here.at_shard(k)
+        return [
+            remote(
+                wup.at[wu_rows, wu_columns(device[1], j)],
+                wu.at[s, x, :, pl.ds(j * 256, 256)],
+                wu_send.at[k],
+                wu_recv.at[k],
+                device,
+            )
+            for j in range(2)
+        ]
+
+    def wu_whole(k):
+        block = wu.at[here.from_shard(k), x]
+        return remote(block, block, wu_send.at[k], wu_recv.at[k], here.at_shard(k))
+
+    for k in range(1, SHARDS):
+        for copy in wu_copies(k):
+            copy.start()
+    for j in range(2):
+        wu[s, x, :, j * 256 : (j + 1) * 256] = wup[wu_rows, wu_columns(s, j)]
+    wu_beside = remote(wu.at[:, x], wu.at[:, x], wu_xsend.at[0], wu_xrecv.at[0], here.beside)
+
+    wq_core.wait_recv()
+    qkv, probs = b["qkv"], b["probs"]
+    qkv[...] = dot(flat(a1[...]), flat(wq[...])).astype(LOW).reshape(qkv.shape)
+    keys = flat(qkv[:, :, LANES : 2 * LANES])
+    values = flat(qkv[:, :, 2 * LANES :])
+    key_items = jnp.concatenate(
+        [jnp.where(live_rows[j : j + 1, :] > 0, item_rows[j : j + 1, :], -1) for j in range(SHARDS)], 1
+    )
+    lane = lax.broadcasted_iota(jnp.int32, (2 * ROWS, LANES), 1)
+    mine = [lane < HEAD_DIM, lane >= HEAD_DIM]
+    o_mine, o_all = b["o_mine"], b["o_all"]
+
+    def o_copy(to, k):
+        send, recv = b["o_sems"]
+        return remote(o_mine.at[to], o_all.at[s], send.at[k], recv.at[k], (g, to))
+
+    def attend(zz):
+        pair = pl.ds(zz * 2, 2)
+        queries = flat(qkv[pair, :, :LANES])
+        items = jnp.concatenate([column(item_rows[pl.ds(zz * 2 + j, 1), :]) for j in range(2)], 0)
+        allowed = jnp.concatenate([items] * SHARDS, 1) == key_items
+        outs = []
+        for h in range(2):
+            scores = dot_nt(jnp.where(mine[h], queries, jnp.zeros_like(queries)), keys) * score_scale
+            scores = jnp.where(allowed, scores, -1e30)
+            peak = jnp.max(scores, -1, keepdims=True)
+            expo = jnp.exp(scores - peak)
+            chance = (expo * (1.0 / jnp.sum(expo, -1, keepdims=True))).astype(LOW)
+            probs[h, pair] = chance.reshape(2, ROWS, WIDTH)
+            outs.append(dot(chance, values))
+        o_mine[pair] = jnp.where(mine[0], outs[0], outs[1]).astype(LOW).reshape(2, ROWS, LANES)
+
+    for step in range(1, 4):
+        zz = (z + step) % 4
+        attend(zz)
+        for j in range(2):
+            to = zz * 2 + j
+            o_copy(to, (to + SHARDS - s) % SHARDS).start()
+        next(wo_step)
+    attend(z)
+    o_all[s] = o_mine[s]
+    o_copy(here.across[1], (here.across[1] + SHARDS - s) % SHARDS).start()
+    dz_step = square_gather(here, dz, b["dz_sems"], ends)
+    next(dz_step)
+    run(wo_step)
+    wo_beside.start()
+    wo_core[0].start()
+    wd_far.wait_recv()
+    wd_beside.start()
+    for k in range(1, SHARDS):
+        wu_whole(k).wait_recv()
+    wu_beside.start()
+    wo_beside.wait_recv()
+    wo_core[1].start()
+    for k in range(1, SHARDS):
+        o_copy(here.from_shard(k), k).wait_recv()
+    for copy in wo_core:
+        copy.wait_recv()
+
+    attended = jnp.concatenate([o_all[j] for j in range(SHARDS)], 1)
+    h1 = tok[...].astype(F32) + dot(attended, wo[...].reshape(WIDTH, WIDTH))
+    b["h1"][...] = h1
+    n2, inverse = centre(h1)
+    b["n2"][...] = n2
+    b["r2"][...] = jnp.broadcast_to(inverse, (ROWS, LANES))
+    a2 = b["a2"]
+    a2[c, corner] = (n2 * wide(norm, 2) + wide(norm, 3)).astype(LOW)
+    a2_step = square_gather(here, a2, b["a2_sems"], ends)
+    next(a2_step)
+    wu_beside.wait_recv()
+    wd_beside.wait_recv()
+
+    act, du, da2 = b["act"], b["du"], b["da2"]
+    up = wu[...].reshape(WIDTH, HIDDEN)
+    down = wd[...].reshape(HIDDEN, WIDTH)
+    start, go, end = square_sum(here, da2, b["e2"], b["da2_sum"], ends)
+    shape = (2, ROWS, HIDDEN)
+
+    def feed(i):
+        at = here.corners[i]
+        u = dot(flat(a2[:, at]), up)
+        half_erf = 0.5 + 0.5 * lax.erf(u * (0.5**0.5))
+        act[:, at] = (u * half_erf).astype(LOW).reshape(shape)
+        slope = half_erf + u * jnp.exp(-0.5 * u * u) * (1.0 / math.sqrt(2.0 * math.pi))
+        grad = (dot_nt(flat(dz[:, at]), down) * slope).astype(LOW)
+        du[:, at] = grad.reshape(shape)
+        da2[:, at] = dot_nt(grad, up).astype(LOW).reshape(2, ROWS, WIDTH)
+
+    for i in range(4):
+        next(dz_step)
+        next(a2_step)
+        feed(i)
+        start(i)
+        if i > 1:
+            go(i - 1)
+    go(3)
+    gd = b["gd"]
+    gd[...] = dot_tn(flat(act[...]), flat(dz[...])).astype(LOW).reshape(gd.shape)
+    gd_step = pair_sum(here, gd.at[:, 1 - x], lambda i: gd.at[i, x], b["gd_total"], b["gd_sum"], ends)
+    next(gd_step)
+    go(0)
+    end()
+
+    e2, n2 = b["e2"][...], b["n2"][...]
+    dh1 = centre_back(e2, n2, b["r2"][:, :1], wide(norm, 2)) + dz[c, corner].astype(F32)
+    b["dh1"][...] = dh1
+    low = dh1.astype(LOW)
+    do_mine, do_all = b["do_mine"], b["do_all"]
+    for k in range(SHARDS):
+        do_mine[k] = dot_nt(low, wo[k].reshape(ROWS, WIDTH)).astype(LOW)
+    do_step = plane_trade(here, do_mine, do_all, b["do_sems"], ends)
+    next(do_step)
+    gu = b["gu"]
+    gu[...] = dot_tn(flat(a2[...]), flat(du[...])).astype(LOW).reshape(gu.shape)
+    gu_step = pair_sum(here, gu.at[1 - x], lambda i: gu.at[x, i], b["gu_total"], b["gu_sum"], ends)
+    next(gu_step)
+    go_part = b["go"]
+    go_part[...] = dot_tn(attended, low).astype(LOW).reshape(go_part.shape)
+    go_step = cross_sum(here, go_part, b["go_total"], b["go_sum"], ends)
+    next(go_step)
+    run(do_step)
+
+    ffn = b["ffn"]
+    f_start, f_go, f_end = square_sum(here, ffn, b["block"], b["ffn_sum"], ends)
+    ffn[...] = dot(flat(act[...]), down).astype(LOW).reshape(ffn.shape)
+    for i in range(4):
+        f_start(i)
+    gk, gv, dqkv = b["gk"], b["gv"], b["dqkv"]
+
+    def back(zz, first):
+        pair = pl.ds(zz * 2, 2)
+        queries, outs = flat(qkv[pair, :, :LANES]), flat(do_all[pair])
+        queries_t, outs_t = queries.T, outs.T
+        grad_query, grad_key, grad_value = [], [], []
+        for h in range(2):
+            chance_low = flat(probs[h, pair])
+            chance = chance_low.astype(F32)
+            grad_chance = dot_nt(jnp.where(mine[h], outs, jnp.zeros_like(outs)), values)
+            inner = jnp.sum(chance * grad_chance, -1, keepdims=True)
+            grad_scores = (chance * (grad_chance - inner)).astype(LOW)
+            lanes = slice(h * HEAD_DIM, (h + 1) * HEAD_DIM)
+            grad_query.append(dot(grad_scores, keys))
+            grad_key.append(dot(queries_t[lanes], grad_scores))
+            grad_value.append(dot(outs_t[lanes], chance_low))
+        grad_query = jnp.where(mine[0], grad_query[0], grad_query[1]) * score_scale
+        dqkv[pair, :, :LANES] = grad_query.astype(LOW).reshape(2, ROWS, LANES)
+        grad_key, grad_value = jnp.concatenate(grad_key, 0), jnp.concatenate(grad_value, 0)
+        if first:
+            gk[...], gv[...] = grad_key, grad_value
+        else:
+            gk[...] += grad_key
+            gv[...] += grad_value
+
+    back(0, True)
+    for i in range(1, 4):
+        f_go(i)
+    f_go(0)
+    next(go_step)
+    back(1, False)
+    next(gd_step)
+    back(2, False)
+    back(3, False)
+    next(gu_step)
+    thirds = (SHARDS, ROWS, LANES)
+    dqkv[:, :, LANES : 2 * LANES] = (gk[...].T * score_scale).astype(LOW).reshape(thirds)
+    dqkv[:, :, 2 * LANES :] = gv[...].T.astype(LOW).reshape(thirds)
+
+    da1, weight = b["da1"], flat(wq[...])
+
+    def spread(zz):
+        pair = pl.ds(zz * 2, 2)
+        da1[pair] = dot_nt(flat(dqkv[pair]), weight).astype(LOW).reshape(2, ROWS, WIDTH)
+
+    da1_step = plane_sum(here, da1, b["e1"], b["da1_sum"], ends, spread)
+    next(da1_step)
+    gq = b["gq"]
+    gq[...] = dot_tn(flat(a1[...]), flat(dqkv[...])).astype(LOW).reshape(gq.shape)
+    gq_step = cross_sum(here, gq, b["gq_total"], b["gq_sum"], ends)
+    next(gq_step)
+    run(go_step)
+    go_out = plane_sum(here, b["go_total"], out_sum, b["go_plane"], ends)
+    next(go_out)
+    next(da1_step)
+    run(gd_step)
+    owner = here.y * 4 + c * 2 + x
+    stays = (z == g) & (owner == s)
+    gd_away = remote(
+        b["gd_total"], b["gd_land"], b["gd_sems"][0].at[0], b["gd_sems"][1].at[0], (z, owner)
+    )
+
+    @pl.when(jnp.logical_not(stays))
+    def _():
+        gd_away.start()
+
+    next(da1_step)
+    next(gq_step)
+    next(go_out)
+    run(gu_step)
+    gu_total, gu_land = b["gu_total"], b["gu_land"]
+    gu_send, gu_recv = b["gu_sems"]
+
+    def gu_copy(k):
+        to = (s + k) % SHARDS
+        return remote(
+            gu_total.at[to], gu_land.at[c, corner], gu_send.at[k], gu_recv.at[c, corner], (x * 2 + half, to)
+        )
+
+    def gu_came(cc, at):
+        return remote(
+            gu_total.at[0], gu_land.at[cc, at], gu_send.at[0], gu_recv.at[cc, at], here.sibling
+        )
+
+    @pl.when(c == half)
+    def _():
+        gu_land[c, corner] = gu_total[s]
+
+    @pl.when(c != half)
+    def _():
+        gu_copy(0).start()
+
+    for k in range(1, SHARDS):
+        gu_copy(k).start()
+    next(da1_step)
+    next(go_out)
+    run(gq_step)
+    gq_out = plane_trade(here, b["gq_total"], b["gq_land"], b["gq_sems"], ends)
+    next(gq_out)
+    run(da1_step)
+
+    e1, n1 = b["e1"][...], b["n1"][...]
+    count = jnp.sum(live_rows[pl.ds(s, 1), :].astype(F32), 1, keepdims=True)
+    part = jnp.concatenate(
+        [
+            jnp.sum(e1 * n1, 0, keepdims=True),
+            jnp.sum(e1, 0, keepdims=True),
+            jnp.sum(e2 * n2, 0, keepdims=True),
+            jnp.sum(e2, 0, keepdims=True),
+            jnp.broadcast_to(count, (4, WIDTH)),
+        ],
+        0,
+    )
+    np_mine, np_land, np_all = b["np_mine"], b["np_land"], b["np_all"]
+    n_send, n_recv, m_send, m_recv = b["np_sems"]
+    for k in range(GROUPS):
+        np_mine[k] = part[:, k * 2 * LANES : (k + 1) * 2 * LANES]
+
+    def grp_copy(k):
+        to = (g + k) % GROUPS
+        return remote(np_mine.at[to], np_land.at[k], n_send.at[k], n_recv.at[k], (to, s))
+
+    for k in range(1, GROUPS):
+        grp_copy(k).start()
+    input_grad[...] = centre_back(e1, n1, b["r1"][:, :1], wide(norm, 0)) + b["dh1"][...]
+    for k in range(1, GROUPS):
+        grp_copy(k).wait_recv()
+    np_all[s] = np_mine[g] + np_land[1] + np_land[2] + np_land[3]
+
+    def all_copy(k):
+        return remote(np_all.at[s], np_all.at[s], m_send.at[k], m_recv.at[k], here.at_shard(k))
+
+    for k in range(1, SHARDS):
+        all_copy(k).start()
+
+    f_end()
+    block_out[...] = b["h1"][...] + b["block"][...]
+    run(go_out)
+    for cc in range(2):
+        for at in range(4):
+
+            @pl.when(jnp.logical_not((cc == c) & (at == corner) & (c == half)))
+            def _():
+                gu_came(cc, at).wait_recv()
+
+            for j in range(2):
+                first = (j * 4 + at) * HIDDEN + cc * 256
+                up_sum[:, first : first + 256] = gu_land[cc, at, :, j * 256 : (j + 1) * 256].astype(F32)
+    run(gq_out)
+    for j in range(SHARDS):
+        for i in range(3):
+            qkv_sum[:, i * WIDTH + j * LANES : i * WIDTH + (j + 1) * LANES] = b["gq_land"][
+                j, :, i * LANES : (i + 1) * LANES
+            ].astype(F32)
+
+    @pl.when(stays)
+    def _():
+        down_sum[...] = b["gd_total"][...].astype(F32)
+
+    @pl.when(jnp.logical_not(stays))
+    def _():
+        gd_away.wait_recv()
+        down_sum[...] = b["gd_land"][...].astype(F32)
+        gd_away.wait_send()
+
+    for k in range(1, SHARDS):
+        all_copy(k).wait_recv()
+    total = np_all[0]
+    for j in range(1, SHARDS):
+        total += np_all[j]
+    norm_sum[...] = pltpu.roll(total, 2 * LANES - s * 32, 1)[:, :LANES]
+
+    for k in range(1, GROUPS):
+        grp_copy(k).wait_send()
+    for k in range(1, SHARDS):
+        all_copy(k).wait_send()
+        norm_copy(k).wait_send()
+        wq_whole(k).wait_send()
+        wu_whole(k).wait_send()
+        o_copy(here.at_shard(k)[1], k).wait_send()
+        gu_copy(k).wait_send()
+
+    @pl.when(c != half)
+    def _():
+        gu_copy(0).wait_send()
+
+    for copy in (wq_core, wd_far, wd_beside, wo_beside, wu_beside, *wo_core):
+        copy.wait_send()
+    for finish in ends:
+        finish()
+
+
+def shaped(kind, *shape):
+    return jax.ShapeDtypeStruct(shape, kind)
+
+
+def fast_body(
+    tokens, cotangent, item_ids, live_mask, qkv_weight, out_weight, up_weight, down_weight, norm_weight,
+    qkv_master, qkv_first, qkv_second, out_master, out_first, out_second, up_master, up_first, up_second,
+    down_master, down_first, down_second, norm_master, norm_first, norm_second,
+):
+    rows = item_ids.shape[0]
+    args = (
+        tokens,
+        cotangent,
+        item_ids.reshape(SHARDS, ROWS),
+        live_mask.reshape(SHARDS, ROWS),
+        norm_weight,
+        qkv_weight,
+        out_weight,
+        up_weight,
+        down_weight,
+    )
+    scratch = []
+    for kind in scratch_plan().values():
+        scratch += kind if isinstance(kind, list) else [kind]
+    block_out, input_grad, qkv_sum, up_sum, out_sum, down_sum, norm_sum = pl.pallas_call(
+        step_kernel,
+        out_shape=[
+            shaped(F32, ROWS, WIDTH),
+            shaped(F32, ROWS, WIDTH),
+            shaped(F32, 32, 3 * WIDTH),
+            shaped(F32, 32, 4 * WIDTH),
+            shaped(F32, 32, WIDTH),
+            shaped(F32, ROWS, WIDTH),
+            shaped(F32, 8, LANES),
+        ],
+        in_specs=[VMEM] * len(args),
+        out_specs=[VMEM] * 7,
+        scratch_shapes=scratch,
+        compiler_params=pltpu.CompilerParams(
+            collective_id=0, has_side_effects=True, vmem_limit_bytes=62 * 2**20
+        ),
+    )(*args)
+    norm_own = norm_sum[:, :32]
+    total_count = norm_own[4, 0]
+    model_width, hidden = tokens.shape[1], up_weight.shape[1]
+    return (
+        block_out,
+        input_grad,
+        *adamw(qkv_sum, total_count, qkv_master, qkv_first, qkv_second, model_width ** (-0.5), 0.1),
+        *adamw(out_sum, total_count, out_master, out_first, out_second, math.sqrt(rows) / 64, 0.1),
+        *adamw(up_sum, total_count, up_master, up_first, up_second, model_width ** (-0.5), 0.1),
+        *adamw(down_sum, total_count, down_master, down_first, down_second, hidden ** (-0.5), 0.1),
+        *adamw(norm_own[:4], total_count, norm_master, norm_first, norm_second, 0.4, 0.0),
+    )
+
+
+def suits(mesh):
+    return mesh.shape["grp"] == GROUPS and mesh.shape["shard"] == SHARDS
+
+
 def solution(mesh):
     placed = (
         P(("grp", "shard"), None),
@@ -363,7 +1381,7 @@
         P(None, ("grp", "shard")),
     )
     return jax.shard_map(
-        body,
+        fast_body if suits(mesh) else body,
         mesh=mesh,
         in_specs=placed,
         out_specs=(

time: 1800 us -> 230 us (0.13)
  waiting for transfers between devices: 1570 us -> 0 us
  Pallas kernels: 0 us -> 214 us
  matrix products: 103 us -> 0 us
  local copies, waits for them, and re-layouts: 41.2 us -> 3.99 us
  blocking collectives: 30.5 us -> 0 us
  other arithmetic: 29.1 us -> 10.5 us
    reduce_scatter x5 -> x0, waiting for transfers between devices: 1040 us -> none  [the longest x1 357 us: body(): lax.psum_scatter(down_term, ('grp', 'shard'), scatter_dimension=0, tiled=...]
    all_gather x5 -> x0, waiting for transfers between devices: 397 us -> none  [the longest x1 123 us: body(): lax.all_gather(up_weight, 'shard', axis=0, tiled=True)]
    pallas_call x0 -> x1, Pallas kernels: none -> 214 us  [fast_body(): pl.pallas_call(step_kernel, out_shape=[shaped(F32, ROWS, WIDTH), shaped(F...]
    unnamed x12 -> x0, waiting for transfers between devices: 133 us -> none
    dot_general x26 -> x0, matrix products: 103 us -> none  [the longest x4 28.2 us: outer_sum(): lax.dot_general(left, right, (((0,), (0,)), ((), ())), preferred_element_...]
    all_gather x1 -> x0, blocking collectives: 22.7 us -> none  [body(): lax.all_gather(norm_weight, 'shard', axis=1, tiled=True)]
  transfers between devices with their start and end apart: 11 -> 0, of which waited for: 11 -> 0; matrix products, arithmetic and copies ran while one was open for 6% -> 0% of each run, Pallas kernels for 0% -> 0%
where the time goes in v2:
time: 230 us
  Pallas kernels  214 us (93%)
  other arithmetic  10.5 us (5%)
  local copies, waits for them, and re-layouts  3.99 us (2%)
    pallas_call x1, Pallas kernels, fast_body(): pl.pallas_call(step_kernel, out_shape=[shaped(F32, ROWS, WIDTH), shaped(F...  214 us
    convert_element_type x5, other arithmetic, adamw(): return (gradient, moment, square, updated, updated.astype(jnp.bfloat16))  10.5 us

profile of v2, /device:TPU:0, one launch (start us, length us, event | category | flops | bytes accessed | tf_op | source)
XLA Modules:
  0.0 229.6 jit_solution(10600293008256834825)
XLA Ops:
  0.7 0.0 copy-start.10
  0.7 0.0 copy-start.11
  0.7 0.0 copy-start.12
  0.7 214.3 %shard_map.439 = (f32[128,1024]{1,0:T(8,128)}, f32[128,1024]{1,0:T(8,128)}, f32[32,3072]{1,0:T(8,128)}, f32[32,4096]{1,0:T(8,128)}, f32[32,1024]{1,0:T(8,128)}, /*index=5*/f32[128,1024]{1,0:T(8,128)}, f32[8,128]{1,0:T(8,128)}) custom-call(bf16[128,1024]{1,0:T(8,128)(2,1)} %refs_0_.1, bf16[128,1024]{1,0:T(8,128)(2,1)} %refs_1_.1, s32[8,128]{1,0:T(8,128)} %bitcast.3, ...), custom_call_target="tpu_custom_call" | custom-call | tf_op jit(solution)/shard_map/pallas_call | solution.py:1320
  215.0 0.0 copy-start.20
  215.0 0.7 copy-done.20
  215.7 0.5 slice.9
  216.2 0.0 copy-done.10
  216.2 0.0 copy-done.11
  216.2 0.0 copy-done.12
  216.2 0.0 copy-start.13
  216.2 0.0 copy-start.14
  216.2 0.0 copy-start.15
  216.3 0.0 copy-start.16
  216.3 0.0 copy-start.2
  216.3 0.0 copy-start.7
  216.3 3.0 %fusion.13 = (bf16[32,3072]{1,0:T(8,128)(2,1)}, f32[32,3072]{1,0:T(8,128)}, f32[32,3072]{1,0:T(8,128)}, f32[32,3072]{1,0:T(8,128)}, f32[32,3072]{1,0:T(8,128)}) fusion(f32[32,3072]{1,0:T(8,128)S(1)} %copy-done.10, f32[32,3072]{1,0:T(8,128)S(1)} %copy-done.11, f32[32,3072]{1,0:T(8,128)S(1)} %copy-done.12, f32[32,3072]{1,0:T(8,128)} %get-tuple-element.36, ...), kind=kLoop, calls=%fused_computation.29 | loop fusion | flops 1572864 | bytes 3342340 | tf_op jit(solution)/shard_map/convert_element_type | solution.py:173
  219.3 0.0 copy-done.13
  219.3 0.0 copy-done.14
  219.3 0.0 copy-done.15
  219.4 0.0 copy-done.16
  219.4 0.0 copy-start
  219.4 0.0 copy-start.1
  219.4 1.6 fusion.11
  221.0 0.0 copy-done.2
  221.0 0.0 copy-done.7
  221.0 0.0 copy-done
  221.0 0.0 copy-done.1
  221.0 0.0 copy-start.3
  221.0 0.0 copy-start.4
  221.0 0.0 copy-start.5
  221.0 0.0 copy-start.6
  221.0 2.3 %fusion.9 = (bf16[32,4096]{1,0:T(8,128)(2,1)}, f32[32,4096]{1,0:T(8,128)}, f32[32,4096]{1,0:T(8,128)}, f32[32,4096]{1,0:T(8,128)}, f32[32,4096]{1,0:T(8,128)}) fusion(f32[32,4096]{1,0:T(8,128)S(1)} %copy-done, f32[32,4096]{1,0:T(8,128)S(1)} %copy-done.1, f32[32,4096]{1,0:T(8,128)S(1)} %copy-done.2, f32[32,4096]{1,0:T(8,128)S(1)} %copy-done.7, f32[]{:T(128)} %bitcast.2), kind=kLoop, calls=%fused_computation.27 | loop fusion | flops 2097152 | bytes 4456452 | tf_op jit(solution)/shard_map/convert_element_type | solution.py:173
  223.3 0.0 copy-done.3
  223.3 0.0 copy-done.4
  223.3 0.0 copy-done.5
  223.4 0.0 copy-done.6
  223.4 0.0 copy-start.19
  223.4 0.0 copy-start.9
  223.4 2.3 fusion.7
  225.7 0.0 copy-done.19
  225.7 0.7 copy-done.18
  226.3 0.0 copy-done.17
  226.4 1.3 fusion.5
  227.6 0.0 copy-done.9
  227.6 0.8 copy.53
  228.4 0.4 copy-done.8
  228.8 0.8 copy.54
  (3 shorter events, 0.0 us)
Async XLA Ops:
  0.7 215.5 %copy-start.10 = (f32[32,3072]{1,0:T(8,128)S(1)}, f32[32,3072]{1,0:T(8,128)}, u32[]{:S(2)}) copy-start(f32[32,3072]{1,0:T(8,128)} %param.33) | copy-start | bytes 1179652
  0.7 215.5 %copy-start.11 = (f32[32,3072]{1,0:T(8,128)S(1)}, f32[32,3072]{1,0:T(8,128)}, u32[]{:S(2)}) copy-start(f32[32,3072]{1,0:T(8,128)} %param.35) | copy-start | bytes 1179652
  0.7 215.5 %copy-start.12 = (f32[32,3072]{1,0:T(8,128)S(1)}, f32[32,3072]{1,0:T(8,128)}, u32[]{:S(2)}) copy-start(f32[32,3072]{1,0:T(8,128)} %param.34) | copy-start | bytes 1179652
  215.0 0.7 copy-start.20
  216.2 3.1 %copy-start.13 = (f32[32,1024]{1,0:T(8,128)S(1)}, f32[32,1024]{1,0:T(8,128)}, u32[]{:S(2)}) copy-start(f32[32,1024]{1,0:T(8,128)} %param.36) | copy-start | bytes 393220
  216.2 3.1 %copy-start.14 = (f32[32,1024]{1,0:T(8,128)S(1)}, f32[32,1024]{1,0:T(8,128)}, u32[]{:S(2)}) copy-start(f32[32,1024]{1,0:T(8,128)} %param.38) | copy-start | bytes 393220
  216.2 3.1 %copy-start.15 = (f32[32,1024]{1,0:T(8,128)S(1)}, f32[32,1024]{1,0:T(8,128)}, u32[]{:S(2)}) copy-start(f32[32,1024]{1,0:T(8,128)} %param.37) | copy-start | bytes 393220
  216.3 3.1 %copy-start.16 = (f32[32,1024]{1,0:T(8,128)S(1)}, f32[32,1024]{1,0:T(8,128)}, u32[]{:S(2)}) copy-start(f32[32,1024]{1,0:T(8,128)} %get-tuple-element.38) | copy-start | bytes 393220
  216.3 4.7 %copy-start.2 = (f32[32,4096]{1,0:T(8,128)S(1)}, f32[32,4096]{1,0:T(8,128)}, u32[]{:S(2)}) copy-start(f32[32,4096]{1,0:T(8,128)} %param.40) | copy-start | bytes 1572868
  216.3 4.7 %copy-start.7 = (f32[32,4096]{1,0:T(8,128)S(1)}, f32[32,4096]{1,0:T(8,128)}, u32[]{:S(2)}) copy-start(f32[32,4096]{1,0:T(8,128)} %get-tuple-element.39) | copy-start | bytes 1572868
  219.4 1.6 copy-start
  219.4 1.6 copy-start.1
  221.0 2.4 %copy-start.3 = (f32[128,1024]{1,0:T(8,128)S(1)}, f32[128,1024]{1,0:T(8,128)}, u32[]{:S(2)}) copy-start(f32[128,1024]{1,0:T(8,128)} %param.42) | copy-start | bytes 1572868
  221.0 2.4 %copy-start.4 = (f32[128,1024]{1,0:T(8,128)S(1)}, f32[128,1024]{1,0:T(8,128)}, u32[]{:S(2)}) copy-start(f32[128,1024]{1,0:T(8,128)} %param.44) | copy-start | bytes 1572868
  221.0 2.4 %copy-start.5 = (f32[128,1024]{1,0:T(8,128)S(1)}, f32[128,1024]{1,0:T(8,128)}, u32[]{:S(2)}) copy-start(f32[128,1024]{1,0:T(8,128)} %param.43) | copy-start | bytes 1572868
  221.0 2.3 %copy-start.6 = (f32[128,1024]{1,0:T(8,128)S(1)}, f32[128,1024]{1,0:T(8,128)}, u32[]{:S(2)}) copy-start(f32[128,1024]{1,0:T(8,128)} %get-tuple-element.40) | copy-start | bytes 1572868
  223.4 2.3 %copy-start.19 = (f32[4,32]{1,0:T(4,128)S(1)}, f32[4,32]{1,0:T(4,128)}, u32[]{:S(2)}) copy-start(f32[4,32]{1,0:T(4,128)} %param.46) | copy-start | bytes 1540
  223.4 4.2 %copy-start.9 = (f32[128,1024]{1,0:T(8,128)S(1)}, f32[128,1024]{1,0:T(8,128)}, u32[]{:S(2)}) copy-start(f32[128,1024]{1,0:T(8,128)} %get-tuple-element.93) | copy-start | bytes 1572868
  225.7 0.7 copy-start.18
  225.7 0.7 copy-start.17
  227.6 1.2 copy-start.8

commit v3 on v2

--- a/solution.py
+++ b/solution.py
@@ -1,3 +1,4 @@
+import functools
 import math
 
 import jax
@@ -340,7 +341,7 @@
 MESH = pl.DeviceIdType.MESH
 F32, LOW = jnp.float32, jnp.bfloat16
 VMEM = pl.BlockSpec(memory_space=pltpu.VMEM)
-ANY = pl.BlockSpec(memory_space=pl.ANY)
+ANY = pl.BlockSpec(memory_space=pltpu.HBM)
 SHARDS, GROUPS = 8, 4
 WIDTH, ROWS, LANES = 1024, 128, 128
 HIDDEN = 512
@@ -429,7 +430,7 @@
     return [DMA((3, 4)), DMA((SHARDS,))]
 
 
-def plane_gather(here, block, sems, ends):
+def plane_gather(here, block, sems, ends, came=None):
     send, recv = sems
     z, y = here.z, here.y
 
@@ -440,6 +441,8 @@
 
     def arrived(zz, yy):
         copy(0, zz, yy).wait_recv()
+        if came is not None:
+            came(zz * 2 + yy)
 
     def finish():
         for zz in range(4):
@@ -464,6 +467,8 @@
         copy(2, z, y).start()
 
     copy(0, z, y).start()
+    if came is not None:
+        came(z * 2 + y)
     yield
     for step in range(1, 4):
 
@@ -571,16 +576,17 @@
 
 
 def square_gather(here, held, sems, ends):
-    send, recv, sib_send, sib_recv = sems
+    send, recv, half_send, half_recv, sib_send, sib_recv = sems
     c = here.c
-
-    def copy(i):
-        block = held.at[c, here.corner]
+    cut = held.shape[2] // 2
+
+    def copy(i, at):
+        block = held.at[c, here.corners[at]]
         return remote(block, block, send.at[i], recv.at[i], here.square[i])
 
-    def came(i):
-        block = held.at[c, here.corners[i]]
-        return remote(block, block, send.at[i], recv.at[i], here.square[i])
+    def onward(i, at):
+        block = held.at[c, here.corners[at], pl.ds((i - 1) * cut, cut)]
+        return remote(block, block, half_send.at[i - 1], half_recv.at[i - 1], here.square[3 - i])
 
     def pass_on(i):
         block = held.at[c, here.corners[i]]
@@ -591,27 +597,37 @@
         return remote(block, block, sib_send.at[i], sib_recv.at[i], here.sibling)
 
     def finish():
-        for i in range(1, 4):
-            copy(i).wait_send()
+        for i in (1, 2):
+            copy(i, 0).wait_send()
+            onward(i, i).wait_send()
         for i in range(4):
             pass_on(i).wait_send()
 
     ends.append(finish)
-    for i in (3, 1, 2):
-        copy(i).start()
+    for i in (1, 2):
+        copy(i, 0).start()
     pass_on(0).start()
     yield
     passed(0).wait_recv()
     yield
-    for i in (1, 2, 3):
-        came(i).wait_recv()
+    for i in (1, 2):
+        copy(i, i).wait_recv()
+        onward(i, i).start()
         pass_on(i).start()
-        passed(i).wait_recv()
-        yield
+    yield
+    passed(1).wait_recv()
+    yield
+    passed(2).wait_recv()
+    for i in (1, 2):
+        onward(i, 3).wait_recv()
+    pass_on(3).start()
+    yield
+    passed(3).wait_recv()
+    yield
 
 
 def square_sems():
-    return [DMA((4,))] * 4
+    return [DMA((4,))] * 2 + [DMA((2,))] * 2 + [DMA((4,))] * 2
 
 
 def square_scratch():
@@ -619,13 +635,13 @@
     return [buffer(LOW, *shape)] * 3 + [DMA((4,))] * 4
 
 
-def square_sum(here, part, total, scratch, ends):
+def square_sum(here, part, total, scratch):
     landed, ready, final, sib_send, sib_recv, send, recv = scratch
     c = here.c
 
     def swap(i):
         return remote(
-            part.at[1 - c, here.corners[i]], landed.at[i], sib_send.at[i], sib_recv.at[i], here.sibling
+            part(1 - c, here.corners[i]), landed.at[i], sib_send.at[i], sib_recv.at[i], here.sibling
         )
 
     def ship(i):
@@ -636,7 +652,7 @@
 
     def go(i):
         swap(i).wait_recv()
-        value = part[c, here.corners[i]].astype(F32) + landed[i].astype(F32)
+        value = part(c, here.corners[i])[...].astype(F32) + landed[i].astype(F32)
         if i:
             ready[i] = value.astype(LOW)
             ship(i).start()
@@ -647,14 +663,11 @@
         for i in range(1, 4):
             ship(i).wait_recv()
         total[...] += final[1].astype(F32) + final[2].astype(F32) + final[3].astype(F32)
-
-    def finish():
         for i in range(4):
             swap(i).wait_send()
         for i in range(1, 4):
             ship(i).wait_send()
 
-    ends.append(finish)
     return start, go, end
 
 
@@ -717,6 +730,41 @@
     yield
 
 
+def spread_scratch(rows):
+    return [buffer(LOW, 4, rows, WIDTH)] * 3 + [DMA((1,))] * 2 + [DMA((4,))] * 2
+
+
+def spread_sum(here, part, total, scratch, ends):
+    landed, ready, final, y_send, y_recv, z_send, z_recv = scratch
+    z, y = here.z, here.y
+    first = remote(part.at[:, 1 - y], landed, y_send.at[0], y_recv.at[0], here.across)
+
+    def second(k):
+        to = (z + k) % 4
+        return remote(ready.at[to], final.at[k], z_send.at[k], z_recv.at[k], (here.g, to * 2 + y))
+
+    first.start()
+    yield
+    first.wait_recv()
+    ready[...] = (part[:, y].astype(F32) + landed[...].astype(F32)).astype(LOW)
+    for k in (2, 1, 3):
+        second(k).start()
+    yield
+    value = ready[z].astype(F32)
+    for k in range(1, 4):
+        second(k).wait_recv()
+        value += final[k].astype(F32)
+    total[...] = value
+
+    def finish():
+        first.wait_send()
+        for k in range(1, 4):
+            second(k).wait_send()
+
+    ends.append(finish)
+    yield
+
+
 def trade_sems():
     return [DMA((SHARDS,))] * 2
 
@@ -769,13 +817,14 @@
 def scratch_plan():
     plan = dict(
         own_norm=buffer(F32, 8, LANES),
+        own_sems=DMA((SHARDS,)),
         norm=buffer(F32, SHARDS, 8, LANES),
         norm_sems=trade_sems(),
-        wq=buffer(LOW, SHARDS, 2, 64, 3 * LANES),
-        wq_sems=trade_sems() + [DMA((1,))] * 2,
+        wq=buffer(LOW, SHARDS, GROUPS, 32, 3 * LANES),
+        wq_sems=trade_sems() + [DMA((3,))] * 2,
         wo=buffer(LOW, SHARDS, GROUPS, 32, WIDTH),
         wo_sems=gather_sems(),
-        wo_more=[DMA((3,))] * 2,
+        wo_more=[DMA((SHARDS + 2,))] * 2,
         wu=buffer(LOW, SHARDS, 2, 64, HIDDEN),
         wu_sems=trade_sems() + [DMA((1,))] * 2,
         wd=buffer(LOW, 2, 2, ROWS, WIDTH),
@@ -798,7 +847,8 @@
         r2=buffer(F32, ROWS, LANES),
         act=buffer(LOW, 2, 4, ROWS, HIDDEN),
         du=buffer(LOW, 2, 4, ROWS, HIDDEN),
-        da2=buffer(LOW, 2, 4, ROWS, WIDTH),
+        dact=buffer(F32, 2, 4, ROWS, HIDDEN),
+        da2=buffer(LOW, SHARDS, ROWS, WIDTH),
         da2_sum=square_scratch(),
         e2=buffer(F32, ROWS, WIDTH),
         ffn=buffer(LOW, 2, 4, ROWS, WIDTH),
@@ -811,7 +861,6 @@
         gk=buffer(F32, LANES, WIDTH),
         gv=buffer(F32, LANES, WIDTH),
         dqkv=buffer(LOW, SHARDS, ROWS, 3 * LANES),
-        da1=buffer(LOW, SHARDS, ROWS, WIDTH),
         da1_sum=sum_scratch(ROWS),
         e1=buffer(F32, ROWS, WIDTH),
         gd=buffer(LOW, 2, 2, ROWS, WIDTH),
@@ -826,8 +875,8 @@
         gu_sems=[DMA((SHARDS,)), DMA((2, 4))],
         go=buffer(LOW, GROUPS, 256, WIDTH),
         go_sum=cross_scratch(256, WIDTH),
-        go_total=buffer(LOW, SHARDS, 32, WIDTH),
-        go_plane=sum_scratch(32),
+        go_total=buffer(LOW, 4, 2, 32, WIDTH),
+        go_plane=spread_scratch(32),
         gq=buffer(LOW, GROUPS, 256, 3 * LANES),
         gq_sum=cross_scratch(256, 3 * LANES),
         gq_total=buffer(LOW, SHARDS, 32, 3 * LANES),
@@ -858,9 +907,32 @@
         here.g, here.s, here.x, here.c, here.z, here.y, here.half, here.corner
     )
     ends = []
+    quarter = pl.ds(pl.multiple_of(g * 32, 32), 32)
+    beside_g = here.beside[0]
+    wq, wo, wu, wd = b["wq"], b["wo"], b["wu"], b["wd"]
+    wu_rows = pl.ds(pl.multiple_of(x * 64, 64), 64)
+
+    def wu_columns(shard, j):
+        return pl.ds(pl.multiple_of((shard % 4 + j * 4) * HIDDEN + c * 256, 256), 256)
+
+    own_pairs = [
+        (
+            wqkv.at[quarter, pl.ds(pl.multiple_of(j * WIDTH + s * LANES, LANES), LANES)],
+            wq.at[s, g, :, pl.ds(j * LANES, LANES)],
+        )
+        for j in range(3)
+    ]
+    own_pairs.append((wout.at[quarter, :], wo.at[s, g]))
+    own_pairs += [(wup.at[wu_rows, wu_columns(s, j)], wu.at[s, x, :, pl.ds(j * 256, 256)]) for j in range(2)]
+    own_pairs += [
+        (wdown.at[pl.ds(pl.multiple_of(c * 256 + j * ROWS, ROWS), ROWS), :], wd.at[half, j]) for j in range(2)
+    ]
+    own_copies = [pltpu.make_async_copy(*pair, b["own_sems"].at[i]) for i, pair in enumerate(own_pairs)]
+    for copy in own_copies:
+        copy.start()
     greet_all(here)
 
-    norm, own_norm, wq = b["norm"], b["own_norm"], b["wq"]
+    norm, own_norm = b["norm"], b["own_norm"]
     own_norm[...] = jnp.zeros_like(own_norm)
     own_norm[0:4, :] = norm_weight[...].astype(F32)
     norm[s] = own_norm[...]
@@ -872,11 +944,10 @@
     def wq_copies(k):
         device = here.at_shard(k)
         send, recv = b["wq_sems"][:2]
-        half_rows = pl.ds(pl.multiple_of(c * 64, 64), 64)
         return [
             remote(
-                wqkv.at[half_rows, pl.ds(pl.multiple_of(j * WIDTH + device[1] * LANES, LANES), LANES)],
-                wq.at[s, c, :, pl.ds(j * LANES, LANES)],
+                wqkv.at[quarter, pl.ds(pl.multiple_of(j * WIDTH + device[1] * LANES, LANES), LANES)],
+                wq.at[s, g, :, pl.ds(j * LANES, LANES)],
                 send.at[k],
                 recv.at[k],
                 device,
@@ -886,7 +957,7 @@
 
     def wq_whole(k):
         send, recv = b["wq_sems"][:2]
-        block = wq.at[here.from_shard(k), c]
+        block = wq.at[here.from_shard(k), g]
         return remote(block, block, send.at[k], recv.at[k], here.at_shard(k))
 
     for k in range(1, SHARDS):
@@ -904,50 +975,31 @@
     a1_step = plane_gather(here, lambda i: a1.at[i], b["a1_sems"], ends)
     next(a1_step)
 
-    wd = b["wd"]
+    own_copies[3].wait()
+    wo_send, wo_recv = b["wo_more"]
+
+    def wo_beside(i, k):
+        block = wo.at[i, k]
+        return remote(block, block, wo_send.at[i], wo_recv.at[i], here.beside)
+
+    def wo_came(i):
+        wo_beside(i, g).start()
+
+    wo_step = plane_gather(here, lambda i: wo.at[i, g], b["wo_sems"], ends, wo_came)
+    next(wo_step)
+    wo_core = [
+        remote(wo.at[:, k], wo.at[:, k], wo_send.at[SHARDS + i], wo_recv.at[SHARDS + i], here.sibling)
+        for i, k in enumerate((g, beside_g))
+    ]
+
     wd_send, wd_recv = b["wd_sems"]
     wd_rows = pl.ds(pl.multiple_of(c * 256 + x * ROWS, ROWS), ROWS)
     wd_far = remote(wdown.at[wd_rows, :], wd.at[half, x], wd_send.at[0], wd_recv.at[0], here.far)
-    wd_far.start()
-    for j in range(2):
-        wd[half, j] = wdown[pl.ds(pl.multiple_of(c * 256 + j * ROWS, ROWS), ROWS), :]
     wd_beside = remote(
         wd.at[1 - half, x], wd.at[1 - half, x], wd_send.at[1], wd_recv.at[1], here.beside
     )
-    for j in range(3):
-        wq[s, c, :, j * LANES : (j + 1) * LANES] = wqkv[
-            pl.ds(pl.multiple_of(c * 64, 64), 64),
-            pl.ds(pl.multiple_of(j * WIDTH + s * LANES, LANES), LANES),
-        ]
-    dz = b["dz"]
-    own_live = column(live_rows[pl.ds(s, 1), :].astype(F32))
-    dz[c, corner] = (cot[...].astype(F32) * jnp.concatenate([own_live] * SHARDS, 1)).astype(LOW)
-    for k in range(1, SHARDS):
-        wq_whole(k).wait_recv()
-    wq_core = remote(
-        wq.at[:, c], wq.at[:, c], b["wq_sems"][2].at[0], b["wq_sems"][3].at[0], here.sibling
-    )
-    wq_core.start()
-    run(a1_step)
-
-    wo = b["wo"]
-    wo[s, g] = wout[pl.ds(pl.multiple_of(g * 32, 32), 32), :]
-    wo_step = plane_gather(here, lambda i: wo.at[i, g], b["wo_sems"], ends)
-    next(wo_step)
-    wo_send, wo_recv = b["wo_more"]
-    beside_g = here.beside[0]
-    wo_beside = remote(wo.at[:, g], wo.at[:, g], wo_send.at[0], wo_recv.at[0], here.beside)
-    wo_core = [
-        remote(wo.at[:, k], wo.at[:, k], wo_send.at[1 + i], wo_recv.at[1 + i], here.sibling)
-        for i, k in enumerate((g, beside_g))
-    ]
-
-    wu = b["wu"]
+
     wu_send, wu_recv, wu_xsend, wu_xrecv = b["wu_sems"]
-    wu_rows = pl.ds(pl.multiple_of(x * 64, 64), 64)
-
-    def wu_columns(shard, j):
-        return pl.ds(pl.multiple_of((shard % 4 + j * 4) * HIDDEN + c * 256, 256), 256)
 
     def wu_copies(k):
         device = here.at_shard(k)
@@ -966,14 +1018,43 @@
         block = wu.at[here.from_shard(k), x]
         return remote(block, block, wu_send.at[k], wu_recv.at[k], here.at_shard(k))
 
+    wu_beside = remote(wu.at[:, x], wu.at[:, x], wu_xsend.at[0], wu_xrecv.at[0], here.beside)
+
+    dz = b["dz"]
+    own_live = column(live_rows[pl.ds(s, 1), :].astype(F32))
+    dz[c, corner] = (cot[...].astype(F32) * jnp.concatenate([own_live] * SHARDS, 1)).astype(LOW)
+    for k in range(1, SHARDS):
+        wq_whole(k).wait_recv()
+    wq_send, wq_recv = b["wq_sems"][2:]
+    wq_beside = remote(wq.at[:, g], wq.at[:, g], wq_send.at[0], wq_recv.at[0], here.beside)
+    wq_core = [
+        remote(wq.at[:, k], wq.at[:, k], wq_send.at[1 + i], wq_recv.at[1 + i], here.sibling)
+        for i, k in enumerate((g, beside_g))
+    ]
+    for copy in own_copies[:3]:
+        copy.wait()
+    wq_beside.start()
+    wq_core[0].start()
+    next(a1_step)
+    next(wo_step)
+    next(a1_step)
+    next(wo_step)
+    wq_beside.wait_recv()
+    wq_core[1].start()
+    wd_far.start()
+    next(a1_step)
+    next(wo_step)
     for k in range(1, SHARDS):
         for copy in wu_copies(k):
             copy.start()
-    for j in range(2):
-        wu[s, x, :, j * 256 : (j + 1) * 256] = wup[wu_rows, wu_columns(s, j)]
-    wu_beside = remote(wu.at[:, x], wu.at[:, x], wu_xsend.at[0], wu_xrecv.at[0], here.beside)
-
-    wq_core.wait_recv()
+    for copy in own_copies[4:]:
+        copy.wait()
+    run(a1_step)
+    dz_step = square_gather(here, dz, b["dz_sems"], ends)
+    next(dz_step)
+
+    for copy in wq_core:
+        copy.wait_recv()
     qkv, probs = b["qkv"], b["probs"]
     qkv[...] = dot(flat(a1[...]), flat(wq[...])).astype(LOW).reshape(qkv.shape)
     keys = flat(qkv[:, :, LANES : 2 * LANES])
@@ -1011,22 +1092,22 @@
         for j in range(2):
             to = zz * 2 + j
             o_copy(to, (to + SHARDS - s) % SHARDS).start()
-        next(wo_step)
+        if step == 1:
+            run(wo_step)
+            wo_core[0].start()
+    for i in range(SHARDS):
+        wo_beside(i, beside_g).wait_recv()
+    wo_core[1].start()
     attend(z)
     o_all[s] = o_mine[s]
     o_copy(here.across[1], (here.across[1] + SHARDS - s) % SHARDS).start()
-    dz_step = square_gather(here, dz, b["dz_sems"], ends)
-    next(dz_step)
-    run(wo_step)
-    wo_beside.start()
-    wo_core[0].start()
     wd_far.wait_recv()
     wd_beside.start()
     for k in range(1, SHARDS):
         wu_whole(k).wait_recv()
     wu_beside.start()
-    wo_beside.wait_recv()
-    wo_core[1].start()
+    next(dz_step)
+    next(dz_step)
     for k in range(1, SHARDS):
         o_copy(here.from_shard(k), k).wait_recv()
     for copy in wo_core:
@@ -1045,10 +1126,10 @@
     wu_beside.wait_recv()
     wd_beside.wait_recv()
 
-    act, du, da2 = b["act"], b["du"], b["da2"]
+    act, du, da2, dact = b["act"], b["du"], b["da2"], b["dact"]
     up = wu[...].reshape(WIDTH, HIDDEN)
     down = wd[...].reshape(HIDDEN, WIDTH)
-    start, go, end = square_sum(here, da2, b["e2"], b["da2_sum"], ends)
+    start, go, end = square_sum(here, lambda cc, at: da2.at[cc * 4 + at], b["e2"], b["da2_sum"])
     shape = (2, ROWS, HIDDEN)
 
     def feed(i):
@@ -1057,22 +1138,43 @@
         half_erf = 0.5 + 0.5 * lax.erf(u * (0.5**0.5))
         act[:, at] = (u * half_erf).astype(LOW).reshape(shape)
         slope = half_erf + u * jnp.exp(-0.5 * u * u) * (1.0 / math.sqrt(2.0 * math.pi))
-        grad = (dot_nt(flat(dz[:, at]), down) * slope).astype(LOW)
+        grad = (flat(dact[:, at]) * slope).astype(LOW)
         du[:, at] = grad.reshape(shape)
-        da2[:, at] = dot_nt(grad, up).astype(LOW).reshape(2, ROWS, WIDTH)
-
+        grad = dot_nt(grad, up).astype(LOW)
+        for cc in range(2):
+            da2[cc * 4 + at] = grad[cc * ROWS : (cc + 1) * ROWS]
+
+    next(a2_step)
+    run(dz_step)
+    dact[...] = dot_nt(flat(dz[...]), down).reshape(dact.shape)
+    feed(0)
+    start(0)
+    next(a2_step)
+    next(a2_step)
+    feed(1)
+    start(1)
+    next(a2_step)
+    feed(2)
+    start(2)
+    go(1)
+    next(a2_step)
+    feed(3)
+    start(3)
+    go(2)
+    go(3)
+    ffn = b["ffn"]
+    f_start, f_go, f_end = square_sum(here, lambda cc, at: ffn.at[cc, at], b["block"], b["ffn_sum"])
+    ffn[...] = dot(flat(act[...]), down).astype(LOW).reshape(ffn.shape)
     for i in range(4):
-        next(dz_step)
-        next(a2_step)
-        feed(i)
-        start(i)
-        if i > 1:
-            go(i - 1)
-    go(3)
+        f_start(i)
     gd = b["gd"]
     gd[...] = dot_tn(flat(act[...]), flat(dz[...])).astype(LOW).reshape(gd.shape)
     gd_step = pair_sum(here, gd.at[:, 1 - x], lambda i: gd.at[i, x], b["gd_total"], b["gd_sum"], ends)
     next(gd_step)
+    gu = b["gu"]
+    gu[...] = dot_tn(flat(a2[...]), flat(du[...])).astype(LOW).reshape(gu.shape)
+    gu_step = pair_sum(here, gu.at[1 - x], lambda i: gu.at[x, i], b["gu_total"], b["gu_sum"], ends)
+    next(gu_step)
     go(0)
     end()
 
@@ -1085,21 +1187,17 @@
         do_mine[k] = dot_nt(low, wo[k].reshape(ROWS, WIDTH)).astype(LOW)
     do_step = plane_trade(here, do_mine, do_all, b["do_sems"], ends)
     next(do_step)
-    gu = b["gu"]
-    gu[...] = dot_tn(flat(a2[...]), flat(du[...])).astype(LOW).reshape(gu.shape)
-    gu_step = pair_sum(here, gu.at[1 - x], lambda i: gu.at[x, i], b["gu_total"], b["gu_sum"], ends)
-    next(gu_step)
     go_part = b["go"]
     go_part[...] = dot_tn(attended, low).astype(LOW).reshape(go_part.shape)
     go_step = cross_sum(here, go_part, b["go_total"], b["go_sum"], ends)
     next(go_step)
+    next(go_step)
     run(do_step)
-
-    ffn = b["ffn"]
-    f_start, f_go, f_end = square_sum(here, ffn, b["block"], b["ffn_sum"], ends)
-    ffn[...] = dot(flat(act[...]), down).astype(LOW).reshape(ffn.shape)
-    for i in range(4):
-        f_start(i)
+    next(gd_step)
+    for i in range(1, 4):
+        f_go(i)
+    f_go(0)
+
     gk, gv, dqkv = b["gk"], b["gv"], b["dqkv"]
 
     def back(zz, first):
@@ -1127,20 +1225,15 @@
             gv[...] += grad_value
 
     back(0, True)
-    for i in range(1, 4):
-        f_go(i)
-    f_go(0)
-    next(go_step)
     back(1, False)
-    next(gd_step)
+    next(gu_step)
     back(2, False)
     back(3, False)
-    next(gu_step)
     thirds = (SHARDS, ROWS, LANES)
     dqkv[:, :, LANES : 2 * LANES] = (gk[...].T * score_scale).astype(LOW).reshape(thirds)
     dqkv[:, :, 2 * LANES :] = gv[...].T.astype(LOW).reshape(thirds)
 
-    da1, weight = b["da1"], flat(wq[...])
+    da1, weight = da2, flat(wq[...])
 
     def spread(zz):
         pair = pl.ds(zz * 2, 2)
@@ -1152,10 +1245,6 @@
     gq[...] = dot_tn(flat(a1[...]), flat(dqkv[...])).astype(LOW).reshape(gq.shape)
     gq_step = cross_sum(here, gq, b["gq_total"], b["gq_sum"], ends)
     next(gq_step)
-    run(go_step)
-    go_out = plane_sum(here, b["go_total"], out_sum, b["go_plane"], ends)
-    next(go_out)
-    next(da1_step)
     run(gd_step)
     owner = here.y * 4 + c * 2 + x
     stays = (z == g) & (owner == s)
@@ -1167,9 +1256,8 @@
     def _():
         gd_away.start()
 
+    next(gq_step)
     next(da1_step)
-    next(gq_step)
-    next(go_out)
     run(gu_step)
     gu_total, gu_land = b["gu_total"], b["gu_land"]
     gu_send, gu_recv = b["gu_sems"]
@@ -1195,11 +1283,16 @@
 
     for k in range(1, SHARDS):
         gu_copy(k).start()
+    run(go_step)
+    go_out = spread_sum(here, b["go_total"], out_sum, b["go_plane"], ends)
+    next(go_out)
     next(da1_step)
-    next(go_out)
     run(gq_step)
     gq_out = plane_trade(here, b["gq_total"], b["gq_land"], b["gq_sems"], ends)
     next(gq_out)
+    next(da1_step)
+    next(go_out)
+    next(da1_step)
     run(da1_step)
 
     e1, n1 = b["e1"][...], b["n1"][...]
@@ -1287,14 +1380,103 @@
     def _():
         gu_copy(0).wait_send()
 
-    for copy in (wq_core, wd_far, wd_beside, wo_beside, wu_beside, *wo_core):
+    for copy in (wq_beside, wd_far, wd_beside, wu_beside, *wq_core, *wo_core):
         copy.wait_send()
+    for i in range(SHARDS):
+        wo_beside(i, g).wait_send()
     for finish in ends:
         finish()
 
 
+SIZES = ((32, 3 * WIDTH), (32, WIDTH), (32, 4 * WIDTH), (ROWS, WIDTH))
+KINDS = (F32, F32, F32, F32, LOW)
+
+
+def adamw_kernel(rates, *refs):
+    refs = list(refs)
+
+    def take(n):
+        got = refs[:n]
+        del refs[:n]
+        return got
+
+    norm_sum, *norm_old = take(4)
+    sums, olds, passed = take(4), [take(3) for _ in SIZES], take(2)
+    norm_new = take(5)
+    news, handed = [take(5) for _ in SIZES], take(2)
+    held_in, held_out = [take(4) for _ in SIZES], [take(5) for _ in SIZES]
+    held_pass = take(2)
+    in_sem, out_sem, pass_sem = take(3)
+    loads = [
+        [
+            pltpu.make_async_copy(src, dst, in_sem.at[i, j])
+            for j, (src, dst) in enumerate(zip([sums[i], *olds[i]], held_in[i]))
+        ]
+        for i in range(4)
+    ]
+    stores = [
+        [pltpu.make_async_copy(src, dst, out_sem.at[i, j]) for j, (src, dst) in enumerate(zip(held_out[i], news[i]))]
+        for i in range(4)
+    ]
+    passes = [pltpu.make_async_copy(passed[i], held_pass[i], pass_sem.at[i]) for i in range(2)]
+    hands = [pltpu.make_async_copy(held_pass[i], handed[i], pass_sem.at[2 + i]) for i in range(2)]
+    order = (2, 0, 3, 1)
+    for i in order:
+        for copy in loads[i]:
+            copy.start()
+    for copy in passes:
+        copy.start()
+    count = norm_sum[4:5, 0:1]
+    results = adamw(norm_sum[0:4, 0:32], count, *[ref[...] for ref in norm_old], rates[4], 0.0)
+    for ref, value in zip(norm_new, results):
+        ref[...] = value
+    for i in order:
+        for copy in loads[i]:
+            copy.wait()
+        rows, cols = SIZES[i]
+        step = 16
+
+        def some(k, carry):
+            at = pl.ds(pl.multiple_of(k * step, step), step)
+            for first in range(0, cols, WIDTH):
+                lanes = slice(first, first + WIDTH)
+                summed, *old = [ref[at, lanes] for ref in held_in[i]]
+                results = adamw(summed, count, *old, rates[i], 0.1)
+                for ref, value in zip(held_out[i], results):
+                    ref[at, lanes] = value
+            return carry
+
+        lax.fori_loop(0, rows // step, some, 0)
+        for copy in stores[i]:
+            copy.start()
+    for i in range(2):
+        passes[i].wait()
+        hands[i].start()
+    for i in order:
+        for copy in stores[i]:
+            copy.wait()
+    for copy in hands:
+        copy.wait()
+
+
 def shaped(kind, *shape):
     return jax.ShapeDtypeStruct(shape, kind)
+
+
+def call_adamw(rates, norms, sums, olds, passed):
+    return pl.pallas_call(
+        functools.partial(adamw_kernel, rates),
+        out_shape=[shaped(kind, *norms[1].shape) for kind in KINDS]
+        + [shaped(kind, *size) for size in SIZES for kind in KINDS]
+        + [shaped(F32, ROWS, WIDTH)] * 2,
+        in_specs=[VMEM] * 4 + [ANY] * 18,
+        out_specs=[VMEM] * 5 + [ANY] * 22,
+        scratch_shapes=[buffer(F32, *size) for size in SIZES for _ in range(4)]
+        + [buffer(kind, *size) for size in SIZES for kind in KINDS]
+        + [buffer(F32, ROWS, WIDTH)] * 2
+        + [DMA((4, 4)), DMA((4, 5)), DMA((4,))],
+        compiler_params=pltpu.CompilerParams(vmem_limit_bytes=32 * 2**20),
+    )(*norms, *sums, *olds, *passed)
 
 
 def fast_body(
@@ -1328,25 +1510,32 @@
             shaped(F32, ROWS, WIDTH),
             shaped(F32, 8, LANES),
         ],
-        in_specs=[VMEM] * len(args),
+        in_specs=[VMEM] * 5 + [ANY] * 4,
         out_specs=[VMEM] * 7,
         scratch_shapes=scratch,
         compiler_params=pltpu.CompilerParams(
-            collective_id=0, has_side_effects=True, vmem_limit_bytes=62 * 2**20
+            collective_id=0, has_side_effects=True, vmem_limit_bytes=60 * 2**20
         ),
     )(*args)
-    norm_own = norm_sum[:, :32]
-    total_count = norm_own[4, 0]
     model_width, hidden = tokens.shape[1], up_weight.shape[1]
-    return (
-        block_out,
-        input_grad,
-        *adamw(qkv_sum, total_count, qkv_master, qkv_first, qkv_second, model_width ** (-0.5), 0.1),
-        *adamw(out_sum, total_count, out_master, out_first, out_second, math.sqrt(rows) / 64, 0.1),
-        *adamw(up_sum, total_count, up_master, up_first, up_second, model_width ** (-0.5), 0.1),
-        *adamw(down_sum, total_count, down_master, down_first, down_second, hidden ** (-0.5), 0.1),
-        *adamw(norm_own[:4], total_count, norm_master, norm_first, norm_second, 0.4, 0.0),
-    )
+    rates = (
+        model_width ** (-0.5),
+        math.sqrt(rows) / 64,
+        model_width ** (-0.5),
+        hidden ** (-0.5),
+        0.4,
+    )
+    news = call_adamw(
+        rates,
+        (norm_sum, norm_master, norm_first, norm_second),
+        (qkv_sum, out_sum, up_sum, down_sum),
+        (
+            qkv_master, qkv_first, qkv_second, out_master, out_first, out_second,
+            up_master, up_first, up_second, down_master, down_first, down_second,
+        ),
+        (block_out, input_grad),
+    )
+    return (*news[25:], *news[5:25], *news[:5])
 
 
 def suits(mesh):

time: 230 us -> 194 us (0.84)
  Pallas kernels: 214 us -> 182 us
  other arithmetic: 10.5 us -> 0 us
  local copies, waits for them, and re-layouts: 3.99 us -> 10.5 us
    pallas_call x1, Pallas kernels: 214 us -> 176 us  [fast_body(): pl.pallas_call(step_kernel, out_shape=[shaped(F32, ROWS, WIDTH), shaped(F...]
    convert_element_type x5 -> x0, other arithmetic: 10.5 us -> none  [adamw(): return (gradient, moment, square, updated, updated.astype(jnp.bfloat16))]
    unnamed x44, local copies, waits for them, and re-layouts: 3.48 us -> 10.5 us
    pallas_call x0 -> x1, Pallas kernels: none -> 6.5 us  [call_adamw(): pl.pallas_call(functools.partial(adamw_kernel, rates), out_shape=[shaped(...]
where the time goes in v3:
time: 194 us
  Pallas kernels  182 us (94%)
  local copies, waits for them, and re-layouts  10.5 us (5%)
    pallas_call x1, Pallas kernels, fast_body(): pl.pallas_call(step_kernel, out_shape=[shaped(F32, ROWS, WIDTH), shaped(F...  176 us
    unnamed x44, local copies, waits for them, and re-layouts  10.5 us
    pallas_call x1, Pallas kernels, call_adamw(): pl.pallas_call(functools.partial(adamw_kernel, rates), out_shape=[shaped(...  6.5 us

profile of v3, /device:TPU:0, one launch (start us, length us, event | category | flops | bytes accessed | tf_op | source)
XLA Modules:
  0.0 193.9 jit_solution(8182294755472594351)
XLA Ops:
  0.7 0.0 copy-start
  0.7 0.0 copy-start.1
  0.7 0.0 copy-start.2
  0.7 0.0 copy-start.3
  0.7 0.0 copy-start.4
  0.7 0.0 copy-start.5
  0.7 0.0 copy-start.10
  0.7 0.0 copy-start.14
  0.8 0.0 copy-start.20
  0.8 0.0 copy-start.21
  0.8 175.8 %shard_map.439 = (f32[128,1024]{1,0:T(8,128)}, f32[128,1024]{1,0:T(8,128)}, f32[32,3072]{1,0:T(8,128)}, f32[32,4096]{1,0:T(8,128)}, f32[32,1024]{1,0:T(8,128)}, /*index=5*/f32[128,1024]{1,0:T(8,128)}, f32[8,128]{1,0:T(8,128)}) custom-call(bf16[128,1024]{1,0:T(8,128)(2,1)} %refs_0_.1, bf16[128,1024]{1,0:T(8,128)(2,1)} %refs_1_.2, s32[8,128]{1,0:T(8,128)} %bitcast.2, ...), custom_call_target="tpu_custom_call" | custom-call | tf_op jit(solution)/shard_map/pallas_call | solution.py:1502
  176.6 0.0 copy-start.18
  176.6 0.0 copy-start.19
  176.6 0.0 copy-done
  176.7 0.0 copy-done.1
  176.7 0.0 copy-done.2
  176.7 0.0 copy-done.3
  176.7 0.0 copy-done.4
  176.7 0.0 copy-done.5
  176.7 0.0 copy-done.10
  176.7 0.0 copy-done.14
  176.7 0.0 copy-done.20
  176.7 0.0 copy-done.21
  176.7 0.5 copy-done.18
  177.3 0.0 copy-done.19
  177.3 0.0 copy-start.6
  177.3 1.0 copy-done.6
  178.4 0.0 copy-start.7
  178.4 1.0 copy-done.7
  179.4 0.0 copy-start.8
  179.4 1.0 copy-done.8
  180.4 0.0 copy-start.9
  180.4 1.0 copy-done.9
  181.5 0.0 copy-start.11
  181.5 1.0 copy-done.11
  182.5 0.0 copy-start.12
  182.5 1.0 copy-done.12
  183.5 0.0 copy-start.13
  183.5 1.0 copy-done.13
  184.5 0.0 copy-start.15
  184.5 0.9 copy-done.15
  185.4 0.0 copy-start.16
  185.4 0.9 copy-done.16
  186.3 0.0 copy-start.17
  186.3 0.9 copy-done.17
  187.2 6.5 %shard_map.440 = (f32[4,32]{1,0:T(4,128)}, f32[4,32]{1,0:T(4,128)}, f32[4,32]{1,0:T(4,128)}, f32[4,32]{1,0:T(4,128)}, bf16[4,32]{1,0:T(4,128)(2,1)}, /*index=5*/...) custom-call(f32[8,128]{1,0:T(8,128)S(1)} %copy-done.18, ...), custom_call_target="tpu_custom_call" | custom-call | tf_op jit(solution)/shard_map/pallas_call | solution.py:1467
Async XLA Ops:
  0.7 176.0 %copy-start = (f32[32,4096]{1,0:T(8,128)S(1)}, f32[32,4096]{1,0:T(8,128)}, u32[]{:S(2)}) copy-start(f32[32,4096]{1,0:T(8,128)} %refs_14_.1) | copy-start | bytes 1572868
  0.7 176.0 %copy-start.1 = (f32[32,4096]{1,0:T(8,128)S(1)}, f32[32,4096]{1,0:T(8,128)}, u32[]{:S(2)}) copy-start(f32[32,4096]{1,0:T(8,128)} %refs_15_.1) | copy-start | bytes 1572868
  0.7 176.0 %copy-start.2 = (f32[32,4096]{1,0:T(8,128)S(1)}, f32[32,4096]{1,0:T(8,128)}, u32[]{:S(2)}) copy-start(f32[32,4096]{1,0:T(8,128)} %refs_16_.1) | copy-start | bytes 1572868
  0.7 176.0 %copy-start.3 = (f32[128,1024]{1,0:T(8,128)S(1)}, f32[128,1024]{1,0:T(8,128)}, u32[]{:S(2)}) copy-start(f32[128,1024]{1,0:T(8,128)} %refs_17_.1) | copy-start | bytes 1572868
  0.7 176.0 %copy-start.4 = (f32[128,1024]{1,0:T(8,128)S(1)}, f32[128,1024]{1,0:T(8,128)}, u32[]{:S(2)}) copy-start(f32[128,1024]{1,0:T(8,128)} %refs_18_.1) | copy-start | bytes 1572868
  0.7 176.0 %copy-start.5 = (f32[128,1024]{1,0:T(8,128)S(1)}, f32[128,1024]{1,0:T(8,128)}, u32[]{:S(2)}) copy-start(f32[128,1024]{1,0:T(8,128)} %refs_19_.1) | copy-start | bytes 1572868
  0.7 176.0 %copy-start.10 = (f32[32,3072]{1,0:T(8,128)S(1)}, f32[32,3072]{1,0:T(8,128)}, u32[]{:S(2)}) copy-start(f32[32,3072]{1,0:T(8,128)} %refs_8_.3) | copy-start | bytes 1179652
  0.7 176.0 %copy-start.14 = (f32[32,1024]{1,0:T(8,128)S(1)}, f32[32,1024]{1,0:T(8,128)}, u32[]{:S(2)}) copy-start(f32[32,1024]{1,0:T(8,128)} %refs_11_.1) | copy-start | bytes 393220
  0.8 176.0 %copy-start.20 = (f32[4,32]{1,0:T(4,128)S(1)}, f32[4,32]{1,0:T(4,128)}, u32[]{:S(2)}) copy-start(f32[4,32]{1,0:T(4,128)} %refs_2_.1) | copy-start | bytes 1540
  0.8 176.0 %copy-start.21 = (f32[4,32]{1,0:T(4,128)S(1)}, f32[4,32]{1,0:T(4,128)}, u32[]{:S(2)}) copy-start(f32[4,32]{1,0:T(4,128)} %refs_3_.1) | copy-start | bytes 1540
  176.6 0.7 copy-start.18
  176.6 0.7 copy-start.19
  177.3 1.0 copy-start.6
  178.4 1.0 copy-start.7
  179.4 1.0 copy-start.8
  180.4 1.0 copy-start.9
  181.5 1.0 copy-start.11
  182.5 1.0 copy-start.12
  183.5 1.0 copy-start.13
  184.5 0.9 copy-start.15
  185.4 0.9 copy-start.16
  186.3 0.9 copy-start.17

commit v4 on v3

--- a/solution.py
+++ b/solution.py
@@ -604,26 +604,27 @@
             pass_on(i).wait_send()
 
     ends.append(finish)
-    for i in (1, 2):
-        copy(i, 0).start()
-    pass_on(0).start()
-    yield
-    passed(0).wait_recv()
-    yield
-    for i in (1, 2):
-        copy(i, i).wait_recv()
-        onward(i, i).start()
-        pass_on(i).start()
-    yield
-    passed(1).wait_recv()
-    yield
-    passed(2).wait_recv()
-    for i in (1, 2):
-        onward(i, 3).wait_recv()
-    pass_on(3).start()
-    yield
-    passed(3).wait_recv()
-    yield
+
+    def start():
+        for i in (1, 2):
+            copy(i, 0).start()
+        pass_on(0).start()
+
+    def relay():
+        for i in (1, 2):
+            copy(i, i).wait_recv()
+            onward(i, i).start()
+            pass_on(i).start()
+
+    def last():
+        for i in (1, 2):
+            onward(i, 3).wait_recv()
+        pass_on(3).start()
+
+    def got(i):
+        passed(i).wait_recv()
+
+    return start, relay, last, got
 
 
 def square_sems():
@@ -703,23 +704,23 @@
     yield
 
 
-def pair_scratch(rows, cols):
-    return [buffer(LOW, 2, rows, cols)] + [buffer(LOW, rows, cols)] * 2 + [DMA((1,))] * 4
-
-
-def pair_sum(here, outgoing, mine, total, scratch, ends):
+def pair_scratch(rows, cols, parts=1):
+    return [buffer(LOW, parts, 2, rows, cols)] + [buffer(LOW, parts, rows, cols)] * 2 + [DMA((1,))] * 4
+
+
+def pair_sum(here, part, total, scratch, ends):
     landed, ready, final, x_send, x_recv, z_send, z_recv = scratch
-    half = here.half
-    first = remote(outgoing, landed, x_send.at[0], x_recv.at[0], here.beside)
+    x, half = here.x, here.half
+    first = remote(part.at[1 - x], landed, x_send.at[0], x_recv.at[0], here.beside)
     second = remote(ready, final, z_send.at[0], z_recv.at[0], here.far)
     first.start()
     yield
     first.wait_recv()
-    ready[...] = (mine(1 - half)[...].astype(F32) + landed[1 - half].astype(F32)).astype(LOW)
+    ready[...] = (part[x, :, 1 - half].astype(F32) + landed[:, 1 - half].astype(F32)).astype(LOW)
     second.start()
     yield
     second.wait_recv()
-    value = mine(half)[...].astype(F32) + landed[half].astype(F32) + final[...].astype(F32)
+    value = part[x, :, half].astype(F32) + landed[:, half].astype(F32) + final[...].astype(F32)
     total[...] = value.astype(LOW).reshape(total.shape)
 
     def finish():
@@ -863,16 +864,16 @@
         dqkv=buffer(LOW, SHARDS, ROWS, 3 * LANES),
         da1_sum=sum_scratch(ROWS),
         e1=buffer(F32, ROWS, WIDTH),
-        gd=buffer(LOW, 2, 2, ROWS, WIDTH),
+        gd=buffer(LOW, 2, 1, 2, ROWS, WIDTH),
         gd_sum=pair_scratch(ROWS, WIDTH),
         gd_total=buffer(LOW, ROWS, WIDTH),
         gd_land=buffer(LOW, ROWS, WIDTH),
         gd_sems=[DMA((1,))] * 2,
-        gu=buffer(LOW, 2, 2, 256, HIDDEN),
-        gu_sum=pair_scratch(256, HIDDEN),
-        gu_total=buffer(LOW, SHARDS, 32, HIDDEN),
+        gu=buffer(LOW, 2, 2, 2, ROWS, HIDDEN),
+        gu_sum=pair_scratch(ROWS, HIDDEN, 2),
+        gu_total=buffer(LOW, 2, 4, 32, HIDDEN),
         gu_land=buffer(LOW, 2, 4, 32, HIDDEN),
-        gu_sems=[DMA((SHARDS,)), DMA((2, 4))],
+        gu_sems=[DMA((2, 4)), DMA((2, 4))],
         go=buffer(LOW, GROUPS, 256, WIDTH),
         go_sum=cross_scratch(256, WIDTH),
         go_total=buffer(LOW, 4, 2, 32, WIDTH),
@@ -1050,8 +1051,8 @@
     for copy in own_copies[4:]:
         copy.wait()
     run(a1_step)
-    dz_step = square_gather(here, dz, b["dz_sems"], ends)
-    next(dz_step)
+    dz_start, dz_relay, dz_last, dz_got = square_gather(here, dz, b["dz_sems"], ends)
+    dz_start()
 
     for copy in wq_core:
         copy.wait_recv()
@@ -1106,8 +1107,7 @@
     for k in range(1, SHARDS):
         wu_whole(k).wait_recv()
     wu_beside.start()
-    next(dz_step)
-    next(dz_step)
+    dz_relay()
     for k in range(1, SHARDS):
         o_copy(here.from_shard(k), k).wait_recv()
     for copy in wo_core:
@@ -1121,8 +1121,10 @@
     b["r2"][...] = jnp.broadcast_to(inverse, (ROWS, LANES))
     a2 = b["a2"]
     a2[c, corner] = (n2 * wide(norm, 2) + wide(norm, 3)).astype(LOW)
-    a2_step = square_gather(here, a2, b["a2_sems"], ends)
-    next(a2_step)
+    a2_start, a2_relay, a2_last, a2_got = square_gather(here, a2, b["a2_sems"], ends)
+    a2_start()
+    dz_last()
+    a2_relay()
     wu_beside.wait_recv()
     wd_beside.wait_recv()
 
@@ -1144,20 +1146,21 @@
         for cc in range(2):
             da2[cc * 4 + at] = grad[cc * ROWS : (cc + 1) * ROWS]
 
-    next(a2_step)
-    run(dz_step)
+    for i in range(4):
+        dz_got(i)
     dact[...] = dot_nt(flat(dz[...]), down).reshape(dact.shape)
+    a2_got(0)
     feed(0)
     start(0)
-    next(a2_step)
-    next(a2_step)
+    a2_got(1)
     feed(1)
     start(1)
-    next(a2_step)
+    a2_last()
+    a2_got(2)
     feed(2)
     start(2)
     go(1)
-    next(a2_step)
+    a2_got(3)
     feed(3)
     start(3)
     go(2)
@@ -1169,11 +1172,11 @@
         f_start(i)
     gd = b["gd"]
     gd[...] = dot_tn(flat(act[...]), flat(dz[...])).astype(LOW).reshape(gd.shape)
-    gd_step = pair_sum(here, gd.at[:, 1 - x], lambda i: gd.at[i, x], b["gd_total"], b["gd_sum"], ends)
+    gd_step = pair_sum(here, gd, b["gd_total"], b["gd_sum"], ends)
     next(gd_step)
     gu = b["gu"]
     gu[...] = dot_tn(flat(a2[...]), flat(du[...])).astype(LOW).reshape(gu.shape)
-    gu_step = pair_sum(here, gu.at[1 - x], lambda i: gu.at[x, i], b["gu_total"], b["gu_sum"], ends)
+    gu_step = pair_sum(here, gu, b["gu_total"], b["gu_sum"], ends)
     next(gu_step)
     go(0)
     end()
@@ -1245,51 +1248,64 @@
     gq[...] = dot_tn(flat(a1[...]), flat(dqkv[...])).astype(LOW).reshape(gq.shape)
     gq_step = cross_sum(here, gq, b["gq_total"], b["gq_sum"], ends)
     next(gq_step)
-    run(gd_step)
-    owner = here.y * 4 + c * 2 + x
-    stays = (z == g) & (owner == s)
+    owner = here.y * 4 + c * 2 + half
+    holder = x * 2 + here.near
+    stays = (holder == g) & (owner == s)
     gd_away = remote(
-        b["gd_total"], b["gd_land"], b["gd_sems"][0].at[0], b["gd_sems"][1].at[0], (z, owner)
-    )
-
-    @pl.when(jnp.logical_not(stays))
-    def _():
-        gd_away.start()
-
+        b["gd_total"], b["gd_land"], b["gd_sems"][0].at[0], b["gd_sems"][1].at[0], (holder, owner)
+    )
+    gu_total, gu_land = b["gu_total"], b["gu_land"]
+    gu_send, gu_recv = b["gu_sems"]
+
+    def gu_copy(k, i):
+        core = here.g if k == 0 else here.sibling[0]
+        cc = c if k == 0 else 1 - c
+        return remote(
+            gu_total.at[cc, here.corners[i]],
+            gu_land.at[c, corner],
+            gu_send.at[k, i],
+            gu_recv.at[k, i],
+            (core, here.square[i][1]),
+        )
+
+    def gu_came(k, i):
+        cc = c if k == 0 else 1 - c
+        block = gu_land.at[cc, here.corners[i]]
+        return remote(block, block, gu_send.at[k, i], gu_recv.at[k, i], here.sibling)
+
+    others = [(k, i) for k in range(2) for i in range(4) if (k, i) != (0, 0)]
+
+    def send_gd():
+        run(gd_step)
+
+        @pl.when(jnp.logical_not(stays))
+        def _():
+            gd_away.start()
+
+    def send_gu():
+        run(gu_step)
+        gu_land[c, corner] = gu_total[c, corner]
+        for k, i in others:
+            gu_copy(k, i).start()
+
+    go_out = spread_sum(here, b["go_total"], out_sum, b["go_plane"], ends)
+    gq_out = plane_trade(here, b["gq_total"], b["gq_land"], b["gq_sems"], ends)
+
+    def send_go():
+        run(go_step)
+        next(go_out)
+
+    def send_gq():
+        run(gq_step)
+        next(gq_out)
+
+    send_gd()
     next(gq_step)
     next(da1_step)
-    run(gu_step)
-    gu_total, gu_land = b["gu_total"], b["gu_land"]
-    gu_send, gu_recv = b["gu_sems"]
-
-    def gu_copy(k):
-        to = (s + k) % SHARDS
-        return remote(
-            gu_total.at[to], gu_land.at[c, corner], gu_send.at[k], gu_recv.at[c, corner], (x * 2 + half, to)
-        )
-
-    def gu_came(cc, at):
-        return remote(
-            gu_total.at[0], gu_land.at[cc, at], gu_send.at[0], gu_recv.at[cc, at], here.sibling
-        )
-
-    @pl.when(c == half)
-    def _():
-        gu_land[c, corner] = gu_total[s]
-
-    @pl.when(c != half)
-    def _():
-        gu_copy(0).start()
-
-    for k in range(1, SHARDS):
-        gu_copy(k).start()
-    run(go_step)
-    go_out = spread_sum(here, b["go_total"], out_sum, b["go_plane"], ends)
-    next(go_out)
+    send_gu()
+    send_go()
     next(da1_step)
-    run(gq_step)
-    gq_out = plane_trade(here, b["gq_total"], b["gq_land"], b["gq_sems"], ends)
-    next(gq_out)
+    send_gq()
     next(da1_step)
     next(go_out)
     next(da1_step)
@@ -1332,13 +1348,10 @@
     f_end()
     block_out[...] = b["h1"][...] + b["block"][...]
     run(go_out)
+    for k, i in others:
+        gu_came(k, i).wait_recv()
     for cc in range(2):
         for at in range(4):
-
-            @pl.when(jnp.logical_not((cc == c) & (at == corner) & (c == half)))
-            def _():
-                gu_came(cc, at).wait_recv()
-
             for j in range(2):
                 first = (j * 4 + at) * HIDDEN + cc * 256
                 up_sum[:, first : first + 256] = gu_land[cc, at, :, j * 256 : (j + 1) * 256].astype(F32)
@@ -1374,12 +1387,8 @@
         wq_whole(k).wait_send()
         wu_whole(k).wait_send()
         o_copy(here.at_shard(k)[1], k).wait_send()
-        gu_copy(k).wait_send()
-
-    @pl.when(c != half)
-    def _():
-        gu_copy(0).wait_send()
-
+    for k, i in others:
+        gu_copy(k, i).wait_send()
     for copy in (wq_beside, wd_far, wd_beside, wu_beside, *wq_core, *wo_core):
         copy.wait_send()
     for i in range(SHARDS):
@@ -1475,7 +1484,7 @@
         + [buffer(kind, *size) for size in SIZES for kind in KINDS]
         + [buffer(F32, ROWS, WIDTH)] * 2
         + [DMA((4, 4)), DMA((4, 5)), DMA((4,))],
-        compiler_params=pltpu.CompilerParams(vmem_limit_bytes=32 * 2**20),
+        compiler_params=pltpu.CompilerParams(vmem_limit_bytes=60 * 2**20),
     )(*norms, *sums, *olds, *passed)
 
 

time: 194 us -> 176 us (0.907)
  local copies, waits for them, and re-layouts: 10.5 us -> 0 us
  Pallas kernels: 182 us -> 175 us
    unnamed x44 -> x0, local copies, waits for them, and re-layouts: 10.5 us -> none
    pallas_call x1, Pallas kernels: 176 us -> 168 us  [fast_body(): pl.pallas_call(step_kernel, out_shape=[shaped(F32, ROWS, WIDTH), shaped(F...]
where the time goes in v4:
time: 176 us
  Pallas kernels  175 us (99%)
    pallas_call x1, Pallas kernels, fast_body(): pl.pallas_call(step_kernel, out_shape=[shaped(F32, ROWS, WIDTH), shaped(F...  168 us
    pallas_call x1, Pallas kernels, call_adamw(): pl.pallas_call(functools.partial(adamw_kernel, rates), out_shape=[shaped(...  6.94 us

profile of v4, /device:TPU:0, one launch (start us, length us, event | category | flops | bytes accessed | tf_op | source)
XLA Modules:
  0.0 176.3 jit_solution(10596510080471089324)
XLA Ops:
  0.7 168.5 %shard_map.439 = (f32[128,1024]{1,0:T(8,128)}, f32[128,1024]{1,0:T(8,128)}, f32[32,3072]{1,0:T(8,128)}, f32[32,4096]{1,0:T(8,128)}, f32[32,1024]{1,0:T(8,128)}, /*index=5*/f32[128,1024]{1,0:T(8,128)}, f32[8,128]{1,0:T(8,128)}) custom-call(bf16[128,1024]{1,0:T(8,128)(2,1)} %refs_0_.1, bf16[128,1024]{1,0:T(8,128)(2,1)} %refs_1_.2, s32[8,128]{1,0:T(8,128)} %bitcast.2, ...), custom_call_target="tpu_custom_call" | custom-call | tf_op jit(solution)/shard_map/pallas_call | solution.py:1511
  169.2 6.9 %shard_map.440 = (f32[4,32]{1,0:T(4,128)}, f32[4,32]{1,0:T(4,128)}, f32[4,32]{1,0:T(4,128)}, f32[4,32]{1,0:T(4,128)}, bf16[4,32]{1,0:T(4,128)(2,1)}, /*index=5*/...) custom-call(f32[8,128]{1,0:T(8,128)} %get-tuple-element.61.refs_0_, ...), custom_call_target="tpu_custom_call" | custom-call | tf_op jit(solution)/shard_map/pallas_call | solution.py:1476

commit v5 on v4

--- a/solution.py
+++ b/solution.py
@@ -375,9 +375,6 @@
     def at_shard(self, k):
         return (self.g, (self.s + k) % SHARDS)
 
-    def from_shard(self, k):
-        return (self.s + SHARDS - k) % SHARDS
-
 
 def remote(src, dst, send, recv, device):
     return pltpu.make_async_remote_copy(
@@ -580,12 +577,14 @@
     c = here.c
     cut = held.shape[2] // 2
 
-    def copy(i, at):
-        block = held.at[c, here.corners[at]]
-        return remote(block, block, send.at[i], recv.at[i], here.square[i])
+    def part(at, k):
+        return held.at[c, here.corners[at], pl.ds(k * cut, cut)]
+
+    def copy(i, at, k):
+        return remote(part(at, k), part(at, k), send.at[i - 1, k], recv.at[i - 1, k], here.square[i])
 
     def onward(i, at):
-        block = held.at[c, here.corners[at], pl.ds((i - 1) * cut, cut)]
+        block = part(at, i - 1)
         return remote(block, block, half_send.at[i - 1], half_recv.at[i - 1], here.square[3 - i])
 
     def pass_on(i):
@@ -598,7 +597,8 @@
 
     def finish():
         for i in (1, 2):
-            copy(i, 0).wait_send()
+            for k in range(2):
+                copy(i, 0, k).wait_send()
             onward(i, i).wait_send()
         for i in range(4):
             pass_on(i).wait_send()
@@ -606,14 +606,17 @@
     ends.append(finish)
 
     def start():
-        for i in (1, 2):
-            copy(i, 0).start()
+        for k in range(2):
+            for i in (1, 2):
+                copy(i, 0, (i - 1 + k) % 2).start()
         pass_on(0).start()
 
     def relay():
         for i in (1, 2):
-            copy(i, i).wait_recv()
+            copy(i, i, i - 1).wait_recv()
             onward(i, i).start()
+        for i in (1, 2):
+            copy(i, i, 2 - i).wait_recv()
             pass_on(i).start()
 
     def last():
@@ -628,7 +631,7 @@
 
 
 def square_sems():
-    return [DMA((4,))] * 2 + [DMA((2,))] * 2 + [DMA((4,))] * 2
+    return [DMA((2, 2))] * 2 + [DMA((2,))] * 2 + [DMA((4,))] * 2
 
 
 def square_scratch():
@@ -767,26 +770,37 @@
 
 
 def trade_sems():
-    return [DMA((SHARDS,))] * 2
-
-
-def plane_trade(here, mine, theirs, sems, ends):
+    return [DMA((1,))] * 2
+
+
+def all_sent(here, seven, sems):
+    remote(seven, seven, sems[0].at[0], sems[1].at[0], here.across).wait_send()
+
+
+def all_came(here, seven, sems):
+    remote(seven, seven, sems[0].at[0], sems[1].at[0], here.across).wait_recv()
+
+
+def plane_trade(here, mine, theirs, sems, ends, stay=None):
     send, recv = sems
 
     def copy(k):
         device = here.at_shard(k)
-        return remote(mine.at[device[1]], theirs.at[here.s], send.at[k], recv.at[k], device)
+        return remote(mine.at[device[1]], theirs.at[here.s], send.at[0], recv.at[0], device)
 
     for k in range(1, SHARDS):
         copy(k).start()
-    theirs[here.s] = mine[here.s]
+    if stay is None:
+        theirs[here.s] = mine[here.s]
+    else:
+        stay.start()
     yield
-    for k in range(1, SHARDS):
-        copy(k).wait_recv()
+    all_came(here, theirs.at[pl.ds(0, SHARDS - 1)], sems)
 
     def finish():
-        for k in range(1, SHARDS):
-            copy(k).wait_send()
+        all_sent(here, mine.at[pl.ds(0, SHARDS - 1)], sems)
+        if stay is not None:
+            stay.wait()
 
     ends.append(finish)
     yield
@@ -852,7 +866,7 @@
         da2=buffer(LOW, SHARDS, ROWS, WIDTH),
         da2_sum=square_scratch(),
         e2=buffer(F32, ROWS, WIDTH),
-        ffn=buffer(LOW, 2, 4, ROWS, WIDTH),
+        ffn=buffer(LOW, SHARDS, ROWS, WIDTH),
         ffn_sum=square_scratch(),
         block=buffer(F32, ROWS, WIDTH),
         dh1=buffer(F32, ROWS, WIDTH),
@@ -867,12 +881,10 @@
         gd=buffer(LOW, 2, 1, 2, ROWS, WIDTH),
         gd_sum=pair_scratch(ROWS, WIDTH),
         gd_total=buffer(LOW, ROWS, WIDTH),
-        gd_land=buffer(LOW, ROWS, WIDTH),
         gd_sems=[DMA((1,))] * 2,
         gu=buffer(LOW, 2, 2, 2, ROWS, HIDDEN),
         gu_sum=pair_scratch(ROWS, HIDDEN, 2),
         gu_total=buffer(LOW, 2, 4, 32, HIDDEN),
-        gu_land=buffer(LOW, 2, 4, 32, HIDDEN),
         gu_sems=[DMA((2, 4)), DMA((2, 4))],
         go=buffer(LOW, GROUPS, 256, WIDTH),
         go_sum=cross_scratch(256, WIDTH),
@@ -881,12 +893,13 @@
         gq=buffer(LOW, GROUPS, 256, 3 * LANES),
         gq_sum=cross_scratch(256, 3 * LANES),
         gq_total=buffer(LOW, SHARDS, 32, 3 * LANES),
-        gq_land=buffer(LOW, SHARDS, 32, 3 * LANES),
         gq_sems=trade_sems(),
-        np_mine=buffer(F32, GROUPS, 8, 2 * LANES),
-        np_land=buffer(F32, GROUPS, 8, 2 * LANES),
-        np_all=buffer(F32, SHARDS, 8, 2 * LANES),
-        np_sems=[DMA((GROUPS,))] * 2 + trade_sems(),
+        np_mine=buffer(F32, SHARDS, 8, LANES),
+        np_land=buffer(F32, GROUPS * SHARDS, 8, LANES),
+        np_sems=trade_sems(),
+        go_sum32=buffer(F32, 32, WIDTH),
+        dx=buffer(F32, ROWS, WIDTH),
+        out_sems=DMA((6,)),
     )
     return plan
 
@@ -896,7 +909,7 @@
     inputs, refs = refs[:9], refs[9:]
     outputs, refs = refs[:7], list(refs[7:])
     tok, cot, item_rows, live_rows, norm_weight, wqkv, wout, wup, wdown = inputs
-    block_out, input_grad, qkv_sum, up_sum, out_sum, down_sum, norm_sum = outputs
+    block_out, input_grad, gq_land, gu_land, out_sum, gd_land, norm_sum = outputs
     b = {}
     for name, kind in plan.items():
         many = isinstance(kind, list)
@@ -940,7 +953,7 @@
 
     def norm_copy(k):
         send, recv = b["norm_sems"]
-        return remote(own_norm, norm.at[s], send.at[k], recv.at[k], here.at_shard(k))
+        return remote(own_norm, norm.at[s], send.at[0], recv.at[0], here.at_shard(k))
 
     def wq_copies(k):
         device = here.at_shard(k)
@@ -949,17 +962,12 @@
             remote(
                 wqkv.at[quarter, pl.ds(pl.multiple_of(j * WIDTH + device[1] * LANES, LANES), LANES)],
                 wq.at[s, g, :, pl.ds(j * LANES, LANES)],
-                send.at[k],
-                recv.at[k],
+                send.at[0],
+                recv.at[0],
                 device,
             )
             for j in range(3)
         ]
-
-    def wq_whole(k):
-        send, recv = b["wq_sems"][:2]
-        block = wq.at[here.from_shard(k), g]
-        return remote(block, block, send.at[k], recv.at[k], here.at_shard(k))
 
     for k in range(1, SHARDS):
         norm_copy(k).start()
@@ -969,12 +977,11 @@
     n1, inverse = centre(tok[...].astype(F32))
     b["n1"][...] = n1
     b["r1"][...] = jnp.broadcast_to(inverse, (ROWS, LANES))
-    for k in range(1, SHARDS):
-        norm_copy(k).wait_recv()
-    a1 = b["a1"]
-    a1[s] = (n1 * wide(norm, 0) + wide(norm, 1)).astype(LOW)
-    a1_step = plane_gather(here, lambda i: a1.at[i], b["a1_sems"], ends)
+    a1, raw = b["a1"], b["ffn"]
+    raw[s] = n1.astype(LOW)
+    a1_step = plane_gather(here, lambda i: raw.at[i], b["a1_sems"], ends)
     next(a1_step)
+    raw_sent = ends.pop()
 
     own_copies[3].wait()
     wo_send, wo_recv = b["wo_more"]
@@ -1008,24 +1015,19 @@
             remote(
                 wup.at[wu_rows, wu_columns(device[1], j)],
                 wu.at[s, x, :, pl.ds(j * 256, 256)],
-                wu_send.at[k],
-                wu_recv.at[k],
+                wu_send.at[0],
+                wu_recv.at[0],
                 device,
             )
             for j in range(2)
         ]
 
-    def wu_whole(k):
-        block = wu.at[here.from_shard(k), x]
-        return remote(block, block, wu_send.at[k], wu_recv.at[k], here.at_shard(k))
-
     wu_beside = remote(wu.at[:, x], wu.at[:, x], wu_xsend.at[0], wu_xrecv.at[0], here.beside)
 
     dz = b["dz"]
     own_live = column(live_rows[pl.ds(s, 1), :].astype(F32))
     dz[c, corner] = (cot[...].astype(F32) * jnp.concatenate([own_live] * SHARDS, 1)).astype(LOW)
-    for k in range(1, SHARDS):
-        wq_whole(k).wait_recv()
+    all_came(here, wq.at[pl.ds(0, SHARDS - 1), g], b["wq_sems"])
     wq_send, wq_recv = b["wq_sems"][2:]
     wq_beside = remote(wq.at[:, g], wq.at[:, g], wq_send.at[0], wq_recv.at[0], here.beside)
     wq_core = [
@@ -1045,19 +1047,32 @@
     wd_far.start()
     next(a1_step)
     next(wo_step)
+    for copy in own_copies[4:]:
+        copy.wait()
+
+    for copy in wq_core:
+        copy.wait_recv()
+    all_came(here, norm.at[pl.ds(0, SHARDS - 1)], b["norm_sems"])
+    qkv, probs = b["qkv"], b["probs"]
+    gain, shift, weight = wide(norm, 0), wide(norm, 1), flat(wq[...])
+
+    def project(yy):
+        rows = []
+        for zz in range(4):
+            value = (raw[zz * 2 + yy].astype(F32) * gain + shift).astype(LOW)
+            a1[zz * 2 + yy] = value
+            rows.append(value)
+        out = dot(jnp.concatenate(rows, 0), weight).astype(LOW)
+        for zz in range(4):
+            qkv[zz * 2 + yy] = out[zz * ROWS : (zz + 1) * ROWS]
+
+    project(y)
+    run(a1_step)
     for k in range(1, SHARDS):
         for copy in wu_copies(k):
             copy.start()
-    for copy in own_copies[4:]:
-        copy.wait()
-    run(a1_step)
     dz_start, dz_relay, dz_last, dz_got = square_gather(here, dz, b["dz_sems"], ends)
-    dz_start()
-
-    for copy in wq_core:
-        copy.wait_recv()
-    qkv, probs = b["qkv"], b["probs"]
-    qkv[...] = dot(flat(a1[...]), flat(wq[...])).astype(LOW).reshape(qkv.shape)
+    project(1 - y)
     keys = flat(qkv[:, :, LANES : 2 * LANES])
     values = flat(qkv[:, :, 2 * LANES :])
     key_items = jnp.concatenate(
@@ -1067,9 +1082,9 @@
     mine = [lane < HEAD_DIM, lane >= HEAD_DIM]
     o_mine, o_all = b["o_mine"], b["o_all"]
 
-    def o_copy(to, k):
+    def o_copy(to):
         send, recv = b["o_sems"]
-        return remote(o_mine.at[to], o_all.at[s], send.at[k], recv.at[k], (g, to))
+        return remote(o_mine.at[to], o_all.at[s], send.at[0], recv.at[0], (g, to))
 
     def attend(zz):
         pair = pl.ds(zz * 2, 2)
@@ -1092,7 +1107,7 @@
         attend(zz)
         for j in range(2):
             to = zz * 2 + j
-            o_copy(to, (to + SHARDS - s) % SHARDS).start()
+            o_copy(to).start()
         if step == 1:
             run(wo_step)
             wo_core[0].start()
@@ -1101,15 +1116,14 @@
     wo_core[1].start()
     attend(z)
     o_all[s] = o_mine[s]
-    o_copy(here.across[1], (here.across[1] + SHARDS - s) % SHARDS).start()
+    dz_start()
+    o_copy(here.across[1]).start()
     wd_far.wait_recv()
     wd_beside.start()
-    for k in range(1, SHARDS):
-        wu_whole(k).wait_recv()
+    all_came(here, wu.at[pl.ds(0, SHARDS - 1), x], b["wu_sems"])
     wu_beside.start()
     dz_relay()
-    for k in range(1, SHARDS):
-        o_copy(here.from_shard(k), k).wait_recv()
+    all_came(here, o_all.at[pl.ds(0, SHARDS - 1)], b["o_sems"])
     for copy in wo_core:
         copy.wait_recv()
 
@@ -1166,7 +1180,8 @@
     go(2)
     go(3)
     ffn = b["ffn"]
-    f_start, f_go, f_end = square_sum(here, lambda cc, at: ffn.at[cc, at], b["block"], b["ffn_sum"])
+    f_start, f_go, f_end = square_sum(here, lambda cc, at: ffn.at[cc * 4 + at], b["block"], b["ffn_sum"])
+    raw_sent()
     ffn[...] = dot(flat(act[...]), down).astype(LOW).reshape(ffn.shape)
     for i in range(4):
         f_start(i)
@@ -1236,7 +1251,7 @@
     dqkv[:, :, LANES : 2 * LANES] = (gk[...].T * score_scale).astype(LOW).reshape(thirds)
     dqkv[:, :, 2 * LANES :] = gv[...].T.astype(LOW).reshape(thirds)
 
-    da1, weight = da2, flat(wq[...])
+    da1 = da2
 
     def spread(zz):
         pair = pl.ds(zz * 2, 2)
@@ -1252,9 +1267,16 @@
     holder = x * 2 + here.near
     stays = (holder == g) & (owner == s)
     gd_away = remote(
-        b["gd_total"], b["gd_land"], b["gd_sems"][0].at[0], b["gd_sems"][1].at[0], (holder, owner)
-    )
-    gu_total, gu_land = b["gu_total"], b["gu_land"]
+        b["gd_total"], gd_land, b["gd_sems"][0].at[0], b["gd_sems"][1].at[0], (holder, owner)
+    )
+    gu_total = b["gu_total"]
+
+    def store(i, src, dst):
+        return pltpu.make_async_copy(src, dst, b["out_sems"].at[i])
+
+    gd_stay = store(0, b["gd_total"], gd_land)
+    gu_stay = store(1, gu_total.at[c, corner], gu_land.at[c, corner])
+    gq_stay = store(2, b["gq_total"].at[s], gq_land.at[s])
     gu_send, gu_recv = b["gu_sems"]
 
     def gu_copy(k, i):
@@ -1278,18 +1300,22 @@
     def send_gd():
         run(gd_step)
 
+        @pl.when(stays)
+        def _():
+            gd_stay.start()
+
         @pl.when(jnp.logical_not(stays))
         def _():
             gd_away.start()
 
     def send_gu():
         run(gu_step)
-        gu_land[c, corner] = gu_total[c, corner]
+        gu_stay.start()
         for k, i in others:
             gu_copy(k, i).start()
 
-    go_out = spread_sum(here, b["go_total"], out_sum, b["go_plane"], ends)
-    gq_out = plane_trade(here, b["gq_total"], b["gq_land"], b["gq_sems"], ends)
+    go_out = spread_sum(here, b["go_total"], b["go_sum32"], b["go_plane"], ends)
+    gq_out = plane_trade(here, b["gq_total"], gq_land, b["gq_sems"], ends, gq_stay)
 
     def send_go():
         run(go_step)
@@ -1323,70 +1349,59 @@
         ],
         0,
     )
-    np_mine, np_land, np_all = b["np_mine"], b["np_land"], b["np_all"]
-    n_send, n_recv, m_send, m_recv = b["np_sems"]
-    for k in range(GROUPS):
-        np_mine[k] = part[:, k * 2 * LANES : (k + 1) * 2 * LANES]
-
-    def grp_copy(k):
-        to = (g + k) % GROUPS
-        return remote(np_mine.at[to], np_land.at[k], n_send.at[k], n_recv.at[k], (to, s))
-
-    for k in range(1, GROUPS):
-        grp_copy(k).start()
-    input_grad[...] = centre_back(e1, n1, b["r1"][:, :1], wide(norm, 0)) + b["dh1"][...]
-    for k in range(1, GROUPS):
-        grp_copy(k).wait_recv()
-    np_all[s] = np_mine[g] + np_land[1] + np_land[2] + np_land[3]
-
-    def all_copy(k):
-        return remote(np_all.at[s], np_all.at[s], m_send.at[k], m_recv.at[k], here.at_shard(k))
-
-    for k in range(1, SHARDS):
-        all_copy(k).start()
+    np_mine, np_land = b["np_mine"], b["np_land"]
+    n_send, n_recv = b["np_sems"]
+    me, everyone = g * SHARDS + s, GROUPS * SHARDS
+    for k in range(SHARDS):
+        np_mine[k] = part[:, k * LANES : (k + 1) * LANES]
+
+    def np_copy(k):
+        to = (me + k) % everyone
+        return remote(
+            np_mine.at[to // 4], np_land.at[k], n_send.at[0], n_recv.at[0], (to // SHARDS, to % SHARDS)
+        )
+
+    def np_start(k, carry):
+        np_copy(k).start()
+        return carry
+
+    lax.fori_loop(1, everyone, np_start, 0)
+    np_land[0] = np_mine[me // 4]
+    b["dx"][...] = centre_back(e1, n1, b["r1"][:, :1], wide(norm, 0)) + b["dh1"][...]
+    dx_store = store(3, b["dx"], input_grad)
+    dx_store.start()
 
     f_end()
-    block_out[...] = b["h1"][...] + b["block"][...]
+    b["block"][...] += b["h1"][...]
+    block_store = store(4, b["block"], block_out)
+    block_store.start()
     run(go_out)
+    out_store = store(5, b["go_sum32"], out_sum)
+    out_store.start()
     for k, i in others:
         gu_came(k, i).wait_recv()
-    for cc in range(2):
-        for at in range(4):
-            for j in range(2):
-                first = (j * 4 + at) * HIDDEN + cc * 256
-                up_sum[:, first : first + 256] = gu_land[cc, at, :, j * 256 : (j + 1) * 256].astype(F32)
+    gu_stay.wait()
     run(gq_out)
-    for j in range(SHARDS):
-        for i in range(3):
-            qkv_sum[:, i * WIDTH + j * LANES : i * WIDTH + (j + 1) * LANES] = b["gq_land"][
-                j, :, i * LANES : (i + 1) * LANES
-            ].astype(F32)
 
     @pl.when(stays)
     def _():
-        down_sum[...] = b["gd_total"][...].astype(F32)
+        gd_stay.wait()
 
     @pl.when(jnp.logical_not(stays))
     def _():
         gd_away.wait_recv()
-        down_sum[...] = b["gd_land"][...].astype(F32)
         gd_away.wait_send()
 
-    for k in range(1, SHARDS):
-        all_copy(k).wait_recv()
-    total = np_all[0]
-    for j in range(1, SHARDS):
-        total += np_all[j]
-    norm_sum[...] = pltpu.roll(total, 2 * LANES - s * 32, 1)[:, :LANES]
-
-    for k in range(1, GROUPS):
-        grp_copy(k).wait_send()
-    for k in range(1, SHARDS):
-        all_copy(k).wait_send()
-        norm_copy(k).wait_send()
-        wq_whole(k).wait_send()
-        wu_whole(k).wait_send()
-        o_copy(here.at_shard(k)[1], k).wait_send()
+    all_came(here, np_land.at[pl.ds(1, everyone - 1)], b["np_sems"])
+    total = jnp.sum(np_land[...], 0)
+    norm_sum[...] = pltpu.roll(total, LANES - (s % 4) * 32, 1)
+    all_sent(here, np_land.at[pl.ds(1, everyone - 1)], b["np_sems"])
+    for copy in (dx_store, block_store, out_store):
+        copy.wait()
+    all_sent(here, norm.at[pl.ds(0, SHARDS - 1)], b["norm_sems"])
+    all_sent(here, wq.at[pl.ds(0, SHARDS - 1), g], b["wq_sems"])
+    all_sent(here, wu.at[pl.ds(0, SHARDS - 1), x], b["wu_sems"])
+    all_sent(here, o_all.at[pl.ds(0, SHARDS - 1)], b["o_sems"])
     for k, i in others:
         gu_copy(k, i).wait_send()
     for copy in (wq_beside, wd_far, wd_beside, wu_beside, *wq_core, *wo_core):
@@ -1397,8 +1412,32 @@
         finish()
 
 
+KERNEL_VMEM = 57 * 2**20
 SIZES = ((32, 3 * WIDTH), (32, WIDTH), (32, 4 * WIDTH), (ROWS, WIDTH))
+SUMS = (
+    (LOW, (SHARDS, 32, 3 * LANES)),
+    (F32, (32, WIDTH)),
+    (LOW, (2, 4, 32, HIDDEN)),
+    (LOW, (ROWS, WIDTH)),
+)
 KINDS = (F32, F32, F32, F32, LOW)
+CHUNKS = ((1, 0, 32), (2, 0, 32), (0, 0, 32), (3, 0, ROWS))
+AHEAD = 4
+
+
+def pieces(i):
+    if i == 0:
+        return [
+            (k * WIDTH + j * LANES, LANES, (j,), k * LANES) for j in range(SHARDS) for k in range(3)
+        ]
+    if i == 2:
+        return [
+            ((j * 4 + at) * HIDDEN + cc * 256, 256, (cc, at), j * 256)
+            for cc in range(2)
+            for at in range(4)
+            for j in range(2)
+        ]
+    return [(first, 256, (), first) for first in range(0, WIDTH, 256)]
 
 
 def adamw_kernel(rates, *refs):
@@ -1413,56 +1452,73 @@
     sums, olds, passed = take(4), [take(3) for _ in SIZES], take(2)
     norm_new = take(5)
     news, handed = [take(5) for _ in SIZES], take(2)
-    held_in, held_out = [take(4) for _ in SIZES], [take(5) for _ in SIZES]
+    held_sum, held_old, held_out = take(4), [take(3) for _ in SIZES], [take(5) for _ in SIZES]
     held_pass = take(2)
-    in_sem, out_sem, pass_sem = take(3)
-    loads = [
-        [
-            pltpu.make_async_copy(src, dst, in_sem.at[i, j])
-            for j, (src, dst) in enumerate(zip([sums[i], *olds[i]], held_in[i]))
-        ]
-        for i in range(4)
-    ]
-    stores = [
-        [pltpu.make_async_copy(src, dst, out_sem.at[i, j]) for j, (src, dst) in enumerate(zip(held_out[i], news[i]))]
-        for i in range(4)
-    ]
+    sum_sem, in_sem, out_sem, pass_sem = take(4)
+    sum_loads = [pltpu.make_async_copy(sums[i], held_sum[i], sum_sem.at[i]) for i in range(4)]
+    loads, stores = [], []
+    for n, (i, first, rows) in enumerate(CHUNKS):
+        at = pl.ds(first, rows)
+        loads.append(
+            [
+                pltpu.make_async_copy(src.at[at, :], dst.at[at, :], in_sem.at[n, j])
+                for j, (src, dst) in enumerate(zip(olds[i], held_old[i]))
+            ]
+        )
+        stores.append(
+            [
+                pltpu.make_async_copy(src.at[at, :], dst.at[at, :], out_sem.at[n, j])
+                for j, (src, dst) in enumerate(zip(held_out[i], news[i]))
+            ]
+        )
     passes = [pltpu.make_async_copy(passed[i], held_pass[i], pass_sem.at[i]) for i in range(2)]
     hands = [pltpu.make_async_copy(held_pass[i], handed[i], pass_sem.at[2 + i]) for i in range(2)]
-    order = (2, 0, 3, 1)
-    for i in order:
-        for copy in loads[i]:
-            copy.start()
-    for copy in passes:
-        copy.start()
+
+    def load(n):
+        if n < len(CHUNKS):
+            i, first, _ = CHUNKS[n]
+            if first == 0:
+                sum_loads[i].start()
+            for copy in loads[n]:
+                copy.start()
+
+    for n in range(AHEAD):
+        load(n)
     count = norm_sum[4:5, 0:1]
     results = adamw(norm_sum[0:4, 0:32], count, *[ref[...] for ref in norm_old], rates[4], 0.0)
     for ref, value in zip(norm_new, results):
         ref[...] = value
-    for i in order:
-        for copy in loads[i]:
+    inverse = 1.0 / count
+    for n, (i, top, rows) in enumerate(CHUNKS):
+        if top == 0:
+            sum_loads[i].wait()
+        for copy in loads[n]:
             copy.wait()
-        rows, cols = SIZES[i]
-        step = 16
+        load(n + AHEAD)
+        if n + AHEAD == len(CHUNKS):
+            for copy in passes:
+                copy.start()
+        step = min(rows, 32)
 
         def some(k, carry):
-            at = pl.ds(pl.multiple_of(k * step, step), step)
-            for first in range(0, cols, WIDTH):
-                lanes = slice(first, first + WIDTH)
-                summed, *old = [ref[at, lanes] for ref in held_in[i]]
-                results = adamw(summed, count, *old, rates[i], 0.1)
+            at = pl.ds(pl.multiple_of(top + k * step, step), step)
+            for first, width, index, start in pieces(i):
+                lanes = slice(first, first + width)
+                summed = held_sum[i][(*index, at, slice(start, start + width))].astype(F32) * inverse
+                old = [ref[at, lanes] for ref in held_old[i]]
+                results = adamw(summed, 1.0, *old, rates[i], 0.1)
                 for ref, value in zip(held_out[i], results):
                     ref[at, lanes] = value
             return carry
 
         lax.fori_loop(0, rows // step, some, 0)
-        for copy in stores[i]:
+        for copy in stores[n]:
             copy.start()
-    for i in range(2):
-        passes[i].wait()
-        hands[i].start()
-    for i in order:
-        for copy in stores[i]:
+    for k in range(2):
+        passes[k].wait()
+        hands[k].start()
+    for copies in stores:
+        for copy in copies:
             copy.wait()
     for copy in hands:
         copy.wait()
@@ -1480,11 +1536,12 @@
         + [shaped(F32, ROWS, WIDTH)] * 2,
         in_specs=[VMEM] * 4 + [ANY] * 18,
         out_specs=[VMEM] * 5 + [ANY] * 22,
-        scratch_shapes=[buffer(F32, *size) for size in SIZES for _ in range(4)]
+        scratch_shapes=[buffer(kind, *shape) for kind, shape in SUMS]
+        + [buffer(F32, *size) for size in SIZES for _ in range(3)]
         + [buffer(kind, *size) for size in SIZES for kind in KINDS]
         + [buffer(F32, ROWS, WIDTH)] * 2
-        + [DMA((4, 4)), DMA((4, 5)), DMA((4,))],
-        compiler_params=pltpu.CompilerParams(vmem_limit_bytes=60 * 2**20),
+        + [DMA((4,)), DMA((len(CHUNKS), 3)), DMA((len(CHUNKS), 5)), DMA((4,))],
+        compiler_params=pltpu.CompilerParams(vmem_limit_bytes=KERNEL_VMEM),
     )(*norms, *sums, *olds, *passed)
 
 
@@ -1513,17 +1570,17 @@
         out_shape=[
             shaped(F32, ROWS, WIDTH),
             shaped(F32, ROWS, WIDTH),
-            shaped(F32, 32, 3 * WIDTH),
-            shaped(F32, 32, 4 * WIDTH),
+            shaped(LOW, SHARDS, 32, 3 * LANES),
+            shaped(LOW, 2, 4, 32, HIDDEN),
             shaped(F32, 32, WIDTH),
-            shaped(F32, ROWS, WIDTH),
+            shaped(LOW, ROWS, WIDTH),
             shaped(F32, 8, LANES),
         ],
         in_specs=[VMEM] * 5 + [ANY] * 4,
-        out_specs=[VMEM] * 7,
+        out_specs=[ANY] * 6 + [VMEM],
         scratch_shapes=scratch,
         compiler_params=pltpu.CompilerParams(
-            collective_id=0, has_side_effects=True, vmem_limit_bytes=60 * 2**20
+            collective_id=0, has_side_effects=True, vmem_limit_bytes=KERNEL_VMEM
         ),
     )(*args)
     model_width, hidden = tokens.shape[1], up_weight.shape[1]

time: 176 us -> 172 us (0.977)
  Pallas kernels: 175 us -> 171 us
    pallas_call x1, Pallas kernels: 168 us -> 164 us  [fast_body(): pl.pallas_call(step_kernel, out_shape=[shaped(F32, ROWS, WIDTH), shaped(F...]
where the time goes in v5:
time: 172 us
  Pallas kernels  171 us (99%)
    pallas_call x1, Pallas kernels, fast_body(): pl.pallas_call(step_kernel, out_shape=[shaped(F32, ROWS, WIDTH), shaped(F...  164 us
    pallas_call x1, Pallas kernels, call_adamw(): pl.pallas_call(functools.partial(adamw_kernel, rates), out_shape=[shaped(...  7.01 us

profile of v5, /device:TPU:0, one launch (start us, length us, event | category | flops | bytes accessed | tf_op | source)
XLA Modules:
  0.0 172.2 jit_solution(7956590585190404587)
XLA Ops:
  0.7 164.3 %shard_map.439 = (f32[128,1024]{1,0:T(8,128)}, f32[128,1024]{1,0:T(8,128)}, bf16[8,32,384]{2,1,0:T(8,128)(2,1)}, bf16[2,4,32,512]{3,2,1,0:T(8,128)(2,1)}, f32[32...) custom-call(bf16[128,1024]{1,0:T(8,128)(2,1)} %refs_0_.1, bf16[128,1024]{1,0:T(8,128)(2,1)} %refs_1_.2, ...), custom_call_target="tpu_custom_call" | custom-call | tf_op jit(solution)/shard_map/pallas_call | solution.py:1568
  165.0 7.0 %shard_map.440 = (f32[4,32]{1,0:T(4,128)}, f32[4,32]{1,0:T(4,128)}, f32[4,32]{1,0:T(4,128)}, f32[4,32]{1,0:T(4,128)}, bf16[4,32]{1,0:T(4,128)(2,1)}, /*index=5*/...) custom-call(f32[8,128]{1,0:T(8,128)} %get-tuple-element.61.refs_0_, ...), custom_call_target="tpu_custom_call" | custom-call | tf_op jit(solution)/shard_map/pallas_call | solution.py:1532

commit v6 on v5

--- a/solution.py
+++ b/solution.py
@@ -507,8 +507,8 @@
     z, y = here.z, here.y
     order = [
         jnp.where(z < 2, 3, 0),
-        jnp.where(z == 0, 2, jnp.where(z == 1, 0, jnp.where(z == 2, 3, 1))),
-        1 + z % 2,
+        jnp.where(z % 3 == 0, jnp.where(z == 0, 2, 1), jnp.where(z == 1, 2, 1)),
+        jnp.where(z % 3 == 0, jnp.where(z == 0, 1, 2), jnp.where(z == 1, 0, 3)),
         z,
     ]
     first = [
@@ -781,7 +781,7 @@
     remote(seven, seven, sems[0].at[0], sems[1].at[0], here.across).wait_recv()
 
 
-def plane_trade(here, mine, theirs, sems, ends, stay=None):
+def plane_trade(here, mine, theirs, sems, ends, stay=None, prepare=None):
     send, recv = sems
 
     def copy(k):
@@ -789,7 +789,11 @@
         return remote(mine.at[device[1]], theirs.at[here.s], send.at[0], recv.at[0], device)
 
     for k in range(1, SHARDS):
+        if prepare is not None:
+            prepare(here.at_shard(k)[1])
         copy(k).start()
+    if prepare is not None:
+        prepare(here.s)
     if stay is None:
         theirs[here.s] = mine[here.s]
     else:
@@ -1111,13 +1115,13 @@
         if step == 1:
             run(wo_step)
             wo_core[0].start()
-    for i in range(SHARDS):
-        wo_beside(i, beside_g).wait_recv()
-    wo_core[1].start()
     attend(z)
     o_all[s] = o_mine[s]
     dz_start()
     o_copy(here.across[1]).start()
+    for i in range(SHARDS):
+        wo_beside(i, beside_g).wait_recv()
+    wo_core[1].start()
     wd_far.wait_recv()
     wd_beside.start()
     all_came(here, wu.at[pl.ds(0, SHARDS - 1), x], b["wu_sems"])
@@ -1201,9 +1205,11 @@
     b["dh1"][...] = dh1
     low = dh1.astype(LOW)
     do_mine, do_all = b["do_mine"], b["do_all"]
-    for k in range(SHARDS):
-        do_mine[k] = dot_nt(low, wo[k].reshape(ROWS, WIDTH)).astype(LOW)
-    do_step = plane_trade(here, do_mine, do_all, b["do_sems"], ends)
+
+    def head_rows(to):
+        do_mine[to] = dot_nt(low, wo[to].reshape(ROWS, WIDTH)).astype(LOW)
+
+    do_step = plane_trade(here, do_mine, do_all, b["do_sems"], ends, prepare=head_rows)
     next(do_step)
     go_part = b["go"]
     go_part[...] = dot_tn(attended, low).astype(LOW).reshape(go_part.shape)
@@ -1211,10 +1217,10 @@
     next(go_step)
     next(go_step)
     run(do_step)
-    next(gd_step)
     for i in range(1, 4):
         f_go(i)
     f_go(0)
+    next(gd_step)
 
     gk, gv, dqkv = b["gk"], b["gv"], b["dqkv"]
 

time: 172 us -> 172 us (level)
  no operation moved by 1% of the time
where the time goes in v6:
time: 172 us; the launch traced here: 171 us
  Pallas kernels  170 us (99%)
    pallas_call x1, Pallas kernels, fast_body(): pl.pallas_call(step_kernel, out_shape=[shaped(F32, ROWS, WIDTH), shaped(F...  163 us
    pallas_call x1, Pallas kernels, call_adamw(): pl.pallas_call(functools.partial(adamw_kernel, rates), out_shape=[shaped(...  7.01 us

profile of v6, /device:TPU:0, one launch (start us, length us, event | category | flops | bytes accessed | tf_op | source)
XLA Modules:
  0.0 171.1 jit_solution(11688571244828156280)
XLA Ops:
  0.7 163.2 %shard_map.439 = (f32[128,1024]{1,0:T(8,128)}, f32[128,1024]{1,0:T(8,128)}, bf16[8,32,384]{2,1,0:T(8,128)(2,1)}, bf16[2,4,32,512]{3,2,1,0:T(8,128)(2,1)}, f32[32...) custom-call(bf16[128,1024]{1,0:T(8,128)(2,1)} %refs_0_.1, bf16[128,1024]{1,0:T(8,128)(2,1)} %refs_1_.2, ...), custom_call_target="tpu_custom_call" | custom-call | tf_op jit(solution)/shard_map/pallas_call | solution.py:1574
  163.9 7.0 %shard_map.440 = (f32[4,32]{1,0:T(4,128)}, f32[4,32]{1,0:T(4,128)}, f32[4,32]{1,0:T(4,128)}, f32[4,32]{1,0:T(4,128)}, bf16[4,32]{1,0:T(4,128)(2,1)}, /*index=5*/...) custom-call(f32[8,128]{1,0:T(8,128)} %get-tuple-element.61.refs_0_, ...), custom_call_target="tpu_custom_call" | custom-call | tf_op jit(solution)/shard_map/pallas_call | solution.py:1538
